TPU v7x, 128 devices: a whole 4x4x4 slice. The times are simulated.
128 devices in a mesh: outer: 4 (over x), shard: 32 (over z, y, core).
Axes of the slice: x: 4, y: 4, z: 4, core: 2. Of those that a mesh axis runs over, the one named last changes fastest.
Arguments:
- acts: bfloat16 [16384, 4096], P(('outer', 'shard')), may hold values from -6 to 6
- grads: bfloat16 [16384, 14336], P(('outer', 'shard')), may hold values from -18 to 18
- basis: float32 [32, 4096], replicated, may hold values from -6 to 6
- error_in: bfloat16 [4, 4096, 14336], P('outer', None, 'shard'), may hold values from -3 to 3
- weight: float32 [4096, 14336], P('outer', 'shard'), may hold values from -0.3 to 0.3
- moment_one: float32 [4096, 14336], P('outer', 'shard'), may hold values from -0.3 to 0.3
- moment_two: float32 [4096, 14336], P('outer', 'shard'), may hold values from 0.0001 to 0.01
Outputs:
- basis_out: float32 [32, 4096], replicated
- error_out: bfloat16 [4, 4096, 14336], P('outer', None, 'shard')
- weight_out: float32 [4096, 14336], P('outer', 'shard')
- moment_one_out: float32 [4096, 14336], P('outer', 'shard')
- moment_two_out: float32 [4096, 14336], P('outer', 'shard')
All inputs are finite; a program needn't handle non-finite values.
Results may differ from a plain program's by a relative error of at most 0.001.
Values may be sent and summed in bfloat16 or wider, within the bound.
No kernel may reach another device: no remote copies, remote signals or barrier semaphores. Data moves between devices by JAX's collectives and lax.ppermute only.
A program may use at most 192 MiB of HBM per device.

v0:
```python
import jax
import jax.numpy as jnp
from jax import lax
from jax.sharding import PartitionSpec as P

beta_one = 0.9
beta_two = 0.95
learn_rate = 0.01
decay_rate = 0.1
adam_epsilon = 1e-08
first_fix = 1.0 - 0.9**8
second_fix = 1.0 - 0.95**8


def per_device(acts, grads, basis, error_in, weight, moment_one, moment_two):
    highest = lax.Precision.HIGHEST
    shards = lax.axis_size("shard")
    pods = lax.axis_size("outer")
    tok_pod = acts.shape[0] * shards
    grad_cols = lax.all_to_all(grads, "shard", split_axis=1, concat_axis=0, tiled=True)
    contract = (((0,), (0,)), ((), ()))
    gathered = lax.all_gather(acts, "shard", axis=0, tiled=True)
    gradient = lax.dot_general(gathered, grad_cols, contract, preferred_element_type=jnp.float32)
    matrix = gradient * tok_pod ** (-0.5) + error_in[0].astype(jnp.float32)
    factor = lax.psum(jnp.dot(basis, matrix, precision=highest), "outer") / pods
    gram = lax.psum(jnp.dot(factor, factor.T, precision=highest), "shard")
    lower = jnp.linalg.cholesky(gram)
    ortho = jax.scipy.linalg.solve_triangular(lower, factor, lower=True)
    terms = lax.dot_general(ortho, matrix, (((1,), (1,)), ((), ())), precision=highest)
    basis_out = lax.psum(terms, ("outer", "shard")) / pods
    approx = lax.dot_general(basis_out, ortho, contract, precision=highest)
    error_out = (matrix - approx).astype(jnp.bfloat16)[None]
    own_rows = weight.shape[0]
    row_start = lax.axis_index("outer") * own_rows
    update = lax.dynamic_slice_in_dim(approx, row_start, own_rows, 0)
    moment_one_out = beta_one * moment_one + (1.0 - beta_one) * update
    moment_two_out = beta_two * moment_two + (1.0 - beta_two) * update * update
    step_size = moment_one_out / first_fix / (jnp.sqrt(moment_two_out / second_fix) + adam_epsilon)
    weight_out = weight * (1.0 - learn_rate * decay_rate) - learn_rate * step_size
    return (basis_out, error_out, weight_out, moment_one_out, moment_two_out)


def solution(mesh):
    return jax.shard_map(
        per_device,
        mesh=mesh,
        in_specs=(
            P(("outer", "shard"), None),
            P(("outer", "shard"), None),
            P(),
            P("outer", None, "shard"),
            P("outer", "shard"),
            P("outer", "shard"),
            P("outer", "shard"),
        ),
        out_specs=(
            P(),
            P("outer", None, "shard"),
            P("outer", "shard"),
            P("outer", "shard"),
            P("outer", "shard"),
        ),
        check_vma=False,
    )
```

profile of v0, /device:TPU:1, one launch (start us, length us, event | category | flops | bytes accessed | tf_op | source)
XLA Modules:
  0.0 519.8 jit_solution(2547676123478645924)
XLA Ops:
  7.2 0.0 copy-start
  7.2 0.0 all-gather.2.cloned.1.call-start
  7.2 0.7 all-gather.2.cloned.1.call-update
  7.9 0.0 all-reduce.2.cloned.1.call-start
  8.0 6.1 %copy.14 = bf16[128,14336]{0,1:T(8,128)(2,1)} copy(bf16[128,14336]{1,0:T(8,128)(2,1)} %param.8) | data formatting | bytes 7340032 | tf_op args[1]
  14.0 71.8 %all_to_all.19 = bf16[128,32,448]{0,2,1:T(8,128)(2,1)} all-to-all(bf16[128,32,448]{0,2,1:T(8,128)(2,1)} %bitcast.32), channel_id=1, replica_groups=mesh['outer'=4,'shard'=32] {'shard'}, dimensions={1} | all-to-all | bytes 7340032 | tf_op jit(solution)/shard_map/all_to_all | solution.py:20
  85.8 79.2 %all-gather.2.cloned.1.call-done = bf16[4096,4096]{1,0:T(8,128)(2,1)} async-done(((bf16[128,4096]{1,0:T(8,128)(2,1)}), bf16[4096,4096]{1,0:T(8,128)(2,1)}) %all-gather.2.cloned.1.call-update) | async-done | bytes 33554448 | tf_op jit(solution)/shard_map/all_gather | solution.py:22
  165.1 24.6 %convert_add_fusion = f32[4096,448]{0,1:T(8,128)} fusion(bf16[4096,4096]{1,0:T(8,128)(2,1)} %all-gather.2.cloned.1.call-done, bf16[1,4096,448]{1,2,0:T(8,128)(2,1)} %param.10, bf16[128,32,448]{0,2,1:T(8,128)(2,1)} %all_to_all.19), kind=kOutput, calls=%fused_computation | convolution fusion | flops 15037890560 | bytes 48234496 | tf_op jit(solution)/shard_map/dot_general | solution.py:23
  189.7 0.0 copy-done
  189.7 8.6 %convolution_bitcast_fusion = f32[32,448]{1,0:T(8,128)S(1)} fusion(f32[4096,448]{0,1:T(8,128)} %convert_add_fusion, f32[32,4096]{1,0:T(8,128)S(1)} %copy-done), kind=kOutput, calls=%fused_computation.9 | convolution fusion | flops 704643072 | bytes 7921664 | tf_op jit(solution)/shard_map/dot_general | solution.py:25
  198.3 13.7 %psum.21 = f32[32,448]{1,0:T(8,128)S(1)} all-reduce(f32[32,448]{1,0:T(8,128)S(1)} %convolution_bitcast_fusion), channel_id=1, replica_groups=mesh['outer'=4,'shard'=32] {'outer'}, use_global_device_ids=true, to_apply=%region_0.0 | all-reduce | flops 14336 | bytes 114688 | tf_op jit(solution)/shard_map/psum | solution.py:25
  212.0 0.2 fusion.6
  212.2 122.3 %psum.22 = f32[32,32]{0,1:T(8,128)S(1)} all-reduce(f32[32,32]{0,1:T(8,128)S(1)} %fusion.6), channel_id=1, replica_groups=mesh['outer'=4,'shard'=32] {'shard'}, use_global_device_ids=true, to_apply=%region_1.0 | all-reduce | flops 1024 | bytes 8192 | tf_op jit(solution)/shard_map/psum | solution.py:26
  334.5 0.1 copy.17
  334.6 2.9 cholesky.16
  337.5 0.6 compare_reduce_fusion
  338.2 0.7 fusion.10
  338.9 2.4 custom-call.7
  341.3 0.3 fusion.4
  341.6 8.0 %fusion.16 = f32[32,4096]{1,0:T(8,128)} fusion(f32[32,448]{1,0:T(8,128)S(1)} %fusion.4, f32[4096,448]{0,1:T(8,128)} %convert_add_fusion), kind=kOutput, calls=%fused_computation.28 | convolution fusion | flops 704643072 | bytes 7921664 | tf_op jit(solution)/shard_map/dot_general | solution.py:29
  349.5 0.0 all-reduce.2.cloned.1.call-update
  349.6 145.1 %all-reduce.2.cloned.1.call-done = f32[32,4096]{1,0:T(8,128)} async-done(((f32[32,4096]{1,0:T(8,128)}), f32[32,4096]{1,0:T(8,128)}) %all-reduce.2.cloned.1.call-update) | async-done | bytes 524304 | tf_op jit(solution)/shard_map/psum | solution.py:30
  494.7 1.1 broadcast_multiply_fusion
  495.7 0.0 copy-start.1
  495.8 5.9 %fusion.17 = f32[4096,448]{0,1:T(8,128)S(1)} fusion(f32[32,4096]{1,0:T(8,128)S(1)} %broadcast_multiply_fusion, f32[32,448]{1,0:T(8,128)S(1)} %fusion.4), kind=kOutput, calls=%fused_computation.29 | convolution fusion | flops 704643072 | bytes 7921664 | tf_op jit(solution)/shard_map/dot_general | solution.py:31
  501.7 0.0 copy-done.1
  501.7 0.0 copy-start.2
  501.7 0.0 copy-start.3
  501.7 6.1 %fusion = bf16[1,4096,448]{1,2,0:T(8,128)(2,1)} fusion(f32[4096,448]{0,1:T(8,128)} %convert_add_fusion, f32[4096,448]{0,1:T(8,128)S(1)} %fusion.17), kind=kLoop, calls=%fused_computation.2 | loop fusion | flops 3670016 | bytes 18350080 | tf_op jit(solution)/shard_map/broadcast_in_dim | solution.py:32
  507.8 0.0 copy-done.2
  507.8 0.0 copy-done.3
  507.8 5.2 multiply_subtract_fusion
  (2 shorter events, 0.0 us)
Async XLA Ops:
  7.2 182.5 %copy-start = (f32[32,4096]{1,0:T(8,128)S(1)}, f32[32,4096]{1,0:T(8,128)}, u32[]{:S(2)}) copy-start(f32[32,4096]{1,0:T(8,128)} %param.9) | copy-start | bytes 1572868
  7.2 157.9 %all-gather.2.cloned.1.call-start = ((), (), s32[]{:S(2)}) async-start(), calls=%async_computation.1 | async-start | bytes 34603008 | tf_op jit(solution)/shard_map/all_gather | solution.py:22
  7.9 486.7 %all-reduce.2.cloned.1.call-start = ((), (), s32[]{:S(2)}) async-start(), calls=%async_computation.2 | async-start | bytes 1048576 | tf_op jit(solution)/shard_map/psum | solution.py:30
  495.7 5.9 %copy-start.1 = (f32[32,4096]{1,0:T(8,128)}, f32[32,4096]{1,0:T(8,128)S(1)}, u32[]{:S(2)}) copy-start(f32[32,4096]{1,0:T(8,128)S(1)} %broadcast_multiply_fusion) | copy-start | bytes 1572868
  501.7 6.2 %copy-start.2 = (f32[1024,448]{0,1:T(8,128)S(1)}, f32[1024,448]{0,1:T(8,128)}, u32[]{:S(2)}) copy-start(f32[1024,448]{0,1:T(8,128)} %param.11) | copy-start | bytes 5505028
  501.7 6.1 %copy-start.3 = (f32[1024,448]{0,1:T(8,128)S(1)}, f32[1024,448]{0,1:T(8,128)}, u32[]{:S(2)}) copy-start(f32[1024,448]{0,1:T(8,128)} %param.12) | copy-start | bytes 5505028
Sparse Core Ops, SparseCore 0:
  10.3 154.7 all-gather.1
  349.7 144.9 all-reduce.1
where the time goes:
time: 520 us
  waiting for transfers between devices  225 us (43%)
  blocking collectives  208 us (40%)
  matrix products  47.5 us (9%)
  other arithmetic  19.1 us (4%)
  between operations  14.1 us (3%)
  local copies, waits for them, and re-layouts  6.15 us (1%)
    psum x1, waiting for transfers between devices, per_device(): basis_out = lax.psum(terms, ('outer', 'shard')) / pods  145 us
    psum x1, blocking collectives, per_device(): gram = lax.psum(jnp.dot(factor, factor.T, precision=highest), 'shard')  122 us
    all_gather x1, waiting for transfers between devices, per_device(): gathered = lax.all_gather(acts, 'shard', axis=0, tiled=True)  79.2 us
    all_to_all x1, blocking collectives, per_device(): lax.all_to_all(grads, 'shard', split_axis=1, concat_axis=0, tiled=True)  71.8 us
    dot_general x1, matrix products, per_device(): lax.dot_general(gathered, grad_cols, contract, preferred_element_type=jnp...  24.6 us
    psum x1, blocking collectives, per_device(): factor = lax.psum(jnp.dot(basis, matrix, precision=highest), 'outer') / pods  13.7 us
  transfers between devices with their start and end apart: 2, of which 2 were waited for; matrix products, arithmetic and copies ran while one was open for 1% of the time, Pallas kernels for 0%

commit v1 on v0

v1 whole, which is shorter than its diff:
```python
import jax
import jax.numpy as jnp
from jax import lax
from jax.sharding import Mesh, PartitionSpec as P

beta_one = 0.9
beta_two = 0.95
learn_rate = 0.01
decay_rate = 0.1
adam_epsilon = 1e-08
first_fix = 1.0 - 0.9**8
second_fix = 1.0 - 0.95**8

SHARD = ("z", "y", "core")
ALL = ("outer", "z", "y", "core")


def split3(x):
    high = lax.reduce_precision(x, 8, 7)
    rest = x - high
    middle = lax.reduce_precision(rest, 8, 7)
    return [p.astype(jnp.bfloat16) for p in (high, middle, rest - middle)]


def swap(x, axis, k):
    n = lax.axis_size(axis)
    return lax.ppermute(x, axis, [(i, i ^ k) for i in range(n)])


def sum4(x, axis):
    a, b, c = swap(x, axis, 1), swap(x, axis, 2), swap(x, axis, 3)
    return (x + a) + (b + c)


def dot(a, b, ca, cb):
    return lax.dot_general(a, b, (((ca,), (cb,)), ((), ())), preferred_element_type=jnp.float32)


def thrice(x, b, cb):
    r = x.shape[0]
    y = dot(jnp.concatenate(split3(x), 0), b, 1, cb)
    return y[:r] + y[r : 2 * r] + y[2 * r :]


def per_device(acts, grads, basis, error_in, weight, moment_one, moment_two):
    highest = lax.Precision.HIGHEST
    shards = lax.axis_size(SHARD)
    devices = lax.axis_size(ALL)
    pods = lax.axis_size("outer")
    tok, width = acts.shape
    cols = error_in.shape[2]
    rank = basis.shape[0]
    scale = (tok * shards) ** (-0.5)
    half = width // 2
    gathered = [lax.all_gather(acts[:, i * half : (i + 1) * half], SHARD, axis=0, tiled=True) for i in range(2)]

    error_t = error_in[0].T
    proj = thrice(basis, acts, 1) * scale
    proj_all = lax.all_to_all(jnp.broadcast_to(proj[None], (shards, rank, tok)), SHARD, 0, 0)
    base = thrice(basis, error_t, 1)
    got = lax.all_to_all(grads.T.reshape(shards, cols, tok), SHARD, 0, 0)
    got_t = got.transpose(1, 0, 2).reshape(cols, shards * tok)

    proj_all = proj_all.transpose(1, 0, 2).reshape(rank, shards * tok)
    factor = sum4(thrice(proj_all, got_t, 1) + base, "outer") / pods
    gram = jnp.dot(factor, factor.T, precision=highest)
    gram = gram + swap(gram, "core", 1)
    gram = sum4(gram, "y")
    gram = sum4(gram, "z")
    lower = jnp.linalg.cholesky(gram)
    ortho = jax.scipy.linalg.solve_triangular(lower, factor, lower=True)

    wide = thrice(ortho, got_t, 0)
    wide = lax.all_to_all(wide.reshape(rank, shards, tok).transpose(1, 0, 2), SHARD, 0, 0)
    inner = wide.sum(0) * scale
    terms = thrice(inner, acts, 0) + thrice(ortho, error_t, 0)
    piece = lax.all_to_all(terms.reshape(devices, -1), ALL, 0, 0, tiled=True).sum(0) / pods
    basis_out = lax.all_to_all(jnp.broadcast_to(piece[None], (devices, piece.shape[0])), ALL, 0, 0, tiled=True)
    basis_out = basis_out.reshape(rank, width)

    approx_t = lax.dot_general(ortho, basis_out, (((0,), (0,)), ((), ())), precision=highest)
    outs = []
    for i in range(2):
        part = slice(i * half, (i + 1) * half)
        gradient = dot(got_t, gathered[i], 1, 0) * scale
        outs.append((gradient + error_t[:, part].astype(jnp.float32) - approx_t[:, part]).astype(jnp.bfloat16))
    error_out = jnp.concatenate(outs, 1).T[None]

    own_rows = weight.shape[0]
    row_start = lax.axis_index("outer") * own_rows
    update = lax.dynamic_slice_in_dim(approx_t, row_start, own_rows, 1).T
    moment_one_out = beta_one * moment_one + (1.0 - beta_one) * update
    moment_two_out = beta_two * moment_two + (1.0 - beta_two) * update * update
    step_size = moment_one_out / first_fix / (jnp.sqrt(moment_two_out / second_fix) + adam_epsilon)
    weight_out = weight * (1.0 - learn_rate * decay_rate) - learn_rate * step_size
    return (basis_out, error_out, weight_out, moment_one_out, moment_two_out)


def solution(mesh):
    devices = mesh.devices
    mesh = Mesh(devices.reshape(devices.shape[0], 4, 4, -1), ALL)
    tokens = P(ALL, None)
    state = P("outer", SHARD)
    errors = P("outer", None, SHARD)
    return jax.shard_map(
        per_device,
        mesh=mesh,
        in_specs=(tokens, tokens, P(), errors, state, state, state),
        out_specs=(P(), errors, state, state, state),
        check_vma=False,
    )
```

time: 520 us -> 273 us (0.53)
  blocking collectives: 208 us -> 18.6 us
  waiting for transfers between devices: 225 us -> 115 us
  starting transfers between devices: 0.08 us -> 45.8 us
  local copies, waits for them, and re-layouts: 6.15 us -> 14.3 us
    psum x1 -> x0, waiting for transfers between devices: 145 us -> none  [per_device(): basis_out = lax.psum(terms, ('outer', 'shard')) / pods]
    psum x2 -> x0, blocking collectives: 136 us -> none  [the longest x1 122 us: per_device(): gram = lax.psum(jnp.dot(factor, factor.T, precision=highest), 'shard')]
    all_to_all x0 -> x4, waiting for transfers between devices: none -> 103 us  [the longest x1 68 us: per_device(): got = lax.all_to_all(grads.T.reshape(shards, cols, tok), SHARD, 0, 0)]
    all_gather x1 -> x2, waiting for transfers between devices: 79.2 us -> 0.02 us  [per_device(): lax.all_gather(acts[:, i * half:(i + 1) * half], SHARD, axis=0, tiled=True)]
    all_to_all x1, blocking collectives: 71.8 us -> 18.6 us  [per_device(): lax.all_to_all(terms.reshape(devices, -1), ALL, 0, 0, tiled=True).sum(0)]
    all_to_all x0 -> x4, starting transfers between devices: none -> 27.2 us  [the longest x1 9.61 us: per_device(): lax.all_to_all(jnp.broadcast_to(proj[None], (shards, rank, tok)), SHARD,...]
    ppermute x0 -> x10, starting transfers between devices: none -> 18.5 us  [swap(): return lax.ppermute(x, axis, [(i, i ^ k) for i in range(n)])]
    ppermute x0 -> x10, waiting for transfers between devices: none -> 11.1 us  [swap(): return lax.ppermute(x, axis, [(i, i ^ k) for i in range(n)])]
  transfers between devices with their start and end apart: 2 -> 16, of which waited for: 2 -> 11; matrix products, arithmetic and copies ran while one was open for 1% -> 21% of each run, Pallas kernels for 0% -> 0%
where the time goes in v1:
time: 273 us; the launch traced here: 272 us
  waiting for transfers between devices  115 us (42%)
  matrix products  47.5 us (17%)
  starting transfers between devices  45.8 us (17%)
  blocking collectives  18.6 us (7%)
  other arithmetic  16.3 us (6%)
  local copies, waits for them, and re-layouts  14.3 us (5%)
  between operations  14.3 us (5%)
    all_to_all x1, waiting for transfers between devices, per_device(): got = lax.all_to_all(grads.T.reshape(shards, cols, tok), SHARD, 0, 0)  68 us
    dot_general x8, matrix products, dot(): lax.dot_general(a, b, (((ca,), (cb,)), ((), ())), preferred_element_type=...  41.1 us
    all_to_all x1, blocking collectives, per_device(): lax.all_to_all(terms.reshape(devices, -1), ALL, 0, 0, tiled=True).sum(0)  18.6 us
    ppermute x10, starting transfers between devices, swap(): return lax.ppermute(x, axis, [(i, i ^ k) for i in range(n)])  18.5 us
    all_to_all x1, waiting for transfers between devices, per_device(): lax.all_to_all(jnp.broadcast_to(piece[None], (devices, piece.shape[0])),...  13.5 us
    all_to_all x1, waiting for transfers between devices, per_device(): lax.all_to_all(wide.reshape(rank, shards, tok).transpose(1, 0, 2), SHARD,...  12.9 us
    ppermute x10, waiting for transfers between devices, swap(): return lax.ppermute(x, axis, [(i, i ^ k) for i in range(n)])  11.1 us
    all_to_all x1, starting transfers between devices, per_device(): lax.all_to_all(jnp.broadcast_to(proj[None], (shards, rank, tok)), SHARD,...  9.61 us
  transfers between devices with their start and end apart: 16, of which 11 were waited for; matrix products, arithmetic and copies ran while one was open for 21% of the time, Pallas kernels for 0%

profile of v1, /device:TPU:1, one launch (start us, length us, event | category | flops | bytes accessed | tf_op | source)
XLA Modules:
  0.0 272.0 jit_solution(5115352238899806848)
XLA Ops:
  7.2 2.4 fusion.56
  9.7 0.7 all-gather.5.cloned.1.call-update
  10.4 1.2 reduce-precision_convert_fusion.3
  11.5 0.5 fusion.33
  12.0 0.9 broadcast_in_dim.8
  12.9 9.6 %all-to-all-start = ((f32[32,32,128]{2,1,0:T(8,128)}), f32[32,32,128]{2,1,0:T(8,128)S(1)}, u32[]{:S(2)}, u32[]{:S(2)}) async-start(f32[32,32,128]{2,1,0:T(8,128)} %broadcast_in_dim.8), calls=%async_computation | async-start | bytes 1048576 | tf_op jit(solution)/shard_map/all_to_all | solution.py:59
  22.5 6.1 %copy.21 = bf16[128,14336]{0,1:T(8,128)(2,1)} copy(bf16[128,14336]{1,0:T(8,128)(2,1)} %param.8) | data formatting | bytes 7340032 | tf_op args[1]
  28.6 8.8 %all-to-all-done = f32[32,32,128]{2,1,0:T(8,128)S(1)} async-done(((f32[32,32,128]{2,1,0:T(8,128)}), f32[32,32,128]{2,1,0:T(8,128)S(1)}, u32[]{:S(2)}, u32[]{:S(2)}) %all-to-all-start) | async-done | bytes 524320 | tf_op jit(solution)/shard_map/all_to_all | solution.py:59
  37.4 5.0 %all-to-all-start.1 = ((bf16[32,448,128]{2,1,0:T(8,128)(2,1)}), bf16[32,448,128]{2,1,0:T(8,128)(2,1)}, u32[]{:S(2)}, u32[]{:S(2)}) async-start(bf16[32,448,128]{2,1,0:T(8,128)(2,1)} %bitcast.86), calls=%async_computation.1 | async-start | bytes 7340032 | tf_op jit(solution)/shard_map/all_to_all | solution.py:61
  42.5 3.2 %fusion.12 = f32[96,448]{1,0:T(8,128)S(1)} fusion(bf16[1,4096,448]{1,2,0:T(8,128)(2,1)} %param.10, bf16[32,4096]{1,0:T(8,128)(2,1)S(1)} %get-tuple-element.14, bf16[32,4096]{1,0:T(8,128)(2,1)S(1)} %get-tuple-element.15, bf16[32,4096]{1,0:T(8,128)(2,1)S(1)} %get-tuple-element.13), kind=kOutput, calls=%fused_computation.15 | convolution fusion | flops 354680832 | bytes 4628480 | tf_op jit(solution)/shard_map/dot_general | solution.py:36
  45.8 68.0 %all-to-all-done.1 = bf16[32,448,128]{2,1,0:T(8,128)(2,1)} async-done(((bf16[32,448,128]{2,1,0:T(8,128)(2,1)}), bf16[32,448,128]{2,1,0:T(8,128)(2,1)}, u32[]{:S(2)}, u32[]{:S(2)}) %all-to-all-start.1) | async-done | bytes 3670048 | tf_op jit(solution)/shard_map/all_to_all | solution.py:61
  113.9 3.3 %fusion.6 = f32[96,448]{1,0:T(8,128)S(1)} fusion(bf16[32,4096]{1,0:T(8,128)(2,1)S(1)} %get-tuple-element.11, bf16[32,4096]{1,0:T(8,128)(2,1)S(1)} %get-tuple-element.12, bf16[32,4096]{1,0:T(8,128)(2,1)S(1)} %get-tuple-element.10, bf16[32,448,128]{2,1,0:T(8,128)(2,1)} %all-to-all-done.1), kind=kOutput, calls=%fused_computation.6 | convolution fusion | flops 354680832 | bytes 4628480 | tf_op jit(solution)/shard_map/dot_general | solution.py:36
  117.2 1.3 collective-permute-start
  118.6 2.5 collective-permute-start.1
  121.2 2.3 collective-permute-done.1
  123.4 2.0 collective-permute-done.2
  125.6 5.8 %collective-permute-start.3 = (f32[32,32]{0,1:T(8,128)S(1)}, f32[32,32]{0,1:T(8,128)S(1)}, u32[]{:S(2)}, u32[]{:S(2)}) collective-permute-start(f32[32,32]{0,1:T(8,128)S(1)} %fusion.57), channel_id=1, source_target_pairs={{0,1},{1,0},{2,3},{3,2},{4,5},{5,4},{6,7},{7,6},{8,9},{9,8},{10,11... | collective-permute-start | bytes 12296 | tf_op jit(solution)/shard_map/ppermute | solution.py:27
  131.4 0.8 collective-permute-done.3
  132.3 2.4 collective-permute-start.4
  134.7 2.2 collective-permute-start.5
  137.1 2.0 collective-permute-done.5
  139.1 2.3 collective-permute-done.6
  141.5 1.1 collective-permute-start.8
  142.6 2.7 %collective-permute-start.9 = (f32[32,32]{0,1:T(8,128)S(1)}, f32[32,32]{0,1:T(8,128)S(1)}, u32[]{:S(2)}, u32[]{:S(2)}) collective-permute-start(f32[32,32]{0,1:T(8,128)S(1)} %add_add_fusion.1), channel_id=1, source_target_pairs={{0,24},{8,16},{16,8},{24,0},{1,25},{9,17},{17,9},{25,1},{2,26},{10... | collective-permute-start | bytes 12296 | tf_op jit(solution)/shard_map/ppermute | solution.py:27
  145.3 0.7 collective-permute-done.8
  146.0 1.0 collective-permute-done.9
  147.2 2.9 %cholesky.16 = f32[32,32]{1,0:T(8,128)S(1)} custom-call(f32[32,32]{1,0:T(8,128)S(1)} %fusion.47), custom_call_target="Cholesky" | custom-call | tf_op jit(solution)/shard_map/jit(cholesky)/cholesky | solution.py:70
  150.1 0.6 compare_reduce_fusion
  150.8 0.7 fusion.42
  151.4 2.4 custom-call.7
  154.2 2.8 %fusion.4 = f32[96,4096]{1,0:T(8,128)S(1)} fusion(bf16[32,448]{1,0:T(8,128)(2,1)S(1)} %get-tuple-element.17, bf16[32,448]{1,0:T(8,128)(2,1)S(1)} %get-tuple-element.18, bf16[32,448]{1,0:T(8,128)(2,1)S(1)} %get-tuple-element.16, bf16[32,448,128]{2,1,0:T(8,128)(2,1)} %all-to-all-done.1), kind=kOutput, calls=%fused_computation.4 | convolution fusion | flops 352579584 | bytes 5328896 | tf_op jit(solution)/shard_map/dot_general | solution.py:36
  156.9 0.9 bitcast_bitcast_fusion
  157.8 6.7 %all-to-all-start.2 = ((f32[32,32,128]{2,1,0:T(8,128)}), f32[32,32,128]{2,1,0:T(8,128)S(1)}, u32[]{:S(2)}, u32[]{:S(2)}) async-start(f32[32,32,128]{2,1,0:T(8,128)} %bitcast_bitcast_fusion), calls=%async_computation.2 | async-start | bytes 1048576 | tf_op jit(solution)/shard_map/all_to_all | solution.py:74
  164.5 3.0 %fusion.10 = f32[96,4096]{1,0:T(8,128)S(1)} fusion(bf16[1,4096,448]{1,2,0:T(8,128)(2,1)} %param.10, bf16[32,448]{1,0:T(8,128)(2,1)S(1)} %get-tuple-element.17, bf16[32,448]{1,0:T(8,128)(2,1)S(1)} %get-tuple-element.18, bf16[32,448]{1,0:T(8,128)(2,1)S(1)} %get-tuple-element.16), kind=kOutput, calls=%fused_computation.13 | convolution fusion | flops 352579584 | bytes 5328896 | tf_op jit(solution)/shard_map/dot_general | solution.py:36
  167.6 12.9 %all-to-all-done.2 = f32[32,32,128]{2,1,0:T(8,128)S(1)} async-done(((f32[32,32,128]{2,1,0:T(8,128)}), f32[32,32,128]{2,1,0:T(8,128)S(1)}, u32[]{:S(2)}, u32[]{:S(2)}) %all-to-all-start.2) | async-done | bytes 524320 | tf_op jit(solution)/shard_map/all_to_all | solution.py:74
  180.6 0.4 fusion.36
  181.2 0.6 all_to_all.25
  181.8 18.6 %all_to_all.31 = f32[128,1,1024]{2,1,0:T(1,128)S(1)} all-to-all(f32[128,1,1024]{2,1,0:T(1,128)S(1)} %all_to_all.25), channel_id=1, replica_groups=mesh['outer'=4,'z'=4,'y'=4,'core'=2] {'outer','z','y','core'}, dimensions={0} | all-to-all | bytes 1048576 | tf_op jit(solution)/shard_map/all_to_all | solution.py:77
  200.8 1.1 broadcast_in_dim.9
  201.9 5.8 %all-to-all-start.4 = ((f32[128,1,1024]{2,1,0:T(1,128)}), f32[128,1,1024]{2,1,0:T(1,128)S(1)}, u32[]{:S(2)}, u32[]{:S(2)}) async-start(f32[128,1,1024]{2,1,0:T(1,128)} %broadcast_in_dim.9), calls=%async_computation.4 | async-start | bytes 1048576 | tf_op jit(solution)/shard_map/all_to_all | solution.py:78
  207.7 13.5 %all-to-all-done.4 = f32[128,1,1024]{2,1,0:T(1,128)S(1)} async-done(((f32[128,1,1024]{2,1,0:T(1,128)}), f32[128,1,1024]{2,1,0:T(1,128)S(1)}, u32[]{:S(2)}, u32[]{:S(2)}) %all-to-all-start.4) | async-done | bytes 524320 | tf_op jit(solution)/shard_map/all_to_all | solution.py:78
  221.2 1.2 reduce.7
  222.8 6.0 %fusion.58 = f32[448,4096]{1,0:T(8,128)S(1)} fusion(f32[32,448]{1,0:T(8,128)S(1)} %get-tuple-element.22, f32[32,4096]{1,0:T(8,128)S(1)} %reshape.54), kind=kOutput, calls=%fused_computation.99 | convolution fusion | flops 704643072 | bytes 7921664 | tf_op jit(solution)/shard_map/dot_general | solution.py:81
  228.8 2.9 %copy-done = f32[448,4096]{1,0:T(8,128)} copy-done((f32[448,4096]{1,0:T(8,128)}, f32[448,4096]{1,0:T(8,128)S(1)}, u32[]{:S(2)}) %copy-start) | copy-done | bytes 7340056
  231.7 3.4 %multiply_subtract_fusion = (f32[1024,448]{0,1:T(8,128)}, f32[1024,448]{0,1:T(8,128)}, f32[1024,448]{0,1:T(8,128)}) fusion(f32[1024,448]{0,1:T(8,128)S(1)} %copy-done.3, f32[448,4096]{1,0:T(8,128)S(1)} %fusion.58, s32[]{:T(128)S(6)} %select_n.8, f32[1024,448]{0,1:T(8,128)S(1)} %copy-done.4, f32[1024,448]{0,1:T(8,128)S(1)} %copy-done.5), kind=kLoop, calls=%fused_computation.25 | loop fusion | flops 6422528 | bytes 12845060 | tf_op jit(solution)/shard_map/sub | solution.py:95
  235.1 13.8 %fusion.9 = bf16[448,2048]{1,0:T(8,128)(2,1)S(1)} fusion(f32[448,4096]{1,0:T(8,128)} %copy-done, bf16[4096,2048]{1,0:T(8,128)(2,1)} %all-gather.3.cloned.1.call-done, bf16[448,4096]{1,0:T(8,128)(2,1)} %bitcast.87, bf16[32,448,128]{2,1,0:T(8,128)(2,1)} %all-to-all-done.1), kind=kOutput, calls=%fused_computation.11 | convolution fusion | flops 7520780288 | bytes 27787264 | tf_op jit(solution)/shard_map/dot_general | solution.py:36
  249.0 14.1 %fusion.8 = bf16[448,2048]{1,0:T(8,128)(2,1)S(1)} fusion(f32[448,4096]{1,0:T(8,128)} %copy-done, bf16[4096,2048]{1,0:T(8,128)(2,1)} %all-gather.5.cloned.1.call-done, bf16[448,4096]{1,0:T(8,128)(2,1)} %bitcast.88, bf16[32,448,128]{2,1,0:T(8,128)(2,1)} %all-to-all-done.1), kind=kOutput, calls=%fused_computation.9 | convolution fusion | flops 7520780288 | bytes 27787264 | tf_op jit(solution)/shard_map/dot_general | solution.py:36
  263.1 2.1 maximum_bitcast_fusion
  (40 shorter events, 2.2 us)
Async XLA Ops:
  7.2 4.4 %copy-start.1 = (bf16[128,4096]{1,0:T(8,128)(2,1)S(1)}, bf16[128,4096]{1,0:T(8,128)(2,1)}, u32[]{:S(2)}) copy-start(bf16[128,4096]{1,0:T(8,128)(2,1)} %param.7) | copy-start | bytes 3145732
  7.2 228.0 %all-gather.3.cloned.1.call-start = ((), (), s32[]{:S(2)}) async-start(), calls=%async_computation.5 | async-start | bytes 17301504 | tf_op jit(solution)/shard_map/all_gather | solution.py:55
  9.6 239.4 %all-gather.5.cloned.1.call-start = ((), (), s32[]{:S(2)}) async-start(), calls=%async_computation.6 | async-start | bytes 17301504 | tf_op jit(solution)/shard_map/all_gather | solution.py:55
  12.9 24.6 %all-to-all-start = ((f32[32,32,128]{2,1,0:T(8,128)}), f32[32,32,128]{2,1,0:T(8,128)S(1)}, u32[]{:S(2)}, u32[]{:S(2)}) async-start(f32[32,32,128]{2,1,0:T(8,128)} %broadcast_in_dim.8), calls=%async_computation | async-start | bytes 1048576 | tf_op jit(solution)/shard_map/all_to_all | solution.py:59
  37.4 76.4 %all-to-all-start.1 = ((bf16[32,448,128]{2,1,0:T(8,128)(2,1)}), bf16[32,448,128]{2,1,0:T(8,128)(2,1)}, u32[]{:S(2)}, u32[]{:S(2)}) async-start(bf16[32,448,128]{2,1,0:T(8,128)(2,1)} %bitcast.86), calls=%async_computation.1 | async-start | bytes 7340032 | tf_op jit(solution)/shard_map/all_to_all | solution.py:61
  117.2 3.9 %collective-permute-start = (f32[32,448]{1,0:T(8,128)S(1)}, f32[32,448]{1,0:T(8,128)S(1)}, u32[]{:S(2)}, u32[]{:S(2)}) collective-permute-start(f32[32,448]{1,0:T(8,128)S(1)} %fusion.35), channel_id=1, source_target_pairs={{0,32},{32,0},{64,96},{96,64},{1,33},{33,1},{65,97},{97,65},{2,34}... | collective-permute-start | bytes 172040 | tf_op jit(solution)/shard_map/ppermute | solution.py:27
  118.6 4.9 %collective-permute-start.1 = (f32[32,448]{1,0:T(8,128)S(1)}, f32[32,448]{1,0:T(8,128)S(1)}, u32[]{:S(2)}, u32[]{:S(2)}) collective-permute-start(f32[32,448]{1,0:T(8,128)S(1)} %fusion.35), channel_id=1, source_target_pairs={{0,64},{32,96},{64,0},{96,32},{1,65},{33,97},{65,1},{97,33},{2,66}... | collective-permute-start | bytes 172040 | tf_op jit(solution)/shard_map/ppermute | solution.py:27
  121.1 4.3 %collective-permute-start.2 = (f32[32,448]{1,0:T(8,128)S(1)}, f32[32,448]{1,0:T(8,128)S(1)}, u32[]{:S(2)}, u32[]{:S(2)}) collective-permute-start(f32[32,448]{1,0:T(8,128)S(1)} %fusion.35), channel_id=1, source_target_pairs={{0,96},{32,64},{64,32},{96,0},{1,97},{33,65},{65,33},{97,1},{2,98}... | collective-permute-start | bytes 172040 | tf_op jit(solution)/shard_map/ppermute | solution.py:27
  125.6 6.6 %collective-permute-start.3 = (f32[32,32]{0,1:T(8,128)S(1)}, f32[32,32]{0,1:T(8,128)S(1)}, u32[]{:S(2)}, u32[]{:S(2)}) collective-permute-start(f32[32,32]{0,1:T(8,128)S(1)} %fusion.57), channel_id=1, source_target_pairs={{0,1},{1,0},{2,3},{3,2},{4,5},{5,4},{6,7},{7,6},{8,9},{9,8},{10,11... | collective-permute-start | bytes 12296 | tf_op jit(solution)/shard_map/ppermute | solution.py:27
  132.3 4.8 %collective-permute-start.4 = (f32[32,32]{0,1:T(8,128)S(1)}, f32[32,32]{0,1:T(8,128)S(1)}, u32[]{:S(2)}, u32[]{:S(2)}) collective-permute-start(f32[32,32]{0,1:T(8,128)S(1)} %add.115), channel_id=1, source_target_pairs={{0,2},{2,0},{4,6},{6,4},{1,3},{3,1},{5,7},{7,5},{8,10},{10,8},{12,... | collective-permute-start | bytes 12296 | tf_op jit(solution)/shard_map/ppermute | solution.py:27
  134.7 4.4 %collective-permute-start.5 = (f32[32,32]{0,1:T(8,128)S(1)}, f32[32,32]{0,1:T(8,128)S(1)}, u32[]{:S(2)}, u32[]{:S(2)}) collective-permute-start(f32[32,32]{0,1:T(8,128)S(1)} %add.115), channel_id=1, source_target_pairs={{0,4},{2,6},{4,0},{6,2},{1,5},{3,7},{5,1},{7,3},{8,12},{10,14},{12... | collective-permute-start | bytes 12296 | tf_op jit(solution)/shard_map/ppermute | solution.py:27
  136.9 4.5 %collective-permute-start.6 = (f32[32,32]{0,1:T(8,128)S(1)}, f32[32,32]{0,1:T(8,128)S(1)}, u32[]{:S(2)}, u32[]{:S(2)}) collective-permute-start(f32[32,32]{0,1:T(8,128)S(1)} %add.115), channel_id=1, source_target_pairs={{0,6},{2,4},{4,2},{6,0},{1,7},{3,5},{5,3},{7,1},{8,14},{10,12},{12... | collective-permute-start | bytes 12296 | tf_op jit(solution)/shard_map/ppermute | solution.py:27
  141.4 3.9 %collective-permute-start.7 = (f32[32,32]{0,1:T(8,128)S(1)}, f32[32,32]{0,1:T(8,128)S(1)}, u32[]{:S(2)}, u32[]{:S(2)}) collective-permute-start(f32[32,32]{0,1:T(8,128)S(1)} %add_add_fusion.1), channel_id=1, source_target_pairs={{0,8},{8,0},{16,24},{24,16},{1,9},{9,1},{17,25},{25,17},{2,10},{10... | collective-permute-start | bytes 12296 | tf_op jit(solution)/shard_map/ppermute | solution.py:27
  141.5 4.6 %collective-permute-start.8 = (f32[32,32]{0,1:T(8,128)S(1)}, f32[32,32]{0,1:T(8,128)S(1)}, u32[]{:S(2)}, u32[]{:S(2)}) collective-permute-start(f32[32,32]{0,1:T(8,128)S(1)} %add_add_fusion.1), channel_id=1, source_target_pairs={{0,16},{8,24},{16,0},{24,8},{1,17},{9,25},{17,1},{25,9},{2,18},{10... | collective-permute-start | bytes 12296 | tf_op jit(solution)/shard_map/ppermute | solution.py:27
  142.6 4.5 %collective-permute-start.9 = (f32[32,32]{0,1:T(8,128)S(1)}, f32[32,32]{0,1:T(8,128)S(1)}, u32[]{:S(2)}, u32[]{:S(2)}) collective-permute-start(f32[32,32]{0,1:T(8,128)S(1)} %add_add_fusion.1), channel_id=1, source_target_pairs={{0,24},{8,16},{16,8},{24,0},{1,25},{9,17},{17,9},{25,1},{2,26},{10... | collective-permute-start | bytes 12296 | tf_op jit(solution)/shard_map/ppermute | solution.py:27
  157.8 22.7 %all-to-all-start.2 = ((f32[32,32,128]{2,1,0:T(8,128)}), f32[32,32,128]{2,1,0:T(8,128)S(1)}, u32[]{:S(2)}, u32[]{:S(2)}) async-start(f32[32,32,128]{2,1,0:T(8,128)} %bitcast_bitcast_fusion), calls=%async_computation.2 | async-start | bytes 1048576 | tf_op jit(solution)/shard_map/all_to_all | solution.py:74
  201.9 19.4 %all-to-all-start.4 = ((f32[128,1,1024]{2,1,0:T(1,128)}), f32[128,1,1024]{2,1,0:T(1,128)S(1)}, u32[]{:S(2)}, u32[]{:S(2)}) async-start(f32[128,1,1024]{2,1,0:T(1,128)} %broadcast_in_dim.9), calls=%async_computation.4 | async-start | bytes 1048576 | tf_op jit(solution)/shard_map/all_to_all | solution.py:78
  222.7 6.0 %copy-start.2 = (f32[32,4096]{1,0:T(8,128)}, f32[32,4096]{1,0:T(8,128)S(1)}, u32[]{:S(2)}) copy-start(f32[32,4096]{1,0:T(8,128)S(1)} %reshape.54) | copy-start | bytes 1572868
  222.7 8.9 %copy-start.3 = (f32[1024,448]{0,1:T(8,128)S(1)}, f32[1024,448]{0,1:T(8,128)}, u32[]{:S(2)}) copy-start(f32[1024,448]{0,1:T(8,128)} %param.11) | copy-start | bytes 5505028
  222.8 8.9 %copy-start.4 = (f32[1024,448]{0,1:T(8,128)S(1)}, f32[1024,448]{0,1:T(8,128)}, u32[]{:S(2)}) copy-start(f32[1024,448]{0,1:T(8,128)} %param.12) | copy-start | bytes 5505028
  222.8 8.9 %copy-start.5 = (f32[1024,448]{0,1:T(8,128)S(1)}, f32[1024,448]{0,1:T(8,128)}, u32[]{:S(2)}) copy-start(f32[1024,448]{0,1:T(8,128)} %param.13) | copy-start | bytes 5505028
  228.8 2.9 %copy-start = (f32[448,4096]{1,0:T(8,128)}, f32[448,4096]{1,0:T(8,128)S(1)}, u32[]{:S(2)}) copy-start(f32[448,4096]{1,0:T(8,128)S(1)} %fusion.58) | copy-start | bytes 22020100
Sparse Core Ops, SparseCore 0:
  10.3 111.6 all-gather.2
  124.2 84.5 all-gather.4

commit v2 on v1

v2 whole, which is shorter than its diff:
```python
import jax
import jax.numpy as jnp
from jax import lax
from jax.experimental import pallas as pl
from jax.experimental.pallas import tpu as pltpu
from jax.sharding import Mesh, PartitionSpec as P

beta_one = 0.9
beta_two = 0.95
learn_rate = 0.01
decay_rate = 0.1
adam_epsilon = 1e-08
first_fix = 1.0 - 0.9**8
second_fix = 1.0 - 0.95**8

SHARD = ("z", "y", "core")
ALL = ("outer", "z", "y", "core")
CHIPS = ("outer", "z", "y")
VMEM_LIMIT = 48 * 1024 * 1024


def split3(x):
    high = lax.reduce_precision(x, 8, 7)
    rest = x - high
    middle = lax.reduce_precision(rest, 8, 7)
    return [p.astype(jnp.bfloat16) for p in (high, middle, rest - middle)]


def dot(a, b, ca, cb):
    return lax.dot_general(a, b, (((ca,), (cb,)), ((), ())), preferred_element_type=jnp.float32)


def thrice(x, b, cb):
    r = x.shape[0]
    y = dot(jnp.concatenate(split3(x), 0), b, 1, cb)
    return y[:r] + y[r : 2 * r] + y[2 * r :]


def swap(x, axis, k):
    return lax.ppermute(x, axis, [(i, i ^ k) for i in range(lax.axis_size(axis))])


def twin(x):
    return swap(x, "core", 1)


def sum4(x, axis):
    a, b, c = swap(x, axis, 1), swap(x, axis, 2), swap(x, axis, 3)
    return (x + a) + (b + c)


def pick(x, i, axis):
    return lax.dynamic_index_in_dim(x, i, axis, keepdims=False)


def scatter4(x, axis, dim):
    i = lax.axis_index(axis)
    a, b, c = (swap(pick(x, i ^ k, dim), axis, k) for k in (1, 2, 3))
    return (pick(x, i, dim) + a) + (b + c)


def gather_axis(x, axis):
    n = lax.axis_size(axis)
    i = lax.axis_index(axis)
    x = jnp.stack([x] + [swap(x, axis, k) for k in range(1, n)])
    bit = 1
    while bit < n:
        y = x.reshape((n // (2 * bit), 2, bit) + x.shape[1:])
        x = jnp.where((i & bit) != 0, y[:, ::-1], y).reshape(x.shape)
        bit *= 2
    return x


def project(core, factor3, got):
    shards, cols, tok = got.shape
    rank = factor3.shape[0] // 3
    chips = shards // 2
    step = min(4, chips)

    def body(c, f_ref, g_ref, keep_ref, send_ref):
        own = c[0] == 0
        for k in range(step):
            pair = jnp.concatenate([g_ref[2 * k], g_ref[2 * k + 1]], axis=1)
            y = jnp.dot(f_ref[...], pair, preferred_element_type=jnp.float32)
            y = y[:rank] + y[rank : 2 * rank] + y[2 * rank :]
            first, second = y[:, :tok], y[:, tok:]
            keep_ref[k] = jnp.where(own, first, second)
            send_ref[k] = jnp.where(own, second, first)

    block = pl.BlockSpec((step, rank, tok), lambda n, c: (n, 0, 0))
    return pl.pallas_call(
        body,
        out_shape=[jax.ShapeDtypeStruct((chips, rank, tok), jnp.float32)] * 2,
        grid_spec=pltpu.PrefetchScalarGridSpec(
            num_scalar_prefetch=1,
            grid=(chips // step,),
            in_specs=[
                pl.BlockSpec((3 * rank, cols), lambda n, c: (0, 0)),
                pl.BlockSpec((2 * step, cols, tok), lambda n, c: (n, 0, 0)),
            ],
            out_specs=[block, block],
        ),
        compiler_params=pltpu.CompilerParams(vmem_limit_bytes=VMEM_LIMIT),
        cost_estimate=pl.CostEstimate(flops=6 * rank * cols * shards * tok, bytes_accessed=2 * shards * cols * tok, transcendentals=0),
    )(core, factor3, got)


def finish(place, ortho6, basis6, matrix, weight, moment_one, moment_two):
    cols, rows = weight.shape
    width = matrix.shape[1]
    steps = min(8, width // 128)
    block = width // steps
    small = rows // steps
    depth6 = ortho6.shape[1]

    def body(p, ortho_ref, basis_ref, own_ref, matrix_ref, w_ref, one_ref, two_ref, e_out, w_out, one_out, two_out):
        approx = jnp.dot(ortho_ref[...], basis_ref[...], preferred_element_type=jnp.float32)
        e_out[...] = (matrix_ref[...] - approx).astype(jnp.bfloat16)
        update = jnp.dot(ortho_ref[...], own_ref[...], preferred_element_type=jnp.float32)
        one = beta_one * one_ref[...] + (1.0 - beta_one) * update
        two = beta_two * two_ref[...] + (1.0 - beta_two) * update * update
        step = one / first_fix / (jnp.sqrt(two / second_fix) + adam_epsilon)
        w_out[...] = w_ref[...] * (1.0 - learn_rate * decay_rate) - learn_rate * step
        one_out[...] = one
        two_out[...] = two

    own = pl.BlockSpec((cols, small), lambda n, p: (0, n))
    wide = pl.BlockSpec((cols, block), lambda n, p: (0, n))
    return pl.pallas_call(
        body,
        out_shape=[jax.ShapeDtypeStruct(matrix.shape, jnp.bfloat16)] + [jax.ShapeDtypeStruct(weight.shape, jnp.float32)] * 3,
        grid_spec=pltpu.PrefetchScalarGridSpec(
            num_scalar_prefetch=1,
            grid=(steps,),
            in_specs=[
                pl.BlockSpec((cols, depth6), lambda n, p: (0, 0)),
                pl.BlockSpec((depth6, block), lambda n, p: (0, n)),
                pl.BlockSpec((depth6, small), lambda n, p: (0, p[0] * steps + n)),
                wide,
                own,
                own,
                own,
            ],
            out_specs=[wide, own, own, own],
        ),
        compiler_params=pltpu.CompilerParams(vmem_limit_bytes=VMEM_LIMIT),
        cost_estimate=pl.CostEstimate(
            flops=2 * cols * (rows + width) * depth6, bytes_accessed=24 * cols * rows + 6 * cols * width, transcendentals=cols * rows
        ),
    )(place, ortho6, basis6, basis6, matrix, weight, moment_one, moment_two)


def per_device(acts, grads, basis, error_in, weight, moment_one, moment_two):
    highest = lax.Precision.HIGHEST
    shards = lax.axis_size(SHARD)
    chips = lax.axis_size(CHIPS)
    pods = lax.axis_size("outer")
    tok, width = acts.shape
    cols = error_in.shape[2]
    rank = basis.shape[0]
    scale = (tok * shards) ** (-0.5)
    core = lax.axis_index("core")
    error_t = error_in[0].T
    gathered = lax.all_gather(acts, SHARD, axis=0, tiled=True)

    proj = gather_axis(gather_axis(thrice(basis, acts, 1) * scale, "core"), "y")
    grads_t, proj = lax.optimization_barrier((grads.T.reshape(shards, cols, tok), proj))
    got = lax.all_to_all(grads_t, SHARD, 0, 0)
    got_t = got.transpose(1, 0, 2).reshape(cols, shards * tok)
    proj = gather_axis(proj, "z").reshape(shards, rank, tok).transpose(1, 0, 2).reshape(rank, shards * tok)
    base = thrice(basis, error_t, 1)

    factor = sum4(thrice(proj, got_t, 1) + base, "outer") / pods
    factor3 = jnp.concatenate(split3(factor), 0)
    keep, send = project(core.astype(jnp.int32).reshape(1), factor3, got)
    inner = (keep + twin(send)).reshape(4, 4, rank, tok)
    inner = scatter4(scatter4(inner, "y", 1), "z", 0) * scale
    terms = thrice(inner, acts, 0) + thrice(factor, error_t, 0)
    rows = rank // 2
    mine = lax.dynamic_slice_in_dim(terms, core * rows, rows, 0)
    other = lax.dynamic_slice_in_dim(terms, (1 - core) * rows, rows, 0)
    tiles = (rows // 8, 8, width // 128, 128)
    mine = (mine + twin(other)).reshape(tiles).transpose(0, 2, 1, 3).reshape(chips, -1, 128)
    piece = lax.all_to_all(mine, CHIPS, 0, 0, tiled=True).sum(0) / pods
    mine = lax.all_to_all(jnp.broadcast_to(piece[None], mine.shape), CHIPS, 0, 0, tiled=True)
    other = twin(mine)
    terms = jnp.concatenate([jnp.where(core == 0, mine, other), jnp.where(core == 0, other, mine)], 0)
    terms = terms.reshape(rank // 8, width // 128, 8, 128).transpose(0, 2, 1, 3).reshape(rank, width)

    gram = jnp.dot(factor, factor.T, precision=highest)
    gram = gram + twin(gram)
    gram = sum4(sum4(gram, "y"), "z")
    lower = jnp.linalg.cholesky(gram)
    inverse = jax.scipy.linalg.solve_triangular(lower, jnp.eye(rank, dtype=jnp.float32), lower=True)
    ortho = jnp.dot(inverse, factor, precision=highest)
    basis_out = jnp.dot(inverse, terms, precision=highest)

    oh, om, ol = split3(ortho)
    bh, bm, bl = split3(basis_out)
    ortho6 = jnp.concatenate([oh, oh, om, oh, ol, om], 0).T
    basis6 = jnp.concatenate([bh, bm, bh, bl, bh, bm], 0)

    matrix = dot(got_t, gathered, 1, 0) * scale + error_t.astype(jnp.float32)
    place = lax.axis_index("outer").astype(jnp.int32).reshape(1)
    error_out, *state = finish(place, ortho6, basis6, matrix, weight.T, moment_one.T, moment_two.T)
    return (basis_out, error_out.T[None], state[0].T, state[1].T, state[2].T)


def solution(mesh):
    devices = mesh.devices
    mesh = Mesh(devices.reshape(devices.shape[0], 4, 4, -1), ALL)
    tokens = P(ALL, None)
    state = P("outer", SHARD)
    errors = P("outer", None, SHARD)
    return jax.shard_map(
        per_device,
        mesh=mesh,
        in_specs=(tokens, tokens, P(), errors, state, state, state),
        out_specs=(P(), errors, state, state, state),
        check_vma=False,
    )
```

time: 273 us -> 226 us (0.83)
  waiting for transfers between devices: 115 us -> 79.7 us
  blocking collectives: 18.6 us -> 0 us
  Pallas kernels: 0 us -> 13.9 us
  starting transfers between devices: 45.8 us -> 59 us
  matrix products: 47.5 us -> 36.1 us
  other arithmetic: 16.3 us -> 10.2 us
  local copies, waits for them, and re-layouts: 14.3 us -> 11.5 us
    all_to_all x4 -> x3, waiting for transfers between devices: 103 us -> 11.7 us  [the longest x1 5.97 us: per_device(): lax.all_to_all(jnp.broadcast_to(piece[None], mine.shape), CHIPS, 0, 0, ti...]
    ppermute x10 -> x26, waiting for transfers between devices: 11.1 us -> 67.3 us  [swap(): lax.ppermute(x, axis, [(i, i ^ k) for i in range(lax.axis_size(axis))])]
    ppermute x10 -> x26, starting transfers between devices: 18.5 us -> 39 us  [swap(): lax.ppermute(x, axis, [(i, i ^ k) for i in range(lax.axis_size(axis))])]
    all_to_all x1 -> x0, blocking collectives: 18.6 us -> none  [per_device(): lax.all_to_all(terms.reshape(devices, -1), ALL, 0, 0, tiled=True).sum(0)]
    pallas_call x0 -> x2, Pallas kernels: none -> 13.9 us  [the longest x1 10.6 us: finish(): pl.pallas_call(body, out_shape=[jax.ShapeDtypeStruct(matrix.shape, jnp.bf...]
    all_to_all x4 -> x3, starting transfers between devices: 27.2 us -> 19.9 us  [the longest x1 7.88 us: per_device(): piece = lax.all_to_all(mine, CHIPS, 0, 0, tiled=True).sum(0) / pods]
    dot_general x8 -> x6, matrix products: 41.1 us -> 34.9 us  [dot(): lax.dot_general(a, b, (((ca,), (cb,)), ((), ())), preferred_element_type=...]
    transpose x0 -> x1, local copies, waits for them, and re-layouts: none -> 6.04 us  [per_device(): grads.T.reshape(shards, cols, tok)]
  transfers between devices with their start and end apart: 16 -> 30, of which waited for: 11 -> 17; matrix products, arithmetic and copies ran while one was open for 21% -> 13% of each run, Pallas kernels for 0% -> 1%
where the time goes in v2:
time: 226 us; the launch traced here: 225 us
  waiting for transfers between devices  79.7 us (35%)
  starting transfers between devices  59 us (26%)
  matrix products  36.1 us (16%)
  between operations  14.5 us (6%)
  Pallas kernels  13.9 us (6%)
  local copies, waits for them, and re-layouts  11.5 us (5%)
  other arithmetic  10.2 us (5%)
    ppermute x26, waiting for transfers between devices, swap(): lax.ppermute(x, axis, [(i, i ^ k) for i in range(lax.axis_size(axis))])  67.3 us
    ppermute x26, starting transfers between devices, swap(): lax.ppermute(x, axis, [(i, i ^ k) for i in range(lax.axis_size(axis))])  39 us
    dot_general x6, matrix products, dot(): lax.dot_general(a, b, (((ca,), (cb,)), ((), ())), preferred_element_type=...  34.9 us
    pallas_call x1, Pallas kernels, finish(): pl.pallas_call(body, out_shape=[jax.ShapeDtypeStruct(matrix.shape, jnp.bf...  10.6 us
    all_to_all x1, starting transfers between devices, per_device(): piece = lax.all_to_all(mine, CHIPS, 0, 0, tiled=True).sum(0) / pods  7.88 us
    all_to_all x1, starting transfers between devices, per_device(): got = lax.all_to_all(grads_t, SHARD, 0, 0)  7.34 us
    transpose x1, local copies, waits for them, and re-layouts, per_device(): grads.T.reshape(shards, cols, tok)  6.04 us
    all_to_all x1, waiting for transfers between devices, per_device(): lax.all_to_all(jnp.broadcast_to(piece[None], mine.shape), CHIPS, 0, 0, ti...  5.97 us
  transfers between devices with their start and end apart: 30, of which 17 were waited for; matrix products, arithmetic and copies ran while one was open for 13% of the time, Pallas kernels for 1%

profile of v2, /device:TPU:1, one launch (start us, length us, event | category | flops | bytes accessed | tf_op | source)
XLA Modules:
  0.0 224.8 jit_solution(2869556676667689098)
XLA Ops:
  7.9 1.2 reduce-precision_convert_fusion.5
  9.6 1.5 collective-permute-start
  11.1 6.0 %copy.26 = bf16[14336,128]{1,0:T(8,128)(2,1)} copy(bf16[14336,128]{0,1:T(8,128)(2,1)} %bitcast.121) | data formatting | bytes 7340032 | tf_op jit(solution)/shard_map/transpose | solution.py:167
  17.1 3.1 %collective-permute-start.2 = (f32[2,32,128]{2,1,0:T(8,128)S(1)}, f32[2,32,128]{2,1,0:T(8,128)S(1)}, u32[]{:S(2)}, u32[]{:S(2)}) collective-permute-start(f32[2,32,128]{2,1,0:T(8,128)S(1)} %reverse_select_fusion.4), channel_id=1, source_target_pairs={{0,4},{2,6},{4,0},{6,2},{1,5},{3,7},{5,1},{7,3},{8,12},{10,14},{12... | collective-permute-start | bytes 98312 | tf_op jit(solution)/shard_map/ppermute | solution.py:40
  21.5 1.5 collective-permute-done.1
  23.0 1.6 collective-permute-done.3
  24.7 7.3 %all-to-all-start = ((bf16[32,448,128]{2,1,0:T(8,128)(2,1)}), bf16[32,448,128]{2,1,0:T(8,128)(2,1)}, u32[]{:S(2)}, u32[]{:S(2)}) async-start(bf16[32,448,128]{2,1,0:T(8,128)(2,1)} %bitcast.120), calls=%async_computation | async-start | bytes 7340032 | tf_op jit(solution)/shard_map/all_to_all | solution.py:168
  32.0 2.7 %collective-permute-start.6 = (f32[4,2,32,128]{3,2,1,0:T(8,128)S(1)}, f32[4,2,32,128]{3,2,1,0:T(8,128)S(1)}, u32[]{:S(2)}, u32[]{:S(2)}) collective-permute-start(f32[4,2,32,128]{3,2,1,0:T(8,128)S(1)} %bitcast.129), channel_id=1, source_target_pairs={{0,24},{8,16},{16,8},{24,0},{1,25},{9,17},{17,9},{25,1},{2,26},{10... | collective-permute-start | bytes 393224 | tf_op jit(solution)/shard_map/ppermute | solution.py:40
  35.4 3.3 %fusion.5 = f32[96,448]{1,0:T(8,128)S(1)} fusion(bf16[1,4096,448]{1,2,0:T(8,128)(2,1)} %param.10, bf16[32,4096]{1,0:T(8,128)(2,1)S(1)} %get-tuple-element.31, bf16[32,4096]{1,0:T(8,128)(2,1)S(1)} %get-tuple-element.32, bf16[32,4096]{1,0:T(8,128)(2,1)S(1)} %get-tuple-element.30), kind=kOutput, calls=%fused_computation.6 | convolution fusion | flops 354680832 | bytes 4628480 | tf_op jit(solution)/shard_map/dot_general | solution.py:30
  38.7 47.5 %collective-permute-done.6 = f32[4,2,32,128]{3,2,1,0:T(8,128)S(1)} collective-permute-done((f32[4,2,32,128]{3,2,1,0:T(8,128)S(1)}, f32[4,2,32,128]{3,2,1,0:T(8,128)S(1)}, u32[]{:S(2)}, u32[]{:S(2)}) %collective-permute-start.6) | collective-permute-done | bytes 131104 | tf_op jit(solution)/shard_map/ppermute | solution.py:40
  86.2 1.7 collective-permute-done.5
  87.9 1.5 collective-permute-done.4
  90.6 3.2 %fusion.1 = f32[96,448]{1,0:T(8,128)S(1)} fusion(bf16[32,4096]{1,0:T(8,128)(2,1)S(1)} %get-tuple-element.28, bf16[32,4096]{1,0:T(8,128)(2,1)S(1)} %get-tuple-element.29, bf16[32,4096]{1,0:T(8,128)(2,1)S(1)} %get-tuple-element.27, bf16[32,448,128]{2,1,0:T(8,128)(2,1)} %all-to-all-done.g_ref), kind=kOutput, calls=%fused_computation.2 | convolution fusion | flops 354680832 | bytes 4628480 | tf_op jit(solution)/shard_map/dot_general | solution.py:30
  93.9 2.5 %collective-permute-start.9 = (f32[32,448]{1,0:T(8,128)S(1)}, f32[32,448]{1,0:T(8,128)S(1)}, u32[]{:S(2)}, u32[]{:S(2)}) collective-permute-start(f32[32,448]{1,0:T(8,128)S(1)} %fusion.24), channel_id=1, source_target_pairs={{0,96},{32,64},{64,32},{96,0},{1,97},{33,65},{65,33},{97,1},{2,98}... | collective-permute-start | bytes 172040 | tf_op jit(solution)/shard_map/ppermute | solution.py:40
  97.2 1.1 collective-permute-done.9
  98.3 2.7 %collective-permute-done.8 = f32[32,448]{1,0:T(8,128)S(1)} collective-permute-done((f32[32,448]{1,0:T(8,128)S(1)}, f32[32,448]{1,0:T(8,128)S(1)}, u32[]{:S(2)}, u32[]{:S(2)}) %collective-permute-start.8) | collective-permute-done | bytes 57376 | tf_op jit(solution)/shard_map/ppermute | solution.py:40
  101.2 3.3 %shard_map.110 = (f32[16,32,128]{2,1,0:T(8,128)S(1)}, f32[16,32,128]{2,1,0:T(8,128)S(1)}) custom-call(s32[1]{0:T(128)} %bitcast.24.c, bf16[96,448]{1,0:T(8,128)(2,1)S(1)} %pad_maximum_fusion.6.f_ref, bf16[32,448,128]{2,1,0:T(8,128)(2,1)} %all-to-all-done.g_ref), custom_call_target="tpu_custom_call" | custom-call | flops 352321536 | bytes 3670016 | tf_op jit(solution)/shard_map/pallas_call | solution.py:91
  104.5 2.0 collective-permute-start.17
  106.5 1.2 collective-permute-done.17
  107.8 3.4 %collective-permute-start.20 = (f32[4,32,128]{2,1,0:T(8,128)S(1)}, f32[4,32,128]{2,1,0:T(8,128)S(1)}, u32[]{:S(2)}, u32[]{:S(2)}) collective-permute-start(f32[4,32,128]{2,1,0:T(8,128)S(1)} %get-tuple-element.35), channel_id=1, source_target_pairs={{0,6},{2,4},{4,2},{6,0},{1,7},{3,5},{5,3},{7,1},{8,14},{10,12},{12... | collective-permute-start | bytes 196616 | tf_op jit(solution)/shard_map/ppermute | solution.py:40
  112.0 1.0 collective-permute-start.10
  113.0 2.1 collective-permute-done.20
  115.1 2.7 %collective-permute-done.19 = f32[4,32,128]{2,1,0:T(8,128)S(1)} collective-permute-done((f32[4,32,128]{2,1,0:T(8,128)S(1)}, f32[4,32,128]{2,1,0:T(8,128)S(1)}, u32[]{:S(2)}, u32[]{:S(2)}) %collective-permute-start.19) | collective-permute-done | bytes 65568 | tf_op jit(solution)/shard_map/ppermute | solution.py:40
  118.6 2.3 %collective-permute-start.23 = (f32[32,128]{1,0:T(8,128)S(1)}, f32[32,128]{1,0:T(8,128)S(1)}, u32[]{:S(2)}, u32[]{:S(2)}) collective-permute-start(f32[32,128]{1,0:T(8,128)S(1)} %get-tuple-element.40), channel_id=1, source_target_pairs={{0,24},{8,16},{16,8},{24,0},{1,25},{9,17},{17,9},{25,1},{2,26},{10... | collective-permute-start | bytes 49160 | tf_op jit(solution)/shard_map/ppermute | solution.py:40
  121.0 0.9 collective-permute-start.22
  121.9 2.8 %fusion.3 = f32[96,4096]{1,0:T(8,128)S(1)} fusion(bf16[1,4096,448]{1,2,0:T(8,128)(2,1)} %param.10, bf16[32,448]{1,0:T(8,128)(2,1)S(1)} %get-tuple-element.43, bf16[32,448]{1,0:T(8,128)(2,1)S(1)} %get-tuple-element.42, bf16[32,448]{1,0:T(8,128)(2,1)S(1)} %get-tuple-element.23), kind=kOutput, calls=%fused_computation.4 | convolution fusion | flops 352579584 | bytes 5328896 | tf_op jit(solution)/shard_map/dot_general | solution.py:30
  124.7 2.5 %collective-permute-start.13 = (f32[32,32]{0,1:T(8,128)S(1)}, f32[32,32]{0,1:T(8,128)S(1)}, u32[]{:S(2)}, u32[]{:S(2)}) collective-permute-start(f32[32,32]{0,1:T(8,128)S(1)} %add.147), channel_id=1, source_target_pairs={{0,6},{2,4},{4,2},{6,0},{1,7},{3,5},{5,3},{7,1},{8,14},{10,12},{12... | collective-permute-start | bytes 12296 | tf_op jit(solution)/shard_map/ppermute | solution.py:40
  127.3 0.7 collective-permute-start.11
  128.7 3.0 %collective-permute-start.24 = (f32[16,4096]{1,0:T(8,128)S(1)}, f32[16,4096]{1,0:T(8,128)S(1)}, u32[]{:S(2)}, u32[]{:S(2)}) collective-permute-start(f32[16,4096]{1,0:T(8,128)S(1)} %constant_dynamic-slice_fusion), channel_id=1, source_target_pairs={{0,1},{1,0},{2,3},{3,2},{4,5},{5,4},{6,7},{7,6},{8,9},{9,8},{10,11... | collective-permute-start | bytes 786440 | tf_op jit(solution)/shard_map/ppermute | solution.py:40
  131.7 1.5 collective-permute-start.16
  133.2 1.2 collective-permute-start.15
  134.4 0.8 collective-permute-start.14
  135.2 1.3 collective-permute-done.16
  136.5 1.2 collective-permute-done.15
  137.8 0.7 dynamic-slice_add_fusion
  138.5 7.9 %all-to-all-start.1 = ((f32[64,8,128]{2,1,0:T(8,128)}), f32[64,8,128]{2,1,0:T(8,128)S(1)}, u32[]{:S(2)}, u32[]{:S(2)}) async-start(f32[64,8,128]{2,1,0:T(8,128)} %bitcast.36), calls=%async_computation.1 | async-start | bytes 524288 | tf_op jit(solution)/shard_map/all_to_all | solution.py:184
  146.4 2.9 %cholesky.17 = f32[32,32]{1,0:T(8,128)S(1)} custom-call(f32[32,32]{1,0:T(8,128)S(1)} %fusion.41), custom_call_target="Cholesky" | custom-call | tf_op jit(solution)/shard_map/jit(cholesky)/cholesky | solution.py:193
  150.0 5.7 %all-to-all-done.1 = f32[64,8,128]{2,1,0:T(8,128)S(1)} async-done(((f32[64,8,128]{2,1,0:T(8,128)}), f32[64,8,128]{2,1,0:T(8,128)S(1)}, u32[]{:S(2)}, u32[]{:S(2)}) %all-to-all-start.1) | async-done | bytes 262176 | tf_op jit(solution)/shard_map/all_to_all | solution.py:184
  155.8 0.7 broadcast_in_dim.6
  156.5 4.7 %all-to-all-start.2 = ((f32[64,8,128]{2,1,0:T(8,128)}), f32[64,8,128]{2,1,0:T(8,128)S(1)}, u32[]{:S(2)}, u32[]{:S(2)}) async-start(f32[64,8,128]{2,1,0:T(8,128)} %broadcast_in_dim.6), calls=%async_computation.2 | async-start | bytes 524288 | tf_op jit(solution)/shard_map/all_to_all | solution.py:185
  161.9 2.4 %custom-call.7 = f32[1,32,32]{1,2,0:T(8,128)S(1)} custom-call(f32[1,32,32]{2,1,0:T(8,128)S(1)} %fusion.34), custom_call_target="InvertDiagBlocksLowerTriangular" | custom-call | tf_op jit(solution)/shard_map/jit(_solve_triangular)/triangular_solve | solution.py:194
  164.5 6.0 %all-to-all-done.2 = f32[64,8,128]{2,1,0:T(8,128)S(1)} async-done(((f32[64,8,128]{2,1,0:T(8,128)}), f32[64,8,128]{2,1,0:T(8,128)S(1)}, u32[]{:S(2)}, u32[]{:S(2)}) %all-to-all-start.2) | async-done | bytes 262176 | tf_op jit(solution)/shard_map/all_to_all | solution.py:185
  170.5 6.6 %collective-permute-start.25 = (f32[64,8,128]{2,1,0:T(8,128)S(1)}, f32[64,8,128]{2,1,0:T(8,128)S(1)}, u32[]{:S(2)}, u32[]{:S(2)}) collective-permute-start(f32[64,8,128]{2,1,0:T(8,128)S(1)} %all-to-all-done.2), channel_id=1, source_target_pairs={{0,1},{1,0},{2,3},{3,2},{4,5},{5,4},{6,7},{7,6},{8,9},{9,8},{10,11... | collective-permute-start | bytes 786440 | tf_op jit(solution)/shard_map/ppermute | solution.py:40
  177.7 0.9 concatenate.28
  180.2 24.8 %bitcast_add_fusion.matrix_ref = f32[448,4096]{1,0:T(8,128)} fusion(bf16[4096,4096]{1,0:T(8,128)(2,1)} %all-gather.2.cloned.1.call-done, bf16[1,4096,448]{1,2,0:T(8,128)(2,1)} %param.10, bf16[32,448,128]{2,1,0:T(8,128)(2,1)} %all-to-all-done.g_ref), kind=kOutput, calls=%fused_computation | convolution fusion | flops 15037890560 | bytes 48234496 | tf_op jit(solution)/shard_map/dot_general | solution.py:30
  204.9 1.5 copy-done.1
  206.4 0.9 copy-done.2
  207.4 10.6 %shard_map.111 = (bf16[448,4096]{1,0:T(8,128)(2,1)}, f32[448,1024]{1,0:T(8,128)}, f32[448,1024]{1,0:T(8,128)}, f32[448,1024]{1,0:T(8,128)}) custom-call(s32[1]{0:T(128)} %bitcast.40.p, bf16[448,192]{1,0:T(8,128)(2,1)S(1)} %bitcast.119, bf16[192,4096]{1,0:T(8,128)(2,1)S(1)} %fusion.27.basis_ref.own_ref, bf16[192,4096]{1,0:T(8,128)(2,1)S(1)} %fusion.27.basis_ref.own_ref, ...), custom_call_target="tpu_custom_call" | custom-call | flops 880803840 | bytes 22020096 | tf_op jit(solution)/shard_map/pallas_call | solution.py:129
  (87 shorter events, 11.6 us)
Async XLA Ops:
  7.2 1.9 copy-start.4
  7.2 173.0 %all-gather.2.cloned.1.call-start = ((), (), s32[]{:S(2)}) async-start(), calls=%async_computation.3 | async-start | bytes 34603008 | tf_op jit(solution)/shard_map/all_gather | solution.py:164
  9.6 7.6 %collective-permute-start = (f32[32,128]{1,0:T(8,128)S(1)}, f32[32,128]{1,0:T(8,128)S(1)}, u32[]{:S(2)}, u32[]{:S(2)}) collective-permute-start(f32[32,128]{1,0:T(8,128)S(1)} %fusion.36), channel_id=1, source_target_pairs={{0,1},{1,0},{2,3},{3,2},{4,5},{5,4},{6,7},{7,6},{8,9},{9,8},{10,11... | collective-permute-start | bytes 49160 | tf_op jit(solution)/shard_map/ppermute | solution.py:40
  17.1 4.4 %collective-permute-start.2 = (f32[2,32,128]{2,1,0:T(8,128)S(1)}, f32[2,32,128]{2,1,0:T(8,128)S(1)}, u32[]{:S(2)}, u32[]{:S(2)}) collective-permute-start(f32[2,32,128]{2,1,0:T(8,128)S(1)} %reverse_select_fusion.4), channel_id=1, source_target_pairs={{0,4},{2,6},{4,0},{6,2},{1,5},{3,7},{5,1},{7,3},{8,12},{10,14},{12... | collective-permute-start | bytes 98312 | tf_op jit(solution)/shard_map/ppermute | solution.py:40
  20.2 2.8 %collective-permute-start.1 = (f32[2,32,128]{2,1,0:T(8,128)S(1)}, f32[2,32,128]{2,1,0:T(8,128)S(1)}, u32[]{:S(2)}, u32[]{:S(2)}) collective-permute-start(f32[2,32,128]{2,1,0:T(8,128)S(1)} %reverse_select_fusion.4), channel_id=1, source_target_pairs={{0,2},{2,0},{4,6},{6,4},{1,3},{3,1},{5,7},{7,5},{8,10},{10,8},{12,... | collective-permute-start | bytes 98312 | tf_op jit(solution)/shard_map/ppermute | solution.py:40
  20.6 4.0 %collective-permute-start.3 = (f32[2,32,128]{2,1,0:T(8,128)S(1)}, f32[2,32,128]{2,1,0:T(8,128)S(1)}, u32[]{:S(2)}, u32[]{:S(2)}) collective-permute-start(f32[2,32,128]{2,1,0:T(8,128)S(1)} %reverse_select_fusion.4), channel_id=1, source_target_pairs={{0,6},{2,4},{4,2},{6,0},{1,7},{3,5},{5,3},{7,1},{8,14},{10,12},{12... | collective-permute-start | bytes 98312 | tf_op jit(solution)/shard_map/ppermute | solution.py:40
  24.7 66.0 %all-to-all-start = ((bf16[32,448,128]{2,1,0:T(8,128)(2,1)}), bf16[32,448,128]{2,1,0:T(8,128)(2,1)}, u32[]{:S(2)}, u32[]{:S(2)}) async-start(bf16[32,448,128]{2,1,0:T(8,128)(2,1)} %bitcast.120), calls=%async_computation | async-start | bytes 7340032 | tf_op jit(solution)/shard_map/all_to_all | solution.py:168
  32.0 54.2 %collective-permute-start.6 = (f32[4,2,32,128]{3,2,1,0:T(8,128)S(1)}, f32[4,2,32,128]{3,2,1,0:T(8,128)S(1)}, u32[]{:S(2)}, u32[]{:S(2)}) collective-permute-start(f32[4,2,32,128]{3,2,1,0:T(8,128)S(1)} %bitcast.129), channel_id=1, source_target_pairs={{0,24},{8,16},{16,8},{24,0},{1,25},{9,17},{17,9},{25,1},{2,26},{10... | collective-permute-start | bytes 393224 | tf_op jit(solution)/shard_map/ppermute | solution.py:40
  34.7 53.2 %collective-permute-start.5 = (f32[4,2,32,128]{3,2,1,0:T(8,128)S(1)}, f32[4,2,32,128]{3,2,1,0:T(8,128)S(1)}, u32[]{:S(2)}, u32[]{:S(2)}) collective-permute-start(f32[4,2,32,128]{3,2,1,0:T(8,128)S(1)} %bitcast.130), channel_id=1, source_target_pairs={{0,16},{8,24},{16,0},{24,8},{1,17},{9,25},{17,1},{25,9},{2,18},{10... | collective-permute-start | bytes 393224 | tf_op jit(solution)/shard_map/ppermute | solution.py:40
  35.3 54.2 %collective-permute-start.4 = (f32[4,2,32,128]{3,2,1,0:T(8,128)S(1)}, f32[4,2,32,128]{3,2,1,0:T(8,128)S(1)}, u32[]{:S(2)}, u32[]{:S(2)}) collective-permute-start(f32[4,2,32,128]{3,2,1,0:T(8,128)S(1)} %bitcast.131), channel_id=1, source_target_pairs={{0,8},{8,0},{16,24},{24,16},{1,9},{9,1},{17,25},{25,17},{2,10},{10... | collective-permute-start | bytes 393224 | tf_op jit(solution)/shard_map/ppermute | solution.py:40
  93.9 4.4 %collective-permute-start.9 = (f32[32,448]{1,0:T(8,128)S(1)}, f32[32,448]{1,0:T(8,128)S(1)}, u32[]{:S(2)}, u32[]{:S(2)}) collective-permute-start(f32[32,448]{1,0:T(8,128)S(1)} %fusion.24), channel_id=1, source_target_pairs={{0,96},{32,64},{64,32},{96,0},{1,97},{33,65},{65,33},{97,1},{2,98}... | collective-permute-start | bytes 172040 | tf_op jit(solution)/shard_map/ppermute | solution.py:40
  96.4 4.6 %collective-permute-start.8 = (f32[32,448]{1,0:T(8,128)S(1)}, f32[32,448]{1,0:T(8,128)S(1)}, u32[]{:S(2)}, u32[]{:S(2)}) collective-permute-start(f32[32,448]{1,0:T(8,128)S(1)} %fusion.24), channel_id=1, source_target_pairs={{0,64},{32,96},{64,0},{96,32},{1,65},{33,97},{65,1},{97,33},{2,66}... | collective-permute-start | bytes 172040 | tf_op jit(solution)/shard_map/ppermute | solution.py:40
  97.0 4.2 %collective-permute-start.7 = (f32[32,448]{1,0:T(8,128)S(1)}, f32[32,448]{1,0:T(8,128)S(1)}, u32[]{:S(2)}, u32[]{:S(2)}) collective-permute-start(f32[32,448]{1,0:T(8,128)S(1)} %fusion.24), channel_id=1, source_target_pairs={{0,32},{32,0},{64,96},{96,64},{1,33},{33,1},{65,97},{97,65},{2,34}... | collective-permute-start | bytes 172040 | tf_op jit(solution)/shard_map/ppermute | solution.py:40
  104.5 3.2 %collective-permute-start.17 = (f32[16,32,128]{2,1,0:T(8,128)S(1)}, f32[16,32,128]{2,1,0:T(8,128)S(1)}, u32[]{:S(2)}, u32[]{:S(2)}) collective-permute-start(f32[16,32,128]{2,1,0:T(8,128)S(1)} %get-tuple-element.16), channel_id=1, source_target_pairs={{0,1},{1,0},{2,3},{3,2},{4,5},{5,4},{6,7},{7,6},{8,9},{9,8},{10,11... | collective-permute-start | bytes 786440 | tf_op jit(solution)/shard_map/ppermute | solution.py:40
  107.8 7.3 %collective-permute-start.20 = (f32[4,32,128]{2,1,0:T(8,128)S(1)}, f32[4,32,128]{2,1,0:T(8,128)S(1)}, u32[]{:S(2)}, u32[]{:S(2)}) collective-permute-start(f32[4,32,128]{2,1,0:T(8,128)S(1)} %get-tuple-element.35), channel_id=1, source_target_pairs={{0,6},{2,4},{4,2},{6,0},{1,7},{3,5},{5,3},{7,1},{8,14},{10,12},{12... | collective-permute-start | bytes 196616 | tf_op jit(solution)/shard_map/ppermute | solution.py:40
  111.2 6.6 %collective-permute-start.19 = (f32[4,32,128]{2,1,0:T(8,128)S(1)}, f32[4,32,128]{2,1,0:T(8,128)S(1)}, u32[]{:S(2)}, u32[]{:S(2)}) collective-permute-start(f32[4,32,128]{2,1,0:T(8,128)S(1)} %get-tuple-element.36), channel_id=1, source_target_pairs={{0,4},{2,6},{4,0},{6,2},{1,5},{3,7},{5,1},{7,3},{8,12},{10,14},{12... | collective-permute-start | bytes 196616 | tf_op jit(solution)/shard_map/ppermute | solution.py:40
  111.2 7.3 %collective-permute-start.18 = (f32[4,32,128]{2,1,0:T(8,128)S(1)}, f32[4,32,128]{2,1,0:T(8,128)S(1)}, u32[]{:S(2)}, u32[]{:S(2)}) collective-permute-start(f32[4,32,128]{2,1,0:T(8,128)S(1)} %get-tuple-element.37), channel_id=1, source_target_pairs={{0,2},{2,0},{4,6},{6,4},{1,3},{3,1},{5,7},{7,5},{8,10},{10,8},{12,... | collective-permute-start | bytes 196616 | tf_op jit(solution)/shard_map/ppermute | solution.py:40
  112.0 12.7 %collective-permute-start.10 = (f32[32,32]{0,1:T(8,128)S(1)}, f32[32,32]{0,1:T(8,128)S(1)}, u32[]{:S(2)}, u32[]{:S(2)}) collective-permute-start(f32[32,32]{0,1:T(8,128)S(1)} %fusion.48), channel_id=1, source_target_pairs={{0,1},{1,0},{2,3},{3,2},{4,5},{5,4},{6,7},{7,6},{8,9},{9,8},{10,11... | collective-permute-start | bytes 12296 | tf_op jit(solution)/shard_map/ppermute | solution.py:40
  118.5 8.8 %collective-permute-start.21 = (f32[32,128]{1,0:T(8,128)S(1)}, f32[32,128]{1,0:T(8,128)S(1)}, u32[]{:S(2)}, u32[]{:S(2)}) collective-permute-start(f32[32,128]{1,0:T(8,128)S(1)} %get-tuple-element.39), channel_id=1, source_target_pairs={{0,8},{8,0},{16,24},{24,16},{1,9},{9,1},{17,25},{25,17},{2,10},{10... | collective-permute-start | bytes 49160 | tf_op jit(solution)/shard_map/ppermute | solution.py:40
  118.6 9.4 %collective-permute-start.23 = (f32[32,128]{1,0:T(8,128)S(1)}, f32[32,128]{1,0:T(8,128)S(1)}, u32[]{:S(2)}, u32[]{:S(2)}) collective-permute-start(f32[32,128]{1,0:T(8,128)S(1)} %get-tuple-element.40), channel_id=1, source_target_pairs={{0,24},{8,16},{16,8},{24,0},{1,25},{9,17},{17,9},{25,1},{2,26},{10... | collective-permute-start | bytes 49160 | tf_op jit(solution)/shard_map/ppermute | solution.py:40
  121.0 7.1 %collective-permute-start.22 = (f32[32,128]{1,0:T(8,128)S(1)}, f32[32,128]{1,0:T(8,128)S(1)}, u32[]{:S(2)}, u32[]{:S(2)}) collective-permute-start(f32[32,128]{1,0:T(8,128)S(1)} %get-tuple-element.41), channel_id=1, source_target_pairs={{0,16},{8,24},{16,0},{24,8},{1,17},{9,25},{17,1},{25,9},{2,18},{10... | collective-permute-start | bytes 49160 | tf_op jit(solution)/shard_map/ppermute | solution.py:40
  124.7 7.0 %collective-permute-start.13 = (f32[32,32]{0,1:T(8,128)S(1)}, f32[32,32]{0,1:T(8,128)S(1)}, u32[]{:S(2)}, u32[]{:S(2)}) collective-permute-start(f32[32,32]{0,1:T(8,128)S(1)} %add.147), channel_id=1, source_target_pairs={{0,6},{2,4},{4,2},{6,0},{1,7},{3,5},{5,3},{7,1},{8,14},{10,12},{12... | collective-permute-start | bytes 12296 | tf_op jit(solution)/shard_map/ppermute | solution.py:40
  127.2 4.5 %collective-permute-start.12 = (f32[32,32]{0,1:T(8,128)S(1)}, f32[32,32]{0,1:T(8,128)S(1)}, u32[]{:S(2)}, u32[]{:S(2)}) collective-permute-start(f32[32,32]{0,1:T(8,128)S(1)} %add.147), channel_id=1, source_target_pairs={{0,4},{2,6},{4,0},{6,2},{1,5},{3,7},{5,1},{7,3},{8,12},{10,14},{12... | collective-permute-start | bytes 12296 | tf_op jit(solution)/shard_map/ppermute | solution.py:40
  127.3 4.3 %collective-permute-start.11 = (f32[32,32]{0,1:T(8,128)S(1)}, f32[32,32]{0,1:T(8,128)S(1)}, u32[]{:S(2)}, u32[]{:S(2)}) collective-permute-start(f32[32,32]{0,1:T(8,128)S(1)} %add.147), channel_id=1, source_target_pairs={{0,2},{2,0},{4,6},{6,4},{1,3},{3,1},{5,7},{7,5},{8,10},{10,8},{12,... | collective-permute-start | bytes 12296 | tf_op jit(solution)/shard_map/ppermute | solution.py:40
  128.7 9.1 %collective-permute-start.24 = (f32[16,4096]{1,0:T(8,128)S(1)}, f32[16,4096]{1,0:T(8,128)S(1)}, u32[]{:S(2)}, u32[]{:S(2)}) collective-permute-start(f32[16,4096]{1,0:T(8,128)S(1)} %constant_dynamic-slice_fusion), channel_id=1, source_target_pairs={{0,1},{1,0},{2,3},{3,2},{4,5},{5,4},{6,7},{7,6},{8,9},{9,8},{10,11... | collective-permute-start | bytes 786440 | tf_op jit(solution)/shard_map/ppermute | solution.py:40
  131.7 4.8 %collective-permute-start.16 = (f32[32,32]{0,1:T(8,128)S(1)}, f32[32,32]{0,1:T(8,128)S(1)}, u32[]{:S(2)}, u32[]{:S(2)}) collective-permute-start(f32[32,32]{0,1:T(8,128)S(1)} %add_add_fusion.1), channel_id=1, source_target_pairs={{0,24},{8,16},{16,8},{24,0},{1,25},{9,17},{17,9},{25,1},{2,26},{10... | collective-permute-start | bytes 12296 | tf_op jit(solution)/shard_map/ppermute | solution.py:40
  133.2 4.5 %collective-permute-start.15 = (f32[32,32]{0,1:T(8,128)S(1)}, f32[32,32]{0,1:T(8,128)S(1)}, u32[]{:S(2)}, u32[]{:S(2)}) collective-permute-start(f32[32,32]{0,1:T(8,128)S(1)} %add_add_fusion.1), channel_id=1, source_target_pairs={{0,16},{8,24},{16,0},{24,8},{1,17},{9,25},{17,1},{25,9},{2,18},{10... | collective-permute-start | bytes 12296 | tf_op jit(solution)/shard_map/ppermute | solution.py:40
  134.4 3.3 %collective-permute-start.14 = (f32[32,32]{0,1:T(8,128)S(1)}, f32[32,32]{0,1:T(8,128)S(1)}, u32[]{:S(2)}, u32[]{:S(2)}) collective-permute-start(f32[32,32]{0,1:T(8,128)S(1)} %add_add_fusion.1), channel_id=1, source_target_pairs={{0,8},{8,0},{16,24},{24,16},{1,9},{9,1},{17,25},{25,17},{2,10},{10... | collective-permute-start | bytes 12296 | tf_op jit(solution)/shard_map/ppermute | solution.py:40
  138.5 17.2 %all-to-all-start.1 = ((f32[64,8,128]{2,1,0:T(8,128)}), f32[64,8,128]{2,1,0:T(8,128)S(1)}, u32[]{:S(2)}, u32[]{:S(2)}) async-start(f32[64,8,128]{2,1,0:T(8,128)} %bitcast.36), calls=%async_computation.1 | async-start | bytes 524288 | tf_op jit(solution)/shard_map/all_to_all | solution.py:184
  156.5 14.0 %all-to-all-start.2 = ((f32[64,8,128]{2,1,0:T(8,128)}), f32[64,8,128]{2,1,0:T(8,128)S(1)}, u32[]{:S(2)}, u32[]{:S(2)}) async-start(f32[64,8,128]{2,1,0:T(8,128)} %broadcast_in_dim.6), calls=%async_computation.2 | async-start | bytes 524288 | tf_op jit(solution)/shard_map/all_to_all | solution.py:185
  170.5 8.1 %collective-permute-start.25 = (f32[64,8,128]{2,1,0:T(8,128)S(1)}, f32[64,8,128]{2,1,0:T(8,128)S(1)}, u32[]{:S(2)}, u32[]{:S(2)}) collective-permute-start(f32[64,8,128]{2,1,0:T(8,128)S(1)} %all-to-all-done.2), channel_id=1, source_target_pairs={{0,1},{1,0},{2,3},{3,2},{4,5},{5,4},{6,7},{7,6},{8,9},{9,8},{10,11... | collective-permute-start | bytes 786440 | tf_op jit(solution)/shard_map/ppermute | solution.py:40
  179.3 0.8 copy-start.3
  180.1 24.8 %copy-start = (f32[1024,448]{0,1:T(8,128)S(1)}, f32[1024,448]{0,1:T(8,128)}, u32[]{:S(2)}) copy-start(f32[1024,448]{0,1:T(8,128)} %param.11) | copy-start | bytes 5505028
  204.9 1.5 copy-start.1
  206.4 0.9 copy-start.2
Sparse Core Ops, SparseCore 0:
  10.3 169.5 all-gather.1

commit v3 on v2

--- a/solution.py
+++ b/solution.py
@@ -47,16 +47,6 @@
 def sum4(x, axis):
     a, b, c = swap(x, axis, 1), swap(x, axis, 2), swap(x, axis, 3)
     return (x + a) + (b + c)
-
-
-def pick(x, i, axis):
-    return lax.dynamic_index_in_dim(x, i, axis, keepdims=False)
-
-
-def scatter4(x, axis, dim):
-    i = lax.axis_index(axis)
-    a, b, c = (swap(pick(x, i ^ k, dim), axis, k) for k in (1, 2, 3))
-    return (pick(x, i, dim) + a) + (b + c)
 
 
 def gather_axis(x, axis):
@@ -71,52 +61,105 @@
     return x
 
 
-def project(core, factor3, got):
+def parts3(x):
+    high = x.astype(jnp.bfloat16)
+    rest = x - high.astype(jnp.float32)
+    middle = rest.astype(jnp.bfloat16)
+    return high, middle, (rest - middle.astype(jnp.float32)).astype(jnp.bfloat16)
+
+
+def project(core, factor, factor3, got):
     shards, cols, tok = got.shape
-    rank = factor3.shape[0] // 3
+    rank = factor.shape[0]
     chips = shards // 2
     step = min(4, chips)
 
-    def body(c, f_ref, g_ref, keep_ref, send_ref):
+    def body(c, f_ref, f3_ref, g_ref, keep_ref, send_ref, gram_ref):
         own = c[0] == 0
+
+        @pl.when(pl.program_id(0) == 0)
+        def _():
+            h, m, l = parts3(f_ref[...])
+            gram = dot(h, l, 1, 1) + dot(l, h, 1, 1) + dot(m, m, 1, 1)
+            gram = gram + (dot(h, m, 1, 1) + dot(m, h, 1, 1)) + dot(h, h, 1, 1)
+            gram_ref[...] = jnp.concatenate([gram, jnp.zeros((rank, tok - rank), jnp.float32)], axis=1)
+
         for k in range(step):
             pair = jnp.concatenate([g_ref[2 * k], g_ref[2 * k + 1]], axis=1)
-            y = jnp.dot(f_ref[...], pair, preferred_element_type=jnp.float32)
+            y = jnp.dot(f3_ref[...], pair, preferred_element_type=jnp.float32)
             y = y[:rank] + y[rank : 2 * rank] + y[2 * rank :]
             first, second = y[:, :tok], y[:, tok:]
-            keep_ref[k] = jnp.where(own, first, second)
-            send_ref[k] = jnp.where(own, second, first)
-
-    block = pl.BlockSpec((step, rank, tok), lambda n, c: (n, 0, 0))
+            keep_ref[k, :rank] = jnp.where(own, first, second)
+            send_ref[k, :rank] = jnp.where(own, second, first)
+            keep_ref[k, rank:] = gram_ref[...]
+            send_ref[k, rank:] = gram_ref[...]
+
+    block = pl.BlockSpec((step, 2 * rank, tok), lambda n, c: (n, 0, 0))
     return pl.pallas_call(
         body,
-        out_shape=[jax.ShapeDtypeStruct((chips, rank, tok), jnp.float32)] * 2,
+        out_shape=[jax.ShapeDtypeStruct((chips, 2 * rank, tok), jnp.float32)] * 2,
         grid_spec=pltpu.PrefetchScalarGridSpec(
             num_scalar_prefetch=1,
             grid=(chips // step,),
             in_specs=[
+                pl.BlockSpec((rank, cols), lambda n, c: (0, 0)),
                 pl.BlockSpec((3 * rank, cols), lambda n, c: (0, 0)),
                 pl.BlockSpec((2 * step, cols, tok), lambda n, c: (n, 0, 0)),
             ],
             out_specs=[block, block],
+            scratch_shapes=[pltpu.VMEM((rank, tok), jnp.float32)],
         ),
         compiler_params=pltpu.CompilerParams(vmem_limit_bytes=VMEM_LIMIT),
         cost_estimate=pl.CostEstimate(flops=6 * rank * cols * shards * tok, bytes_accessed=2 * shards * cols * tok, transcendentals=0),
-    )(core, factor3, got)
-
-
-def finish(place, ortho6, basis6, matrix, weight, moment_one, moment_two):
+    )(core, factor, factor3, got)
+
+
+def finish_error(got, gathered, error_t, ortho6, basis6, scale):
+    shards, cols, tok = got.shape
+    tokens, width = gathered.shape
+    block = min(1024, width)
+    depth6 = ortho6.shape[1]
+
+    def body(got_ref, acts_ref, error_ref, ortho_ref, basis_ref, out_ref, columns):
+        @pl.when(pl.program_id(0) == 0)
+        def _():
+            for s in range(shards):
+                columns[:, s * tok : (s + 1) * tok] = got_ref[s]
+
+        gradient = jnp.dot(columns[...], acts_ref[...], preferred_element_type=jnp.float32)
+        approx = jnp.dot(ortho_ref[...], basis_ref[...], preferred_element_type=jnp.float32)
+        matrix = gradient * scale + error_ref[...].astype(jnp.float32)
+        out_ref[...] = (matrix - approx).astype(jnp.bfloat16)
+
+    wide = pl.BlockSpec((cols, block), lambda n: (0, n))
+    return pl.pallas_call(
+        body,
+        out_shape=jax.ShapeDtypeStruct(error_t.shape, jnp.bfloat16),
+        grid=(width // block,),
+        in_specs=[
+            pl.BlockSpec((shards, cols, tok), lambda n: (0, 0, 0)),
+            pl.BlockSpec((tokens, block), lambda n: (0, n)),
+            wide,
+            pl.BlockSpec((cols, depth6), lambda n: (0, 0)),
+            pl.BlockSpec((depth6, block), lambda n: (0, n)),
+        ],
+        out_specs=wide,
+        scratch_shapes=[pltpu.VMEM((cols, tokens), got.dtype)],
+        compiler_params=pltpu.CompilerParams(vmem_limit_bytes=VMEM_LIMIT),
+        cost_estimate=pl.CostEstimate(
+            flops=2 * cols * width * (tokens + depth6), bytes_accessed=2 * tokens * (width + cols) + 4 * cols * width, transcendentals=0
+        ),
+    )(got, gathered, error_t, ortho6, basis6)
+
+
+def adam(place, ortho6, basis6, weight, moment_one, moment_two):
     cols, rows = weight.shape
-    width = matrix.shape[1]
-    steps = min(8, width // 128)
-    block = width // steps
-    small = rows // steps
+    block = min(256, rows)
+    steps = rows // block
     depth6 = ortho6.shape[1]
 
-    def body(p, ortho_ref, basis_ref, own_ref, matrix_ref, w_ref, one_ref, two_ref, e_out, w_out, one_out, two_out):
-        approx = jnp.dot(ortho_ref[...], basis_ref[...], preferred_element_type=jnp.float32)
-        e_out[...] = (matrix_ref[...] - approx).astype(jnp.bfloat16)
-        update = jnp.dot(ortho_ref[...], own_ref[...], preferred_element_type=jnp.float32)
+    def body(p, ortho_ref, basis_ref, w_ref, one_ref, two_ref, w_out, one_out, two_out):
+        update = jnp.dot(ortho_ref[...], basis_ref[...], preferred_element_type=jnp.float32)
         one = beta_one * one_ref[...] + (1.0 - beta_one) * update
         two = beta_two * two_ref[...] + (1.0 - beta_two) * update * update
         step = one / first_fix / (jnp.sqrt(two / second_fix) + adam_epsilon)
@@ -124,30 +167,25 @@
         one_out[...] = one
         two_out[...] = two
 
-    own = pl.BlockSpec((cols, small), lambda n, p: (0, n))
-    wide = pl.BlockSpec((cols, block), lambda n, p: (0, n))
+    own = pl.BlockSpec((cols, block), lambda n, p: (0, n))
     return pl.pallas_call(
         body,
-        out_shape=[jax.ShapeDtypeStruct(matrix.shape, jnp.bfloat16)] + [jax.ShapeDtypeStruct(weight.shape, jnp.float32)] * 3,
+        out_shape=[jax.ShapeDtypeStruct(weight.shape, jnp.float32)] * 3,
         grid_spec=pltpu.PrefetchScalarGridSpec(
             num_scalar_prefetch=1,
             grid=(steps,),
             in_specs=[
                 pl.BlockSpec((cols, depth6), lambda n, p: (0, 0)),
-                pl.BlockSpec((depth6, block), lambda n, p: (0, n)),
-                pl.BlockSpec((depth6, small), lambda n, p: (0, p[0] * steps + n)),
-                wide,
+                pl.BlockSpec((depth6, block), lambda n, p: (0, p[0] * steps + n)),
                 own,
                 own,
                 own,
             ],
-            out_specs=[wide, own, own, own],
+            out_specs=[own, own, own],
         ),
         compiler_params=pltpu.CompilerParams(vmem_limit_bytes=VMEM_LIMIT),
-        cost_estimate=pl.CostEstimate(
-            flops=2 * cols * (rows + width) * depth6, bytes_accessed=24 * cols * rows + 6 * cols * width, transcendentals=cols * rows
-        ),
-    )(place, ortho6, basis6, basis6, matrix, weight, moment_one, moment_two)
+        cost_estimate=pl.CostEstimate(flops=2 * cols * rows * depth6, bytes_accessed=24 * cols * rows, transcendentals=cols * rows),
+    )(place, ortho6, basis6, weight, moment_one, moment_two)
 
 
 def per_device(acts, grads, basis, error_in, weight, moment_one, moment_two):
@@ -172,10 +210,10 @@
 
     factor = sum4(thrice(proj, got_t, 1) + base, "outer") / pods
     factor3 = jnp.concatenate(split3(factor), 0)
-    keep, send = project(core.astype(jnp.int32).reshape(1), factor3, got)
-    inner = (keep + twin(send)).reshape(4, 4, rank, tok)
-    inner = scatter4(scatter4(inner, "y", 1), "z", 0) * scale
-    terms = thrice(inner, acts, 0) + thrice(factor, error_t, 0)
+    keep, send = project(core.astype(jnp.int32).reshape(1), factor, factor3, got)
+    inner = lax.all_to_all(keep + twin(send), ("z", "y"), 0, 0, tiled=True).sum(0)
+    gram = inner[rank:, :rank]
+    terms = thrice(inner[:rank] * scale, acts, 0) + thrice(factor, error_t, 0)
     rows = rank // 2
     mine = lax.dynamic_slice_in_dim(terms, core * rows, rows, 0)
     other = lax.dynamic_slice_in_dim(terms, (1 - core) * rows, rows, 0)
@@ -187,9 +225,6 @@
     terms = jnp.concatenate([jnp.where(core == 0, mine, other), jnp.where(core == 0, other, mine)], 0)
     terms = terms.reshape(rank // 8, width // 128, 8, 128).transpose(0, 2, 1, 3).reshape(rank, width)
 
-    gram = jnp.dot(factor, factor.T, precision=highest)
-    gram = gram + twin(gram)
-    gram = sum4(sum4(gram, "y"), "z")
     lower = jnp.linalg.cholesky(gram)
     inverse = jax.scipy.linalg.solve_triangular(lower, jnp.eye(rank, dtype=jnp.float32), lower=True)
     ortho = jnp.dot(inverse, factor, precision=highest)
@@ -200,9 +235,9 @@
     ortho6 = jnp.concatenate([oh, oh, om, oh, ol, om], 0).T
     basis6 = jnp.concatenate([bh, bm, bh, bl, bh, bm], 0)
 
-    matrix = dot(got_t, gathered, 1, 0) * scale + error_t.astype(jnp.float32)
     place = lax.axis_index("outer").astype(jnp.int32).reshape(1)
-    error_out, *state = finish(place, ortho6, basis6, matrix, weight.T, moment_one.T, moment_two.T)
+    state = adam(place, ortho6, basis6, weight.T, moment_one.T, moment_two.T)
+    error_out = finish_error(got, gathered, error_t, ortho6, basis6, scale)
     return (basis_out, error_out.T[None], state[0].T, state[1].T, state[2].T)
 
 

time: 226 us -> 214 us (0.947)
  matrix products: 36.1 us -> 11.1 us
  Pallas kernels: 13.9 us -> 32.5 us
  starting transfers between devices: 59 us -> 41.8 us
  waiting for transfers between devices: 79.7 us -> 93.1 us
    dot_general x6 -> x5, matrix products: 34.9 us -> 10.1 us  [dot(): lax.dot_general(a, b, (((ca,), (cb,)), ((), ())), preferred_element_type=...]
    ppermute x26 -> x13, starting transfers between devices: 39 us -> 17.9 us  [swap(): lax.ppermute(x, axis, [(i, i ^ k) for i in range(lax.axis_size(axis))])]
    pallas_call x2 -> x3, Pallas kernels: 13.9 us -> 32.5 us  [the longest x1 23.7 us: finish_error(): pl.pallas_call(body, out_shape=jax.ShapeDtypeStruct(error_t.shape, jnp.bf...]
    all_to_all x0 -> x1, waiting for transfers between devices: none -> 14.6 us  [per_device(): lax.all_to_all(keep + twin(send), ('z', 'y'), 0, 0, tiled=True).sum(0)]
    all_to_all x0 -> x1, starting transfers between devices: none -> 6.83 us  [per_device(): lax.all_to_all(keep + twin(send), ('z', 'y'), 0, 0, tiled=True).sum(0)]
    ppermute x26 -> x13, waiting for transfers between devices: 67.3 us -> 61.9 us  [swap(): lax.ppermute(x, axis, [(i, i ^ k) for i in range(lax.axis_size(axis))])]
    all_gather x1, waiting for transfers between devices: 0.02 us -> 3.61 us  [per_device(): gathered = lax.all_gather(acts, SHARD, axis=0, tiled=True)]
    all_to_all x1, starting transfers between devices: 7.88 us -> 4.62 us  [per_device(): piece = lax.all_to_all(mine, CHIPS, 0, 0, tiled=True).sum(0) / pods]
  transfers between devices with their start and end apart: 30 -> 18, of which waited for: 17 -> 16; matrix products, arithmetic and copies ran while one was open for 13% -> 14% of each run, Pallas kernels for 1% -> 4%
where the time goes in v3:
time: 214 us; the launch traced here: 213 us
  waiting for transfers between devices  93.1 us (44%)
  starting transfers between devices  41.8 us (20%)
  Pallas kernels  32.5 us (15%)
  between operations  14.4 us (7%)
  matrix products  11.1 us (5%)
  other arithmetic  10.8 us (5%)
  local copies, waits for them, and re-layouts  9.73 us (5%)
    ppermute x13, waiting for transfers between devices, swap(): lax.ppermute(x, axis, [(i, i ^ k) for i in range(lax.axis_size(axis))])  61.9 us
    pallas_call x1, Pallas kernels, finish_error(): pl.pallas_call(body, out_shape=jax.ShapeDtypeStruct(error_t.shape, jnp.bf...  23.7 us
    ppermute x13, starting transfers between devices, swap(): lax.ppermute(x, axis, [(i, i ^ k) for i in range(lax.axis_size(axis))])  17.9 us
    all_to_all x1, waiting for transfers between devices, per_device(): lax.all_to_all(keep + twin(send), ('z', 'y'), 0, 0, tiled=True).sum(0)  14.6 us
    dot_general x5, matrix products, dot(): lax.dot_general(a, b, (((ca,), (cb,)), ((), ())), preferred_element_type=...  10.1 us
    all_to_all x1, starting transfers between devices, per_device(): got = lax.all_to_all(grads_t, SHARD, 0, 0)  7.34 us
    all_to_all x1, starting transfers between devices, per_device(): lax.all_to_all(keep + twin(send), ('z', 'y'), 0, 0, tiled=True).sum(0)  6.83 us
    all_to_all x1, waiting for transfers between devices, per_device(): piece = lax.all_to_all(mine, CHIPS, 0, 0, tiled=True).sum(0) / pods  6.36 us
  transfers between devices with their start and end apart: 18, of which 16 were waited for; matrix products, arithmetic and copies ran while one was open for 14% of the time, Pallas kernels for 4%

profile of v3, /device:TPU:1, one launch (start us, length us, event | category | flops | bytes accessed | tf_op | source)
XLA Modules:
  0.0 213.5 jit_solution(119072477026927729)
XLA Ops:
  7.2 0.7 all-gather.2.cloned.1.call-update
  7.9 1.2 reduce-precision_convert_fusion.5
  9.6 1.5 collective-permute-start
  11.1 6.0 %copy.40 = bf16[14336,128]{1,0:T(8,128)(2,1)} copy(bf16[14336,128]{0,1:T(8,128)(2,1)} %bitcast.89) | data formatting | bytes 7340032 | tf_op jit(solution)/shard_map/transpose | solution.py:205
  17.1 3.1 %collective-permute-start.2 = (f32[2,32,128]{2,1,0:T(8,128)S(1)}, f32[2,32,128]{2,1,0:T(8,128)S(1)}, u32[]{:S(2)}, u32[]{:S(2)}) collective-permute-start(f32[2,32,128]{2,1,0:T(8,128)S(1)} %reverse_select_fusion.4), channel_id=1, source_target_pairs={{0,4},{2,6},{4,0},{6,2},{1,5},{3,7},{5,1},{7,3},{8,12},{10,14},{12... | collective-permute-start | bytes 98312 | tf_op jit(solution)/shard_map/ppermute | solution.py:40
  21.0 0.5 collective-permute-done.2
  21.5 1.5 collective-permute-done.1
  23.0 1.6 collective-permute-done.3
  24.7 7.3 %all-to-all-start = ((bf16[32,448,128]{2,1,0:T(8,128)(2,1)}), bf16[32,448,128]{2,1,0:T(8,128)(2,1)}, u32[]{:S(2)}, u32[]{:S(2)}) async-start(bf16[32,448,128]{2,1,0:T(8,128)(2,1)} %bitcast.88), calls=%async_computation | async-start | bytes 7340032 | tf_op jit(solution)/shard_map/all_to_all | solution.py:206
  32.0 2.7 %collective-permute-start.6 = (f32[4,2,32,128]{3,2,1,0:T(8,128)S(1)}, f32[4,2,32,128]{3,2,1,0:T(8,128)S(1)}, u32[]{:S(2)}, u32[]{:S(2)}) collective-permute-start(f32[4,2,32,128]{3,2,1,0:T(8,128)S(1)} %bitcast.96), channel_id=1, source_target_pairs={{0,24},{8,16},{16,8},{24,0},{1,25},{9,17},{17,9},{25,1},{2,26},{10... | collective-permute-start | bytes 393224 | tf_op jit(solution)/shard_map/ppermute | solution.py:40
  34.7 0.5 collective-permute-start.5
  35.4 3.3 %fusion.5 = f32[96,448]{1,0:T(8,128)S(1)} fusion(bf16[1,4096,448]{1,2,0:T(8,128)(2,1)} %param.10, bf16[32,4096]{1,0:T(8,128)(2,1)S(1)} %get-tuple-element.27, bf16[32,4096]{1,0:T(8,128)(2,1)S(1)} %get-tuple-element.28, bf16[32,4096]{1,0:T(8,128)(2,1)S(1)} %get-tuple-element.26), kind=kOutput, calls=%fused_computation.5 | convolution fusion | flops 354680832 | bytes 4628480 | tf_op jit(solution)/shard_map/dot_general | solution.py:30
  38.7 47.5 %collective-permute-done.6 = f32[4,2,32,128]{3,2,1,0:T(8,128)S(1)} collective-permute-done((f32[4,2,32,128]{3,2,1,0:T(8,128)S(1)}, f32[4,2,32,128]{3,2,1,0:T(8,128)S(1)}, u32[]{:S(2)}, u32[]{:S(2)}) %collective-permute-start.6) | collective-permute-done | bytes 131104 | tf_op jit(solution)/shard_map/ppermute | solution.py:40
  86.2 1.7 collective-permute-done.5
  87.9 1.5 collective-permute-done.4
  90.4 3.2 %fusion = f32[96,448]{1,0:T(8,128)S(1)} fusion(bf16[32,4096]{1,0:T(8,128)(2,1)S(1)} %get-tuple-element.24, bf16[32,4096]{1,0:T(8,128)(2,1)S(1)} %get-tuple-element.25, bf16[32,4096]{1,0:T(8,128)(2,1)S(1)} %get-tuple-element.23, bf16[32,448,128]{2,1,0:T(8,128)(2,1)} %all-to-all-done.g_ref.got_ref), kind=kOutput, calls=%fused_computation | convolution fusion | flops 354680832 | bytes 4628480 | tf_op jit(solution)/shard_map/dot_general | solution.py:30
  93.6 2.5 %collective-permute-start.9 = (f32[32,448]{1,0:T(8,128)S(1)}, f32[32,448]{1,0:T(8,128)S(1)}, u32[]{:S(2)}, u32[]{:S(2)}) collective-permute-start(f32[32,448]{1,0:T(8,128)S(1)} %fusion.22), channel_id=1, source_target_pairs={{0,96},{32,64},{64,32},{96,0},{1,97},{33,65},{65,33},{97,1},{2,98}... | collective-permute-start | bytes 172040 | tf_op jit(solution)/shard_map/ppermute | solution.py:40
  96.1 0.6 collective-permute-start.8
  97.0 1.1 collective-permute-done.9
  98.0 2.7 %collective-permute-done.8 = f32[32,448]{1,0:T(8,128)S(1)} collective-permute-done((f32[32,448]{1,0:T(8,128)S(1)}, f32[32,448]{1,0:T(8,128)S(1)}, u32[]{:S(2)}, u32[]{:S(2)}) %collective-permute-start.8) | collective-permute-done | bytes 57376 | tf_op jit(solution)/shard_map/ppermute | solution.py:40
  100.9 3.5 %shard_map.110 = (f32[16,64,128]{2,1,0:T(8,128)S(1)}, f32[16,64,128]{2,1,0:T(8,128)S(1)}) custom-call(s32[1]{0:T(128)} %bitcast.c, f32[32,448]{1,0:T(8,128)S(1)} %get-tuple-element.20.f_ref, bf16[96,448]{1,0:T(8,128)(2,1)S(1)} %pad_maximum_fusion.6.f3_ref, bf16[32,448,128]{2,1,0:T(8,128)(2,1)} %all-to-all-done.g_ref.got_ref), custom_call_target="tpu_custom_call" | custom-call | flops 352321536 | bytes 3670016 | tf_op jit(solution)/shard_map/pallas_call | solution.py:98
  104.4 2.0 collective-permute-start.10
  106.5 1.5 collective-permute-done.10
  108.0 0.9 add.79
  108.9 6.8 %all-to-all-start.1 = ((f32[16,64,128]{2,1,0:T(8,128)}), f32[16,64,128]{2,1,0:T(8,128)S(1)}, u32[]{:S(2)}, u32[]{:S(2)}) async-start(f32[16,64,128]{2,1,0:T(8,128)} %add.79), calls=%async_computation.1 | async-start | bytes 1048576 | tf_op jit(solution)/shard_map/all_to_all | solution.py:214
  115.7 2.8 %fusion.3 = f32[96,4096]{1,0:T(8,128)S(1)} fusion(bf16[1,4096,448]{1,2,0:T(8,128)(2,1)} %param.10, bf16[32,448]{1,0:T(8,128)(2,1)S(1)} %get-tuple-element.33, bf16[32,448]{1,0:T(8,128)(2,1)S(1)} %get-tuple-element.32, bf16[32,448]{1,0:T(8,128)(2,1)S(1)} %get-tuple-element.19), kind=kOutput, calls=%fused_computation.3 | convolution fusion | flops 352579584 | bytes 5328896 | tf_op jit(solution)/shard_map/dot_general | solution.py:30
  118.5 14.6 %all-to-all-done.1 = f32[16,64,128]{2,1,0:T(8,128)S(1)} async-done(((f32[16,64,128]{2,1,0:T(8,128)}), f32[16,64,128]{2,1,0:T(8,128)S(1)}, u32[]{:S(2)}, u32[]{:S(2)}) %all-to-all-start.1) | async-done | bytes 524320 | tf_op jit(solution)/shard_map/all_to_all | solution.py:214
  133.7 1.4 collective-permute-start.11
  135.2 1.4 collective-permute-done.11
  136.6 0.7 dynamic-slice_add_fusion
  137.3 4.6 %all-to-all-start.2 = ((f32[64,8,128]{2,1,0:T(8,128)}), f32[64,8,128]{2,1,0:T(8,128)S(1)}, u32[]{:S(2)}, u32[]{:S(2)}) async-start(f32[64,8,128]{2,1,0:T(8,128)} %bitcast.27), calls=%async_computation.2 | async-start | bytes 524288 | tf_op jit(solution)/shard_map/all_to_all | solution.py:222
  142.0 2.9 %cholesky.17 = f32[32,32]{1,0:T(8,128)S(1)} custom-call(f32[32,32]{1,0:T(8,128)S(1)} %fusion.36), custom_call_target="Cholesky" | custom-call | tf_op jit(solution)/shard_map/jit(cholesky)/cholesky | solution.py:228
  144.9 0.6 compare_reduce_fusion
  145.6 6.4 %all-to-all-done.2 = f32[64,8,128]{2,1,0:T(8,128)S(1)} async-done(((f32[64,8,128]{2,1,0:T(8,128)}), f32[64,8,128]{2,1,0:T(8,128)S(1)}, u32[]{:S(2)}, u32[]{:S(2)}) %all-to-all-start.2) | async-done | bytes 262176 | tf_op jit(solution)/shard_map/all_to_all | solution.py:222
  152.0 0.7 broadcast_in_dim.6
  152.7 5.1 %all-to-all-start.3 = ((f32[64,8,128]{2,1,0:T(8,128)}), f32[64,8,128]{2,1,0:T(8,128)S(1)}, u32[]{:S(2)}, u32[]{:S(2)}) async-start(f32[64,8,128]{2,1,0:T(8,128)} %broadcast_in_dim.6), calls=%async_computation.3 | async-start | bytes 524288 | tf_op jit(solution)/shard_map/all_to_all | solution.py:223
  157.8 0.7 fusion.31
  158.5 2.4 %custom-call.7 = f32[1,32,32]{1,2,0:T(8,128)S(1)} custom-call(f32[1,32,32]{2,1,0:T(8,128)S(1)} %fusion.31), custom_call_target="InvertDiagBlocksLowerTriangular" | custom-call | tf_op jit(solution)/shard_map/jit(_solve_triangular)/triangular_solve | solution.py:229
  161.2 6.0 %all-to-all-done.3 = f32[64,8,128]{2,1,0:T(8,128)S(1)} async-done(((f32[64,8,128]{2,1,0:T(8,128)}), f32[64,8,128]{2,1,0:T(8,128)S(1)}, u32[]{:S(2)}, u32[]{:S(2)}) %all-to-all-start.3) | async-done | bytes 262176 | tf_op jit(solution)/shard_map/all_to_all | solution.py:223
  167.2 2.4 %collective-permute-start.12 = (f32[64,8,128]{2,1,0:T(8,128)S(1)}, f32[64,8,128]{2,1,0:T(8,128)S(1)}, u32[]{:S(2)}, u32[]{:S(2)}) collective-permute-start(f32[64,8,128]{2,1,0:T(8,128)S(1)} %all-to-all-done.3), channel_id=1, source_target_pairs={{0,1},{1,0},{2,3},{3,2},{4,5},{5,4},{6,7},{7,6},{8,9},{9,8},{10,11... | collective-permute-start | bytes 786440 | tf_op jit(solution)/shard_map/ppermute | solution.py:40
  170.4 0.7 collective-permute-done.12
  171.1 0.6 constant_dynamic-update-slice_fusion.2
  172.0 0.5 copy-done.2
  172.5 0.9 copy-done.1
  173.4 0.6 copy-done
  174.0 5.3 %shard_map.112 = (f32[448,1024]{1,0:T(8,128)}, f32[448,1024]{1,0:T(8,128)}, f32[448,1024]{1,0:T(8,128)}) custom-call(s32[1]{0:T(128)} %bitcast.35.p, bf16[448,192]{1,0:T(8,128)(2,1)S(1)} %bitcast.86, bf16[192,4096]{1,0:T(8,128)(2,1)S(1)} %fusion.24.basis_ref, f32[448,1024]{1,0:T(8,128)S(1)} %bitcast.84, f32[448,1024]{1,0:T(8,128)S(1)} %bitcast.85, ...), custom_call_target="tpu_custom_call" | custom-call | flops 176160768 | bytes 11010048 | tf_op jit(solution)/shard_map/pallas_call | solution.py:171
  179.3 3.6 %all-gather.2.cloned.1.call-done.acts_ref = bf16[4096,4096]{1,0:T(8,128)(2,1)} async-done(((bf16[128,4096]{1,0:T(8,128)(2,1)}), bf16[4096,4096]{1,0:T(8,128)(2,1)}) %all-gather.2.cloned.1.call-update) | async-done | bytes 33554448 | tf_op jit(solution)/shard_map/all_gather | solution.py:202
  182.9 23.7 %shard_map.111 = bf16[448,4096]{1,0:T(8,128)(2,1)} custom-call(bf16[32,448,128]{2,1,0:T(8,128)(2,1)} %all-to-all-done.g_ref.got_ref, bf16[4096,4096]{1,0:T(8,128)(2,1)} %all-gather.2.cloned.1.call-done.acts_ref, bf16[448,4096]{1,0:T(8,128)(2,1)} %bitcast.90, bf16[448,192]{1,0:T(8,128)(2,1)S(1)} %bitcast.87, bf16[192,4096]{1,0:T(8,128)(2,1)S(1)} %fusion.24.basis_ref), custom_call_target="tpu_custom_call" | custom-call | flops 15737028608 | bytes 44564480 | tf_op jit(solution)/shard_map/pallas_call | solution.py:135
  (55 shorter events, 5.0 us)
Async XLA Ops:
  7.2 1.9 copy-start.3
  7.2 175.7 %all-gather.2.cloned.1.call-start = ((), (), s32[]{:S(2)}) async-start(), calls=%async_computation.4 | async-start | bytes 34603008 | tf_op jit(solution)/shard_map/all_gather | solution.py:202
  9.6 7.6 %collective-permute-start = (f32[32,128]{1,0:T(8,128)S(1)}, f32[32,128]{1,0:T(8,128)S(1)}, u32[]{:S(2)}, u32[]{:S(2)}) collective-permute-start(f32[32,128]{1,0:T(8,128)S(1)} %fusion.33), channel_id=1, source_target_pairs={{0,1},{1,0},{2,3},{3,2},{4,5},{5,4},{6,7},{7,6},{8,9},{9,8},{10,11... | collective-permute-start | bytes 49160 | tf_op jit(solution)/shard_map/ppermute | solution.py:40
  17.1 4.4 %collective-permute-start.2 = (f32[2,32,128]{2,1,0:T(8,128)S(1)}, f32[2,32,128]{2,1,0:T(8,128)S(1)}, u32[]{:S(2)}, u32[]{:S(2)}) collective-permute-start(f32[2,32,128]{2,1,0:T(8,128)S(1)} %reverse_select_fusion.4), channel_id=1, source_target_pairs={{0,4},{2,6},{4,0},{6,2},{1,5},{3,7},{5,1},{7,3},{8,12},{10,14},{12... | collective-permute-start | bytes 98312 | tf_op jit(solution)/shard_map/ppermute | solution.py:40
  20.2 2.8 %collective-permute-start.1 = (f32[2,32,128]{2,1,0:T(8,128)S(1)}, f32[2,32,128]{2,1,0:T(8,128)S(1)}, u32[]{:S(2)}, u32[]{:S(2)}) collective-permute-start(f32[2,32,128]{2,1,0:T(8,128)S(1)} %reverse_select_fusion.4), channel_id=1, source_target_pairs={{0,2},{2,0},{4,6},{6,4},{1,3},{3,1},{5,7},{7,5},{8,10},{10,8},{12,... | collective-permute-start | bytes 98312 | tf_op jit(solution)/shard_map/ppermute | solution.py:40
  20.6 4.0 %collective-permute-start.3 = (f32[2,32,128]{2,1,0:T(8,128)S(1)}, f32[2,32,128]{2,1,0:T(8,128)S(1)}, u32[]{:S(2)}, u32[]{:S(2)}) collective-permute-start(f32[2,32,128]{2,1,0:T(8,128)S(1)} %reverse_select_fusion.4), channel_id=1, source_target_pairs={{0,6},{2,4},{4,2},{6,0},{1,7},{3,5},{5,3},{7,1},{8,14},{10,12},{12... | collective-permute-start | bytes 98312 | tf_op jit(solution)/shard_map/ppermute | solution.py:40
  24.7 65.7 %all-to-all-start = ((bf16[32,448,128]{2,1,0:T(8,128)(2,1)}), bf16[32,448,128]{2,1,0:T(8,128)(2,1)}, u32[]{:S(2)}, u32[]{:S(2)}) async-start(bf16[32,448,128]{2,1,0:T(8,128)(2,1)} %bitcast.88), calls=%async_computation | async-start | bytes 7340032 | tf_op jit(solution)/shard_map/all_to_all | solution.py:206
  32.0 54.2 %collective-permute-start.6 = (f32[4,2,32,128]{3,2,1,0:T(8,128)S(1)}, f32[4,2,32,128]{3,2,1,0:T(8,128)S(1)}, u32[]{:S(2)}, u32[]{:S(2)}) collective-permute-start(f32[4,2,32,128]{3,2,1,0:T(8,128)S(1)} %bitcast.96), channel_id=1, source_target_pairs={{0,24},{8,16},{16,8},{24,0},{1,25},{9,17},{17,9},{25,1},{2,26},{10... | collective-permute-start | bytes 393224 | tf_op jit(solution)/shard_map/ppermute | solution.py:40
  34.7 53.2 %collective-permute-start.5 = (f32[4,2,32,128]{3,2,1,0:T(8,128)S(1)}, f32[4,2,32,128]{3,2,1,0:T(8,128)S(1)}, u32[]{:S(2)}, u32[]{:S(2)}) collective-permute-start(f32[4,2,32,128]{3,2,1,0:T(8,128)S(1)} %bitcast.97), channel_id=1, source_target_pairs={{0,16},{8,24},{16,0},{24,8},{1,17},{9,25},{17,1},{25,9},{2,18},{10... | collective-permute-start | bytes 393224 | tf_op jit(solution)/shard_map/ppermute | solution.py:40
  35.3 54.2 %collective-permute-start.4 = (f32[4,2,32,128]{3,2,1,0:T(8,128)S(1)}, f32[4,2,32,128]{3,2,1,0:T(8,128)S(1)}, u32[]{:S(2)}, u32[]{:S(2)}) collective-permute-start(f32[4,2,32,128]{3,2,1,0:T(8,128)S(1)} %bitcast.98), channel_id=1, source_target_pairs={{0,8},{8,0},{16,24},{24,16},{1,9},{9,1},{17,25},{25,17},{2,10},{10... | collective-permute-start | bytes 393224 | tf_op jit(solution)/shard_map/ppermute | solution.py:40
  93.6 4.4 %collective-permute-start.9 = (f32[32,448]{1,0:T(8,128)S(1)}, f32[32,448]{1,0:T(8,128)S(1)}, u32[]{:S(2)}, u32[]{:S(2)}) collective-permute-start(f32[32,448]{1,0:T(8,128)S(1)} %fusion.22), channel_id=1, source_target_pairs={{0,96},{32,64},{64,32},{96,0},{1,97},{33,65},{65,33},{97,1},{2,98}... | collective-permute-start | bytes 172040 | tf_op jit(solution)/shard_map/ppermute | solution.py:40
  96.1 4.6 %collective-permute-start.8 = (f32[32,448]{1,0:T(8,128)S(1)}, f32[32,448]{1,0:T(8,128)S(1)}, u32[]{:S(2)}, u32[]{:S(2)}) collective-permute-start(f32[32,448]{1,0:T(8,128)S(1)} %fusion.22), channel_id=1, source_target_pairs={{0,64},{32,96},{64,0},{96,32},{1,65},{33,97},{65,1},{97,33},{2,66}... | collective-permute-start | bytes 172040 | tf_op jit(solution)/shard_map/ppermute | solution.py:40
  96.7 4.2 %collective-permute-start.7 = (f32[32,448]{1,0:T(8,128)S(1)}, f32[32,448]{1,0:T(8,128)S(1)}, u32[]{:S(2)}, u32[]{:S(2)}) collective-permute-start(f32[32,448]{1,0:T(8,128)S(1)} %fusion.22), channel_id=1, source_target_pairs={{0,32},{32,0},{64,96},{96,64},{1,33},{33,1},{65,97},{97,65},{2,34}... | collective-permute-start | bytes 172040 | tf_op jit(solution)/shard_map/ppermute | solution.py:40
  104.4 3.6 %collective-permute-start.10 = (f32[16,64,128]{2,1,0:T(8,128)S(1)}, f32[16,64,128]{2,1,0:T(8,128)S(1)}, u32[]{:S(2)}, u32[]{:S(2)}) collective-permute-start(f32[16,64,128]{2,1,0:T(8,128)S(1)} %get-tuple-element.15), channel_id=1, source_target_pairs={{0,1},{1,0},{2,3},{3,2},{4,5},{5,4},{6,7},{7,6},{8,9},{9,8},{10,11... | collective-permute-start | bytes 1572872 | tf_op jit(solution)/shard_map/ppermute | solution.py:40
  108.9 24.2 %all-to-all-start.1 = ((f32[16,64,128]{2,1,0:T(8,128)}), f32[16,64,128]{2,1,0:T(8,128)S(1)}, u32[]{:S(2)}, u32[]{:S(2)}) async-start(f32[16,64,128]{2,1,0:T(8,128)} %add.79), calls=%async_computation.1 | async-start | bytes 1048576 | tf_op jit(solution)/shard_map/all_to_all | solution.py:214
  133.7 2.9 %collective-permute-start.11 = (f32[16,4096]{1,0:T(8,128)S(1)}, f32[16,4096]{1,0:T(8,128)S(1)}, u32[]{:S(2)}, u32[]{:S(2)}) collective-permute-start(f32[16,4096]{1,0:T(8,128)S(1)} %constant_dynamic-slice_fusion), channel_id=1, source_target_pairs={{0,1},{1,0},{2,3},{3,2},{4,5},{5,4},{6,7},{7,6},{8,9},{9,8},{10,11... | collective-permute-start | bytes 786440 | tf_op jit(solution)/shard_map/ppermute | solution.py:40
  137.3 14.6 %all-to-all-start.2 = ((f32[64,8,128]{2,1,0:T(8,128)}), f32[64,8,128]{2,1,0:T(8,128)S(1)}, u32[]{:S(2)}, u32[]{:S(2)}) async-start(f32[64,8,128]{2,1,0:T(8,128)} %bitcast.27), calls=%async_computation.2 | async-start | bytes 524288 | tf_op jit(solution)/shard_map/all_to_all | solution.py:222
  152.7 14.5 %all-to-all-start.3 = ((f32[64,8,128]{2,1,0:T(8,128)}), f32[64,8,128]{2,1,0:T(8,128)S(1)}, u32[]{:S(2)}, u32[]{:S(2)}) async-start(f32[64,8,128]{2,1,0:T(8,128)} %broadcast_in_dim.6), calls=%async_computation.3 | async-start | bytes 524288 | tf_op jit(solution)/shard_map/all_to_all | solution.py:223
  167.2 3.8 %collective-permute-start.12 = (f32[64,8,128]{2,1,0:T(8,128)S(1)}, f32[64,8,128]{2,1,0:T(8,128)S(1)}, u32[]{:S(2)}, u32[]{:S(2)}) collective-permute-start(f32[64,8,128]{2,1,0:T(8,128)S(1)} %all-to-all-done.3), channel_id=1, source_target_pairs={{0,1},{1,0},{2,3},{3,2},{4,5},{5,4},{6,7},{7,6},{8,9},{9,8},{10,11... | collective-permute-start | bytes 786440 | tf_op jit(solution)/shard_map/ppermute | solution.py:40
  171.7 0.8 copy-start.2
  171.7 1.7 copy-start.1
  171.8 2.2 %copy-start = (f32[1024,448]{0,1:T(8,128)S(1)}, f32[1024,448]{0,1:T(8,128)}, u32[]{:S(2)}) copy-start(f32[1024,448]{0,1:T(8,128)} %param.11) | copy-start | bytes 5505028
Sparse Core Ops, SparseCore 0:
  10.3 172.5 all-gather.1

commit v4 on v3

--- a/solution.py
+++ b/solution.py
@@ -73,6 +73,7 @@
     rank = factor.shape[0]
     chips = shards // 2
     step = min(4, chips)
+    extra = rank * rank // tok
 
     def body(c, f_ref, f3_ref, g_ref, keep_ref, send_ref, gram_ref):
         own = c[0] == 0
@@ -82,7 +83,7 @@
             h, m, l = parts3(f_ref[...])
             gram = dot(h, l, 1, 1) + dot(l, h, 1, 1) + dot(m, m, 1, 1)
             gram = gram + (dot(h, m, 1, 1) + dot(m, h, 1, 1)) + dot(h, h, 1, 1)
-            gram_ref[...] = jnp.concatenate([gram, jnp.zeros((rank, tok - rank), jnp.float32)], axis=1)
+            gram_ref[...] = jnp.concatenate([gram[i * extra : (i + 1) * extra] for i in range(rank // extra)], axis=1)
 
         for k in range(step):
             pair = jnp.concatenate([g_ref[2 * k], g_ref[2 * k + 1]], axis=1)
@@ -94,10 +95,10 @@
             keep_ref[k, rank:] = gram_ref[...]
             send_ref[k, rank:] = gram_ref[...]
 
-    block = pl.BlockSpec((step, 2 * rank, tok), lambda n, c: (n, 0, 0))
+    block = pl.BlockSpec((step, rank + extra, tok), lambda n, c: (n, 0, 0))
     return pl.pallas_call(
         body,
-        out_shape=[jax.ShapeDtypeStruct((chips, 2 * rank, tok), jnp.float32)] * 2,
+        out_shape=[jax.ShapeDtypeStruct((chips, rank + extra, tok), jnp.float32)] * 2,
         grid_spec=pltpu.PrefetchScalarGridSpec(
             num_scalar_prefetch=1,
             grid=(chips // step,),
@@ -107,7 +108,7 @@
                 pl.BlockSpec((2 * step, cols, tok), lambda n, c: (n, 0, 0)),
             ],
             out_specs=[block, block],
-            scratch_shapes=[pltpu.VMEM((rank, tok), jnp.float32)],
+            scratch_shapes=[pltpu.VMEM((extra, tok), jnp.float32)],
         ),
         compiler_params=pltpu.CompilerParams(vmem_limit_bytes=VMEM_LIMIT),
         cost_estimate=pl.CostEstimate(flops=6 * rank * cols * shards * tok, bytes_accessed=2 * shards * cols * tok, transcendentals=0),
@@ -201,18 +202,18 @@
     error_t = error_in[0].T
     gathered = lax.all_gather(acts, SHARD, axis=0, tiled=True)
 
-    proj = gather_axis(gather_axis(thrice(basis, acts, 1) * scale, "core"), "y")
+    proj = gather_axis(thrice(basis, acts, 1) * scale, "y")
     grads_t, proj = lax.optimization_barrier((grads.T.reshape(shards, cols, tok), proj))
     got = lax.all_to_all(grads_t, SHARD, 0, 0)
     got_t = got.transpose(1, 0, 2).reshape(cols, shards * tok)
-    proj = gather_axis(proj, "z").reshape(shards, rank, tok).transpose(1, 0, 2).reshape(rank, shards * tok)
+    proj = gather_axis(gather_axis(proj, "z"), "core").transpose(3, 1, 2, 0, 4).reshape(rank, shards * tok)
     base = thrice(basis, error_t, 1)
 
     factor = sum4(thrice(proj, got_t, 1) + base, "outer") / pods
     factor3 = jnp.concatenate(split3(factor), 0)
     keep, send = project(core.astype(jnp.int32).reshape(1), factor, factor3, got)
     inner = lax.all_to_all(keep + twin(send), ("z", "y"), 0, 0, tiled=True).sum(0)
-    gram = inner[rank:, :rank]
+    gram = jnp.concatenate([inner[rank:, i : i + rank] for i in range(0, tok, rank)], 0)
     terms = thrice(inner[:rank] * scale, acts, 0) + thrice(factor, error_t, 0)
     rows = rank // 2
     mine = lax.dynamic_slice_in_dim(terms, core * rows, rows, 0)

time: 214 us -> 210 us (0.981)
  waiting for transfers between devices: 93.1 us -> 83 us
  starting transfers between devices: 41.8 us -> 45.1 us
    all_to_all x1, waiting for transfers between devices: 14.6 us -> 9.95 us  [per_device(): lax.all_to_all(keep + twin(send), ('z', 'y'), 0, 0, tiled=True).sum(0)]
    all_gather x1, waiting for transfers between devices: 3.61 us -> 0.8 us  [per_device(): gathered = lax.all_gather(acts, SHARD, axis=0, tiled=True)]
  transfers between devices with their start and end apart: 18 -> 18, of which waited for: 16 -> 12; matrix products, arithmetic and copies ran while one was open for 14% -> 15% of each run, Pallas kernels for 4% -> 4%
where the time goes in v4:
time: 210 us
  waiting for transfers between devices  83 us (40%)
  starting transfers between devices  45.1 us (21%)
  Pallas kernels  32.7 us (16%)
  between operations  14.4 us (7%)
  local copies, waits for them, and re-layouts  11.8 us (6%)
  other arithmetic  11.5 us (5%)
  matrix products  11.1 us (5%)
    ppermute x13, waiting for transfers between devices, swap(): lax.ppermute(x, axis, [(i, i ^ k) for i in range(lax.axis_size(axis))])  59.8 us
    pallas_call x1, Pallas kernels, finish_error(): pl.pallas_call(body, out_shape=jax.ShapeDtypeStruct(error_t.shape, jnp.bf...  23.7 us
    ppermute x13, starting transfers between devices, swap(): lax.ppermute(x, axis, [(i, i ^ k) for i in range(lax.axis_size(axis))])  18.5 us
    dot_general x5, matrix products, dot(): lax.dot_general(a, b, (((ca,), (cb,)), ((), ())), preferred_element_type=...  10.1 us
    all_to_all x1, waiting for transfers between devices, per_device(): lax.all_to_all(keep + twin(send), ('z', 'y'), 0, 0, tiled=True).sum(0)  9.95 us
    all_to_all x1, starting transfers between devices, per_device(): got = lax.all_to_all(grads_t, SHARD, 0, 0)  9.23 us
    all_to_all x1, starting transfers between devices, per_device(): lax.all_to_all(keep + twin(send), ('z', 'y'), 0, 0, tiled=True).sum(0)  6.64 us
    transpose x1, local copies, waits for them, and re-layouts, per_device(): grads.T.reshape(shards, cols, tok)  6.04 us
  transfers between devices with their start and end apart: 18, of which 12 were waited for; matrix products, arithmetic and copies ran while one was open for 15% of the time, Pallas kernels for 4%

profile of v4, /device:TPU:1, one launch (start us, length us, event | category | flops | bytes accessed | tf_op | source)
XLA Modules:
  0.0 209.5 jit_solution(14090555811681923928)
XLA Ops:
  7.2 0.7 all-gather.2.cloned.1.call-update
  7.9 1.2 reduce-precision_convert_fusion.5
  9.1 0.5 fusion.16
  9.6 3.8 %collective-permute-start.1 = (f32[32,128]{1,0:T(8,128)S(1)}, f32[32,128]{1,0:T(8,128)S(1)}, u32[]{:S(2)}, u32[]{:S(2)}) collective-permute-start(f32[32,128]{1,0:T(8,128)S(1)} %fusion.33), channel_id=1, source_target_pairs={{0,4},{2,6},{4,0},{6,2},{1,5},{3,7},{5,1},{7,3},{8,12},{10,14},{12... | collective-permute-start | bytes 49160 | tf_op jit(solution)/shard_map/ppermute | solution.py:40
  14.2 6.0 %copy.39 = bf16[14336,128]{1,0:T(8,128)(2,1)} copy(bf16[14336,128]{0,1:T(8,128)(2,1)} %bitcast.80) | data formatting | bytes 7340032 | tf_op jit(solution)/shard_map/transpose | solution.py:206
  20.3 9.2 %all-to-all-start = ((bf16[32,448,128]{2,1,0:T(8,128)(2,1)}), bf16[32,448,128]{2,1,0:T(8,128)(2,1)}, u32[]{:S(2)}, u32[]{:S(2)}) async-start(bf16[32,448,128]{2,1,0:T(8,128)(2,1)} %bitcast.79), calls=%async_computation | async-start | bytes 7340032 | tf_op jit(solution)/shard_map/all_to_all | solution.py:207
  29.5 2.7 %collective-permute-start.5 = (f32[4,32,128]{2,1,0:T(8,128)S(1)}, f32[4,32,128]{2,1,0:T(8,128)S(1)}, u32[]{:S(2)}, u32[]{:S(2)}) collective-permute-start(f32[4,32,128]{2,1,0:T(8,128)S(1)} %bitcast.91), channel_id=1, source_target_pairs={{0,24},{8,16},{16,8},{24,0},{1,25},{9,17},{17,9},{25,1},{2,26},{10... | collective-permute-start | bytes 196616 | tf_op jit(solution)/shard_map/ppermute | solution.py:40
  32.3 0.5 collective-permute-start.4
  32.9 29.8 %collective-permute-done.5 = f32[4,32,128]{2,1,0:T(8,128)S(1)} collective-permute-done((f32[4,32,128]{2,1,0:T(8,128)S(1)}, f32[4,32,128]{2,1,0:T(8,128)S(1)}, u32[]{:S(2)}, u32[]{:S(2)}) %collective-permute-start.5) | collective-permute-done | bytes 65568 | tf_op jit(solution)/shard_map/ppermute | solution.py:40
  62.7 20.8 %collective-permute-done.4 = f32[4,32,128]{2,1,0:T(8,128)S(1)} collective-permute-done((f32[4,32,128]{2,1,0:T(8,128)S(1)}, f32[4,32,128]{2,1,0:T(8,128)S(1)}, u32[]{:S(2)}, u32[]{:S(2)}) %collective-permute-start.4) | collective-permute-done | bytes 65568 | tf_op jit(solution)/shard_map/ppermute | solution.py:40
  83.5 3.1 %collective-permute-done.3 = f32[4,32,128]{2,1,0:T(8,128)S(1)} collective-permute-done((f32[4,32,128]{2,1,0:T(8,128)S(1)}, f32[4,32,128]{2,1,0:T(8,128)S(1)}, u32[]{:S(2)}, u32[]{:S(2)}) %collective-permute-start.3) | collective-permute-done | bytes 65568 | tf_op jit(solution)/shard_map/ppermute | solution.py:40
  86.9 0.6 collective-permute-start.6
  87.5 3.2 %fusion.5 = f32[96,448]{1,0:T(8,128)S(1)} fusion(bf16[1,4096,448]{1,2,0:T(8,128)(2,1)} %param.10, bf16[32,4096]{1,0:T(8,128)(2,1)S(1)} %get-tuple-element.27, bf16[32,4096]{1,0:T(8,128)(2,1)S(1)} %get-tuple-element.28, bf16[32,4096]{1,0:T(8,128)(2,1)S(1)} %get-tuple-element.26), kind=kOutput, calls=%fused_computation.5 | convolution fusion | flops 354680832 | bytes 4628480 | tf_op jit(solution)/shard_map/dot_general | solution.py:30
  90.7 0.5 pad_maximum_fusion.1
  91.2 1.4 reverse.3
  92.6 0.5 select_bitcast_fusion
  93.7 3.2 %fusion = f32[96,448]{1,0:T(8,128)S(1)} fusion(bf16[32,4096]{1,0:T(8,128)(2,1)S(1)} %get-tuple-element.24, bf16[32,4096]{1,0:T(8,128)(2,1)S(1)} %get-tuple-element.25, bf16[32,4096]{1,0:T(8,128)(2,1)S(1)} %get-tuple-element.23, bf16[32,448,128]{2,1,0:T(8,128)(2,1)} %all-to-all-done.g_ref.got_ref), kind=kOutput, calls=%fused_computation | convolution fusion | flops 354680832 | bytes 4628480 | tf_op jit(solution)/shard_map/dot_general | solution.py:30
  97.0 2.5 %collective-permute-start.9 = (f32[32,448]{1,0:T(8,128)S(1)}, f32[32,448]{1,0:T(8,128)S(1)}, u32[]{:S(2)}, u32[]{:S(2)}) collective-permute-start(f32[32,448]{1,0:T(8,128)S(1)} %fusion.22), channel_id=1, source_target_pairs={{0,96},{32,64},{64,32},{96,0},{1,97},{33,65},{65,33},{97,1},{2,98}... | collective-permute-start | bytes 172040 | tf_op jit(solution)/shard_map/ppermute | solution.py:40
  99.5 0.6 collective-permute-start.8
  100.3 1.7 collective-permute-done.9
  102.1 2.1 collective-permute-done.8
  104.2 3.6 %shard_map.110 = (f32[16,40,128]{2,1,0:T(8,128)S(1)}, f32[16,40,128]{2,1,0:T(8,128)S(1)}) custom-call(s32[1]{0:T(128)} %bitcast.c, f32[32,448]{1,0:T(8,128)S(1)} %get-tuple-element.20.f_ref, bf16[96,448]{1,0:T(8,128)(2,1)S(1)} %pad_maximum_fusion.6.f3_ref, bf16[32,448,128]{2,1,0:T(8,128)(2,1)} %all-to-all-done.g_ref.got_ref), custom_call_target="tpu_custom_call" | custom-call | flops 352321536 | bytes 3670016 | tf_op jit(solution)/shard_map/pallas_call | solution.py:99
  107.8 2.3 %collective-permute-start.10 = (f32[16,40,128]{2,1,0:T(8,128)S(1)}, f32[16,40,128]{2,1,0:T(8,128)S(1)}, u32[]{:S(2)}, u32[]{:S(2)}) collective-permute-start(f32[16,40,128]{2,1,0:T(8,128)S(1)} %get-tuple-element.15), channel_id=1, source_target_pairs={{0,1},{1,0},{2,3},{3,2},{4,5},{5,4},{6,7},{7,6},{8,9},{9,8},{10,11... | collective-permute-start | bytes 983048 | tf_op jit(solution)/shard_map/ppermute | solution.py:40
  110.2 1.3 collective-permute-done.10
  111.4 0.8 add.79
  112.2 6.6 %all-to-all-start.1 = ((f32[16,40,128]{2,1,0:T(8,128)}), f32[16,40,128]{2,1,0:T(8,128)S(1)}, u32[]{:S(2)}, u32[]{:S(2)}) async-start(f32[16,40,128]{2,1,0:T(8,128)} %add.79), calls=%async_computation.1 | async-start | bytes 655360 | tf_op jit(solution)/shard_map/all_to_all | solution.py:215
  118.8 2.8 %fusion.3 = f32[96,4096]{1,0:T(8,128)S(1)} fusion(bf16[1,4096,448]{1,2,0:T(8,128)(2,1)} %param.10, bf16[32,448]{1,0:T(8,128)(2,1)S(1)} %get-tuple-element.33, bf16[32,448]{1,0:T(8,128)(2,1)S(1)} %get-tuple-element.32, bf16[32,448]{1,0:T(8,128)(2,1)S(1)} %get-tuple-element.19), kind=kOutput, calls=%fused_computation.3 | convolution fusion | flops 352579584 | bytes 5328896 | tf_op jit(solution)/shard_map/dot_general | solution.py:30
  121.6 10.0 %all-to-all-done.1 = f32[16,40,128]{2,1,0:T(8,128)S(1)} async-done(((f32[16,40,128]{2,1,0:T(8,128)}), f32[16,40,128]{2,1,0:T(8,128)S(1)}, u32[]{:S(2)}, u32[]{:S(2)}) %all-to-all-start.1) | async-done | bytes 327712 | tf_op jit(solution)/shard_map/all_to_all | solution.py:215
  132.3 1.9 collective-permute-start.11
  134.7 0.6 collective-permute-done.11
  135.3 0.7 dynamic-slice_add_fusion
  136.0 4.8 %all-to-all-start.2 = ((f32[64,8,128]{2,1,0:T(8,128)}), f32[64,8,128]{2,1,0:T(8,128)S(1)}, u32[]{:S(2)}, u32[]{:S(2)}) async-start(f32[64,8,128]{2,1,0:T(8,128)} %bitcast.27), calls=%async_computation.2 | async-start | bytes 524288 | tf_op jit(solution)/shard_map/all_to_all | solution.py:223
  140.9 2.9 %cholesky.17 = f32[32,32]{1,0:T(8,128)S(1)} custom-call(f32[32,32]{1,0:T(8,128)S(1)} %fusion.36), custom_call_target="Cholesky" | custom-call | tf_op jit(solution)/shard_map/jit(cholesky)/cholesky | solution.py:229
  143.8 0.6 compare_reduce_fusion
  144.5 5.7 %all-to-all-done.2 = f32[64,8,128]{2,1,0:T(8,128)S(1)} async-done(((f32[64,8,128]{2,1,0:T(8,128)}), f32[64,8,128]{2,1,0:T(8,128)S(1)}, u32[]{:S(2)}, u32[]{:S(2)}) %all-to-all-start.2) | async-done | bytes 262176 | tf_op jit(solution)/shard_map/all_to_all | solution.py:223
  150.3 0.7 broadcast_in_dim.6
  151.0 5.8 %all-to-all-start.3 = ((f32[64,8,128]{2,1,0:T(8,128)}), f32[64,8,128]{2,1,0:T(8,128)S(1)}, u32[]{:S(2)}, u32[]{:S(2)}) async-start(f32[64,8,128]{2,1,0:T(8,128)} %broadcast_in_dim.6), calls=%async_computation.3 | async-start | bytes 524288 | tf_op jit(solution)/shard_map/all_to_all | solution.py:224
  156.8 0.7 fusion.31
  157.5 2.4 %custom-call.7 = f32[1,32,32]{1,2,0:T(8,128)S(1)} custom-call(f32[1,32,32]{2,1,0:T(8,128)S(1)} %fusion.31), custom_call_target="InvertDiagBlocksLowerTriangular" | custom-call | tf_op jit(solution)/shard_map/jit(_solve_triangular)/triangular_solve | solution.py:230
  160.2 6.0 %all-to-all-done.3 = f32[64,8,128]{2,1,0:T(8,128)S(1)} async-done(((f32[64,8,128]{2,1,0:T(8,128)}), f32[64,8,128]{2,1,0:T(8,128)S(1)}, u32[]{:S(2)}, u32[]{:S(2)}) %all-to-all-start.3) | async-done | bytes 262176 | tf_op jit(solution)/shard_map/all_to_all | solution.py:224
  166.2 2.4 %collective-permute-start.12 = (f32[64,8,128]{2,1,0:T(8,128)S(1)}, f32[64,8,128]{2,1,0:T(8,128)S(1)}, u32[]{:S(2)}, u32[]{:S(2)}) collective-permute-start(f32[64,8,128]{2,1,0:T(8,128)S(1)} %all-to-all-done.3), channel_id=1, source_target_pairs={{0,1},{1,0},{2,3},{3,2},{4,5},{5,4},{6,7},{7,6},{8,9},{9,8},{10,11... | collective-permute-start | bytes 786440 | tf_op jit(solution)/shard_map/ppermute | solution.py:40
  169.9 0.6 constant_dynamic-update-slice_fusion.2
  170.7 0.5 copy-done.2
  171.3 1.0 copy-done.1
  172.3 0.6 copy-done
  172.8 5.3 %shard_map.112 = (f32[448,1024]{1,0:T(8,128)}, f32[448,1024]{1,0:T(8,128)}, f32[448,1024]{1,0:T(8,128)}) custom-call(s32[1]{0:T(128)} %bitcast.35.p, bf16[448,192]{1,0:T(8,128)(2,1)S(1)} %bitcast.77, bf16[192,4096]{1,0:T(8,128)(2,1)S(1)} %fusion.24.basis_ref, f32[448,1024]{1,0:T(8,128)S(1)} %bitcast.75, f32[448,1024]{1,0:T(8,128)S(1)} %bitcast.76, ...), custom_call_target="tpu_custom_call" | custom-call | flops 176160768 | bytes 11010048 | tf_op jit(solution)/shard_map/pallas_call | solution.py:172
  178.2 0.8 all-gather.2.cloned.1.call-done.acts_ref
  179.0 23.7 %shard_map.111 = bf16[448,4096]{1,0:T(8,128)(2,1)} custom-call(bf16[32,448,128]{2,1,0:T(8,128)(2,1)} %all-to-all-done.g_ref.got_ref, bf16[4096,4096]{1,0:T(8,128)(2,1)} %all-gather.2.cloned.1.call-done.acts_ref, bf16[448,4096]{1,0:T(8,128)(2,1)} %bitcast.81, bf16[448,192]{1,0:T(8,128)(2,1)S(1)} %bitcast.78, bf16[192,4096]{1,0:T(8,128)(2,1)S(1)} %fusion.24.basis_ref), custom_call_target="tpu_custom_call" | custom-call | flops 15737028608 | bytes 44564480 | tf_op jit(solution)/shard_map/pallas_call | solution.py:136
  (61 shorter events, 5.2 us)
Async XLA Ops:
  7.2 1.9 copy-start.3
  7.2 171.8 %all-gather.2.cloned.1.call-start = ((), (), s32[]{:S(2)}) async-start(), calls=%async_computation.4 | async-start | bytes 34603008 | tf_op jit(solution)/shard_map/all_gather | solution.py:203
  9.6 10.7 %collective-permute-start.1 = (f32[32,128]{1,0:T(8,128)S(1)}, f32[32,128]{1,0:T(8,128)S(1)}, u32[]{:S(2)}, u32[]{:S(2)}) collective-permute-start(f32[32,128]{1,0:T(8,128)S(1)} %fusion.33), channel_id=1, source_target_pairs={{0,4},{2,6},{4,0},{6,2},{1,5},{3,7},{5,1},{7,3},{8,12},{10,14},{12... | collective-permute-start | bytes 49160 | tf_op jit(solution)/shard_map/ppermute | solution.py:40
  13.4 6.8 %collective-permute-start = (f32[32,128]{1,0:T(8,128)S(1)}, f32[32,128]{1,0:T(8,128)S(1)}, u32[]{:S(2)}, u32[]{:S(2)}) collective-permute-start(f32[32,128]{1,0:T(8,128)S(1)} %fusion.33), channel_id=1, source_target_pairs={{0,2},{2,0},{4,6},{6,4},{1,3},{3,1},{5,7},{7,5},{8,10},{10,8},{12,... | collective-permute-start | bytes 49160 | tf_op jit(solution)/shard_map/ppermute | solution.py:40
  13.8 6.4 %collective-permute-start.2 = (f32[32,128]{1,0:T(8,128)S(1)}, f32[32,128]{1,0:T(8,128)S(1)}, u32[]{:S(2)}, u32[]{:S(2)}) collective-permute-start(f32[32,128]{1,0:T(8,128)S(1)} %fusion.33), channel_id=1, source_target_pairs={{0,6},{2,4},{4,2},{6,0},{1,7},{3,5},{5,3},{7,1},{8,14},{10,12},{12... | collective-permute-start | bytes 49160 | tf_op jit(solution)/shard_map/ppermute | solution.py:40
  20.3 73.4 %all-to-all-start = ((bf16[32,448,128]{2,1,0:T(8,128)(2,1)}), bf16[32,448,128]{2,1,0:T(8,128)(2,1)}, u32[]{:S(2)}, u32[]{:S(2)}) async-start(bf16[32,448,128]{2,1,0:T(8,128)(2,1)} %bitcast.79), calls=%async_computation | async-start | bytes 7340032 | tf_op jit(solution)/shard_map/all_to_all | solution.py:207
  29.5 33.2 %collective-permute-start.5 = (f32[4,32,128]{2,1,0:T(8,128)S(1)}, f32[4,32,128]{2,1,0:T(8,128)S(1)}, u32[]{:S(2)}, u32[]{:S(2)}) collective-permute-start(f32[4,32,128]{2,1,0:T(8,128)S(1)} %bitcast.91), channel_id=1, source_target_pairs={{0,24},{8,16},{16,8},{24,0},{1,25},{9,17},{17,9},{25,1},{2,26},{10... | collective-permute-start | bytes 196616 | tf_op jit(solution)/shard_map/ppermute | solution.py:40
  32.3 51.3 %collective-permute-start.4 = (f32[4,32,128]{2,1,0:T(8,128)S(1)}, f32[4,32,128]{2,1,0:T(8,128)S(1)}, u32[]{:S(2)}, u32[]{:S(2)}) collective-permute-start(f32[4,32,128]{2,1,0:T(8,128)S(1)} %bitcast.92), channel_id=1, source_target_pairs={{0,16},{8,24},{16,0},{24,8},{1,17},{9,25},{17,1},{25,9},{2,18},{10... | collective-permute-start | bytes 196616 | tf_op jit(solution)/shard_map/ppermute | solution.py:40
  32.8 53.8 %collective-permute-start.3 = (f32[4,32,128]{2,1,0:T(8,128)S(1)}, f32[4,32,128]{2,1,0:T(8,128)S(1)}, u32[]{:S(2)}, u32[]{:S(2)}) collective-permute-start(f32[4,32,128]{2,1,0:T(8,128)S(1)} %bitcast.93), channel_id=1, source_target_pairs={{0,8},{8,0},{16,24},{24,16},{1,9},{9,1},{17,25},{25,17},{2,10},{10... | collective-permute-start | bytes 196616 | tf_op jit(solution)/shard_map/ppermute | solution.py:40
  86.9 3.8 %collective-permute-start.6 = (f32[4,4,32,128]{3,1,0,2:T(4,128)S(1)}, f32[4,4,32,128]{3,1,0,2:T(4,128)S(1)}, u32[]{:S(2)}, u32[]{:S(2)}) collective-permute-start(f32[4,4,32,128]{3,1,0,2:T(4,128)S(1)} %bitcast.82), channel_id=1, source_target_pairs={{0,1},{1,0},{2,3},{3,2},{4,5},{5,4},{6,7},{7,6},{8,9},{9,8},{10,11... | collective-permute-start | bytes 786440 | tf_op jit(solution)/shard_map/ppermute | solution.py:40
  97.0 5.1 %collective-permute-start.9 = (f32[32,448]{1,0:T(8,128)S(1)}, f32[32,448]{1,0:T(8,128)S(1)}, u32[]{:S(2)}, u32[]{:S(2)}) collective-permute-start(f32[32,448]{1,0:T(8,128)S(1)} %fusion.22), channel_id=1, source_target_pairs={{0,96},{32,64},{64,32},{96,0},{1,97},{33,65},{65,33},{97,1},{2,98}... | collective-permute-start | bytes 172040 | tf_op jit(solution)/shard_map/ppermute | solution.py:40
  99.5 4.7 %collective-permute-start.8 = (f32[32,448]{1,0:T(8,128)S(1)}, f32[32,448]{1,0:T(8,128)S(1)}, u32[]{:S(2)}, u32[]{:S(2)}) collective-permute-start(f32[32,448]{1,0:T(8,128)S(1)} %fusion.22), channel_id=1, source_target_pairs={{0,64},{32,96},{64,0},{96,32},{1,65},{33,97},{65,1},{97,33},{2,66}... | collective-permute-start | bytes 172040 | tf_op jit(solution)/shard_map/ppermute | solution.py:40
  100.0 4.1 %collective-permute-start.7 = (f32[32,448]{1,0:T(8,128)S(1)}, f32[32,448]{1,0:T(8,128)S(1)}, u32[]{:S(2)}, u32[]{:S(2)}) collective-permute-start(f32[32,448]{1,0:T(8,128)S(1)} %fusion.22), channel_id=1, source_target_pairs={{0,32},{32,0},{64,96},{96,64},{1,33},{33,1},{65,97},{97,65},{2,34}... | collective-permute-start | bytes 172040 | tf_op jit(solution)/shard_map/ppermute | solution.py:40
  107.8 3.6 %collective-permute-start.10 = (f32[16,40,128]{2,1,0:T(8,128)S(1)}, f32[16,40,128]{2,1,0:T(8,128)S(1)}, u32[]{:S(2)}, u32[]{:S(2)}) collective-permute-start(f32[16,40,128]{2,1,0:T(8,128)S(1)} %get-tuple-element.15), channel_id=1, source_target_pairs={{0,1},{1,0},{2,3},{3,2},{4,5},{5,4},{6,7},{7,6},{8,9},{9,8},{10,11... | collective-permute-start | bytes 983048 | tf_op jit(solution)/shard_map/ppermute | solution.py:40
  112.2 19.4 %all-to-all-start.1 = ((f32[16,40,128]{2,1,0:T(8,128)}), f32[16,40,128]{2,1,0:T(8,128)S(1)}, u32[]{:S(2)}, u32[]{:S(2)}) async-start(f32[16,40,128]{2,1,0:T(8,128)} %add.79), calls=%async_computation.1 | async-start | bytes 655360 | tf_op jit(solution)/shard_map/all_to_all | solution.py:215
  132.3 3.0 %collective-permute-start.11 = (f32[16,4096]{1,0:T(8,128)S(1)}, f32[16,4096]{1,0:T(8,128)S(1)}, u32[]{:S(2)}, u32[]{:S(2)}) collective-permute-start(f32[16,4096]{1,0:T(8,128)S(1)} %constant_dynamic-slice_fusion), channel_id=1, source_target_pairs={{0,1},{1,0},{2,3},{3,2},{4,5},{5,4},{6,7},{7,6},{8,9},{9,8},{10,11... | collective-permute-start | bytes 786440 | tf_op jit(solution)/shard_map/ppermute | solution.py:40
  136.0 14.2 %all-to-all-start.2 = ((f32[64,8,128]{2,1,0:T(8,128)}), f32[64,8,128]{2,1,0:T(8,128)S(1)}, u32[]{:S(2)}, u32[]{:S(2)}) async-start(f32[64,8,128]{2,1,0:T(8,128)} %bitcast.27), calls=%async_computation.2 | async-start | bytes 524288 | tf_op jit(solution)/shard_map/all_to_all | solution.py:223
  151.0 15.2 %all-to-all-start.3 = ((f32[64,8,128]{2,1,0:T(8,128)}), f32[64,8,128]{2,1,0:T(8,128)S(1)}, u32[]{:S(2)}, u32[]{:S(2)}) async-start(f32[64,8,128]{2,1,0:T(8,128)} %broadcast_in_dim.6), calls=%async_computation.3 | async-start | bytes 524288 | tf_op jit(solution)/shard_map/all_to_all | solution.py:224
  166.2 3.6 %collective-permute-start.12 = (f32[64,8,128]{2,1,0:T(8,128)S(1)}, f32[64,8,128]{2,1,0:T(8,128)S(1)}, u32[]{:S(2)}, u32[]{:S(2)}) collective-permute-start(f32[64,8,128]{2,1,0:T(8,128)S(1)} %all-to-all-done.3), channel_id=1, source_target_pairs={{0,1},{1,0},{2,3},{3,2},{4,5},{5,4},{6,7},{7,6},{8,9},{9,8},{10,11... | collective-permute-start | bytes 786440 | tf_op jit(solution)/shard_map/ppermute | solution.py:40
  170.5 0.8 copy-start.2
  170.5 1.8 copy-start.1
  170.5 2.3 %copy-start = (f32[1024,448]{0,1:T(8,128)S(1)}, f32[1024,448]{0,1:T(8,128)}, u32[]{:S(2)}) copy-start(f32[1024,448]{0,1:T(8,128)} %param.11) | copy-start | bytes 5505028
Sparse Core Ops, SparseCore 0:
  10.3 168.6 all-gather.1

commit v5 on v4

--- a/solution.py
+++ b/solution.py
@@ -47,6 +47,13 @@
 def sum4(x, axis):
     a, b, c = swap(x, axis, 1), swap(x, axis, 2), swap(x, axis, 3)
     return (x + a) + (b + c)
+
+
+def scatter4(x, axis):
+    i = lax.axis_index(axis)
+    own, a, b, c = (lax.dynamic_index_in_dim(x, i ^ k, 0, keepdims=False) for k in range(4))
+    a, b, c = (swap(v, axis, k) for v, k in ((a, 1), (b, 2), (c, 3)))
+    return (own + a) + (b + c)
 
 
 def gather_axis(x, axis):
@@ -119,33 +126,71 @@
     shards, cols, tok = got.shape
     tokens, width = gathered.shape
     block = min(1024, width)
+    steps = width // block
     depth6 = ortho6.shape[1]
-
-    def body(got_ref, acts_ref, error_ref, ortho_ref, basis_ref, out_ref, columns):
-        @pl.when(pl.program_id(0) == 0)
+    parts = 4
+    rows = tokens // parts
+
+    def body(got_ref, acts_ref, error_ref, ortho_ref, basis_ref, out_ref, columns, held, gradient, sems):
+        n = pl.program_id(0)
+        slot = lax.rem(n, 2)
+
+        def copy(m, s, k):
+            piece = pl.ds(k * rows, rows)
+            place = pl.ds(pl.multiple_of(m * block, block), block)
+            return pltpu.make_async_copy(acts_ref.at[piece, place], held.at[s, piece], sems.at[s, k])
+
+        @pl.when(n == 0)
         def _():
+            for k in range(parts):
+                copy(0, 0, k).start()
+            if steps > 1:
+                for k in range(parts):
+                    copy(1, 1, k).start()
             for s in range(shards):
                 columns[:, s * tok : (s + 1) * tok] = got_ref[s]
-
-        gradient = jnp.dot(columns[...], acts_ref[...], preferred_element_type=jnp.float32)
+            total = None
+            for k in range(parts):
+                copy(0, 0, k).wait()
+                piece = slice(k * rows, (k + 1) * rows)
+                d = jnp.dot(columns[:, piece], held[0, piece], preferred_element_type=jnp.float32)
+                total = d if total is None else total + d
+            gradient[...] = total
+
+        @pl.when(n > 0)
+        def _():
+            for k in range(parts):
+                copy(n, slot, k).wait()
+            gradient[...] = jnp.dot(columns[...], held[slot], preferred_element_type=jnp.float32)
+
+        @pl.when(n + 2 < steps)
+        def _():
+            for k in range(parts):
+                copy(n + 2, slot, k).start()
+
         approx = jnp.dot(ortho_ref[...], basis_ref[...], preferred_element_type=jnp.float32)
-        matrix = gradient * scale + error_ref[...].astype(jnp.float32)
+        matrix = gradient[...] * scale + error_ref[...].astype(jnp.float32)
         out_ref[...] = (matrix - approx).astype(jnp.bfloat16)
 
     wide = pl.BlockSpec((cols, block), lambda n: (0, n))
     return pl.pallas_call(
         body,
         out_shape=jax.ShapeDtypeStruct(error_t.shape, jnp.bfloat16),
-        grid=(width // block,),
+        grid=(steps,),
         in_specs=[
             pl.BlockSpec((shards, cols, tok), lambda n: (0, 0, 0)),
-            pl.BlockSpec((tokens, block), lambda n: (0, n)),
+            pl.BlockSpec(memory_space=pl.ANY),
             wide,
             pl.BlockSpec((cols, depth6), lambda n: (0, 0)),
             pl.BlockSpec((depth6, block), lambda n: (0, n)),
         ],
         out_specs=wide,
-        scratch_shapes=[pltpu.VMEM((cols, tokens), got.dtype)],
+        scratch_shapes=[
+            pltpu.VMEM((cols, tokens), got.dtype),
+            pltpu.VMEM((2, tokens, block), gathered.dtype),
+            pltpu.VMEM((cols, block), jnp.float32),
+            pltpu.SemaphoreType.DMA((2, parts)),
+        ],
         compiler_params=pltpu.CompilerParams(vmem_limit_bytes=VMEM_LIMIT),
         cost_estimate=pl.CostEstimate(
             flops=2 * cols * width * (tokens + depth6), bytes_accessed=2 * tokens * (width + cols) + 4 * cols * width, transcendentals=0
@@ -163,8 +208,9 @@
         update = jnp.dot(ortho_ref[...], basis_ref[...], preferred_element_type=jnp.float32)
         one = beta_one * one_ref[...] + (1.0 - beta_one) * update
         two = beta_two * two_ref[...] + (1.0 - beta_two) * update * update
-        step = one / first_fix / (jnp.sqrt(two / second_fix) + adam_epsilon)
-        w_out[...] = w_ref[...] * (1.0 - learn_rate * decay_rate) - learn_rate * step
+        root = jnp.sqrt(two * (1.0 / second_fix)) + adam_epsilon
+        step = one * (learn_rate / first_fix) / root
+        w_out[...] = w_ref[...] * (1.0 - learn_rate * decay_rate) - step
         one_out[...] = one
         two_out[...] = two
 
@@ -206,8 +252,11 @@
     grads_t, proj = lax.optimization_barrier((grads.T.reshape(shards, cols, tok), proj))
     got = lax.all_to_all(grads_t, SHARD, 0, 0)
     got_t = got.transpose(1, 0, 2).reshape(cols, shards * tok)
-    proj = gather_axis(gather_axis(proj, "z"), "core").transpose(3, 1, 2, 0, 4).reshape(rank, shards * tok)
     base = thrice(basis, error_t, 1)
+    proj, base = lax.optimization_barrier((gather_axis(proj, "z"), base))
+    other = twin(proj)
+    proj = jnp.stack([jnp.where(core == 0, proj, other), jnp.where(core == 0, other, proj)], 2)
+    proj = proj.transpose(3, 0, 1, 2, 4).reshape(rank, shards * tok)
 
     factor = sum4(thrice(proj, got_t, 1) + base, "outer") / pods
     factor3 = jnp.concatenate(split3(factor), 0)
@@ -215,16 +264,19 @@
     inner = lax.all_to_all(keep + twin(send), ("z", "y"), 0, 0, tiled=True).sum(0)
     gram = jnp.concatenate([inner[rank:, i : i + rank] for i in range(0, tok, rank)], 0)
     terms = thrice(inner[:rank] * scale, acts, 0) + thrice(factor, error_t, 0)
-    rows = rank // 2
-    mine = lax.dynamic_slice_in_dim(terms, core * rows, rows, 0)
-    other = lax.dynamic_slice_in_dim(terms, (1 - core) * rows, rows, 0)
-    tiles = (rows // 8, 8, width // 128, 128)
-    mine = (mine + twin(other)).reshape(tiles).transpose(0, 2, 1, 3).reshape(chips, -1, 128)
-    piece = lax.all_to_all(mine, CHIPS, 0, 0, tiled=True).sum(0) / pods
-    mine = lax.all_to_all(jnp.broadcast_to(piece[None], mine.shape), CHIPS, 0, 0, tiled=True)
+
+    half = width // 2
+    mine = lax.dynamic_slice_in_dim(terms, core * half, half, 1)
+    other = lax.dynamic_slice_in_dim(terms, (1 - core) * half, half, 1)
+    mine = scatter4((mine + twin(other)).reshape(pods, rank // pods, half), "outer")
+    mine, gram = lax.optimization_barrier((mine, gram))
+    mine = mine.reshape(rank // pods, chips // pods, -1).transpose(1, 0, 2)
+    piece = lax.all_to_all(mine, ("z", "y"), 0, 0, tiled=True).sum(0) / pods
+    mine = lax.all_to_all(jnp.broadcast_to(piece[None], (chips,) + piece.shape), CHIPS, 0, 0, tiled=True)
+    mine = mine.reshape((pods, chips // pods) + piece.shape)
     other = twin(mine)
-    terms = jnp.concatenate([jnp.where(core == 0, mine, other), jnp.where(core == 0, other, mine)], 0)
-    terms = terms.reshape(rank // 8, width // 128, 8, 128).transpose(0, 2, 1, 3).reshape(rank, width)
+    terms = jnp.concatenate([jnp.where(core == 0, mine, other), jnp.where(core == 0, other, mine)], 1)
+    terms = terms.transpose(0, 2, 1, 3).reshape(rank, width)
 
     lower = jnp.linalg.cholesky(gram)
     inverse = jax.scipy.linalg.solve_triangular(lower, jnp.eye(rank, dtype=jnp.float32), lower=True)

time: 210 us -> 208 us (level)
  starting transfers between devices: 45.1 us -> 47.5 us
    ppermute x13 -> x16, starting transfers between devices: 18.5 us -> 22.7 us  [swap(): lax.ppermute(x, axis, [(i, i ^ k) for i in range(lax.axis_size(axis))])]
    all_to_all x2, waiting for transfers between devices: 11.7 us -> 9.25 us  [the longest x1 5.8 us: per_device(): lax.all_to_all(jnp.broadcast_to(piece[None], (chips,) + piece.shape), CHI...]
    ppermute x13 -> x16, waiting for transfers between devices: 59.8 us -> 61.2 us  [swap(): lax.ppermute(x, axis, [(i, i ^ k) for i in range(lax.axis_size(axis))])]
  transfers between devices with their start and end apart: 18 -> 21, of which waited for: 12 -> 15; matrix products, arithmetic and copies ran while one was open for 15% -> 15% of each run, Pallas kernels for 4% -> 4%
where the time goes in v5:
time: 208 us
  waiting for transfers between devices  81.2 us (39%)
  starting transfers between devices  47.5 us (23%)
  Pallas kernels  32.3 us (16%)
  between operations  14.4 us (7%)
  matrix products  11.1 us (5%)
  other arithmetic  10.8 us (5%)
  local copies, waits for them, and re-layouts  10.3 us (5%)
    ppermute x16, waiting for transfers between devices, swap(): lax.ppermute(x, axis, [(i, i ^ k) for i in range(lax.axis_size(axis))])  61.2 us
    pallas_call x1, Pallas kernels, finish_error(): pl.pallas_call(body, out_shape=jax.ShapeDtypeStruct(error_t.shape, jnp.bf...  23.3 us
    ppermute x16, starting transfers between devices, swap(): lax.ppermute(x, axis, [(i, i ^ k) for i in range(lax.axis_size(axis))])  22.7 us
    dot_general x5, matrix products, dot(): lax.dot_general(a, b, (((ca,), (cb,)), ((), ())), preferred_element_type=...  10.1 us
    all_to_all x1, waiting for transfers between devices, per_device(): lax.all_to_all(keep + twin(send), ('z', 'y'), 0, 0, tiled=True).sum(0)  9.99 us
    all_to_all x1, starting transfers between devices, per_device(): got = lax.all_to_all(grads_t, SHARD, 0, 0)  9.23 us
    transpose x1, local copies, waits for them, and re-layouts, per_device(): grads.T.reshape(shards, cols, tok)  6.04 us
    all_to_all x1, starting transfers between devices, per_device(): lax.all_to_all(jnp.broadcast_to(piece[None], (chips,) + piece.shape), CHI...  6 us
  transfers between devices with their start and end apart: 21, of which 15 were waited for; matrix products, arithmetic and copies ran while one was open for 15% of the time, Pallas kernels for 4%

profile of v5, /device:TPU:1, one launch (start us, length us, event | category | flops | bytes accessed | tf_op | source)
XLA Modules:
  0.0 207.6 jit_solution(14554994277222861461)
XLA Ops:
  7.2 0.7 all-gather.2.cloned.1.call-update
  7.9 1.2 reduce-precision_convert_fusion.5
  9.6 3.8 %collective-permute-start.1 = (f32[32,128]{1,0:T(8,128)S(1)}, f32[32,128]{1,0:T(8,128)S(1)}, u32[]{:S(2)}, u32[]{:S(2)}) collective-permute-start(f32[32,128]{1,0:T(8,128)S(1)} %fusion.37), channel_id=1, source_target_pairs={{0,4},{2,6},{4,0},{6,2},{1,5},{3,7},{5,1},{7,3},{8,12},{10,14},{12... | collective-permute-start | bytes 49160 | tf_op jit(solution)/shard_map/ppermute | solution.py:40
  14.2 6.0 %copy.40 = bf16[14336,128]{1,0:T(8,128)(2,1)} copy(bf16[14336,128]{0,1:T(8,128)(2,1)} %bitcast.98) | data formatting | bytes 7340032 | tf_op jit(solution)/shard_map/transpose | solution.py:252
  20.3 9.2 %all-to-all-start = ((bf16[32,448,128]{2,1,0:T(8,128)(2,1)}), bf16[32,448,128]{2,1,0:T(8,128)(2,1)}, u32[]{:S(2)}, u32[]{:S(2)}) async-start(bf16[32,448,128]{2,1,0:T(8,128)(2,1)} %bitcast.97), calls=%async_computation | async-start | bytes 7340032 | tf_op jit(solution)/shard_map/all_to_all | solution.py:253
  29.5 3.3 %fusion.5 = f32[96,448]{1,0:T(8,128)S(1)} fusion(bf16[1,4096,448]{1,2,0:T(8,128)(2,1)} %param.10, bf16[32,4096]{1,0:T(8,128)(2,1)S(1)} %get-tuple-element.37, bf16[32,4096]{1,0:T(8,128)(2,1)S(1)} %get-tuple-element.38, bf16[32,4096]{1,0:T(8,128)(2,1)S(1)} %get-tuple-element.36), kind=kOutput, calls=%fused_computation.5 | convolution fusion | flops 354680832 | bytes 4628480 | tf_op jit(solution)/shard_map/dot_general | solution.py:30
  32.8 2.7 %collective-permute-start.5 = (f32[4,32,128]{2,1,0:T(8,128)S(1)}, f32[4,32,128]{2,1,0:T(8,128)S(1)}, u32[]{:S(2)}, u32[]{:S(2)}) collective-permute-start(f32[4,32,128]{2,1,0:T(8,128)S(1)} %bitcast.110), channel_id=1, source_target_pairs={{0,24},{8,16},{16,8},{24,0},{1,25},{9,17},{17,9},{25,1},{2,26},{10... | collective-permute-start | bytes 196616 | tf_op jit(solution)/shard_map/ppermute | solution.py:40
  36.3 26.5 %collective-permute-done.5 = f32[4,32,128]{2,1,0:T(8,128)S(1)} collective-permute-done((f32[4,32,128]{2,1,0:T(8,128)S(1)}, f32[4,32,128]{2,1,0:T(8,128)S(1)}, u32[]{:S(2)}, u32[]{:S(2)}) %collective-permute-start.5) | collective-permute-done | bytes 65568 | tf_op jit(solution)/shard_map/ppermute | solution.py:40
  62.7 20.8 %collective-permute-done.4 = f32[4,32,128]{2,1,0:T(8,128)S(1)} collective-permute-done((f32[4,32,128]{2,1,0:T(8,128)S(1)}, f32[4,32,128]{2,1,0:T(8,128)S(1)}, u32[]{:S(2)}, u32[]{:S(2)}) %collective-permute-start.4) | collective-permute-done | bytes 65568 | tf_op jit(solution)/shard_map/ppermute | solution.py:40
  83.5 3.1 %collective-permute-done.3 = f32[4,32,128]{2,1,0:T(8,128)S(1)} collective-permute-done((f32[4,32,128]{2,1,0:T(8,128)S(1)}, f32[4,32,128]{2,1,0:T(8,128)S(1)}, u32[]{:S(2)}, u32[]{:S(2)}) %collective-permute-start.3) | collective-permute-done | bytes 65568 | tf_op jit(solution)/shard_map/ppermute | solution.py:40
  86.9 0.6 collective-permute-start.6
  87.5 1.2 collective-permute-done.6
  89.7 3.2 %fusion = f32[96,448]{1,0:T(8,128)S(1)} fusion(bf16[32,4096]{1,0:T(8,128)(2,1)S(1)} %get-tuple-element.32, bf16[32,4096]{1,0:T(8,128)(2,1)S(1)} %get-tuple-element.33, bf16[32,4096]{1,0:T(8,128)(2,1)S(1)} %get-tuple-element.31, bf16[32,448,128]{2,1,0:T(8,128)(2,1)} %all-to-all-done.g_ref.got_ref), kind=kOutput, calls=%fused_computation | convolution fusion | flops 354680832 | bytes 4628480 | tf_op jit(solution)/shard_map/dot_general | solution.py:30
  93.0 2.5 %collective-permute-start.9 = (f32[32,448]{1,0:T(8,128)S(1)}, f32[32,448]{1,0:T(8,128)S(1)}, u32[]{:S(2)}, u32[]{:S(2)}) collective-permute-start(f32[32,448]{1,0:T(8,128)S(1)} %fusion.25), channel_id=1, source_target_pairs={{0,96},{32,64},{64,32},{96,0},{1,97},{33,65},{65,33},{97,1},{2,98}... | collective-permute-start | bytes 172040 | tf_op jit(solution)/shard_map/ppermute | solution.py:40
  95.4 0.6 collective-permute-start.8
  96.3 1.1 collective-permute-done.9
  97.4 2.7 %collective-permute-done.8 = f32[32,448]{1,0:T(8,128)S(1)} collective-permute-done((f32[32,448]{1,0:T(8,128)S(1)}, f32[32,448]{1,0:T(8,128)S(1)}, u32[]{:S(2)}, u32[]{:S(2)}) %collective-permute-start.8) | collective-permute-done | bytes 57376 | tf_op jit(solution)/shard_map/ppermute | solution.py:40
  100.2 3.6 %shard_map.110 = (f32[16,40,128]{2,1,0:T(8,128)S(1)}, f32[16,40,128]{2,1,0:T(8,128)S(1)}) custom-call(s32[1]{0:T(128)} %bitcast.c, f32[32,448]{1,0:T(8,128)S(1)} %get-tuple-element.28.f_ref, bf16[96,448]{1,0:T(8,128)(2,1)S(1)} %pad_maximum_fusion.4.f3_ref, bf16[32,448,128]{2,1,0:T(8,128)(2,1)} %all-to-all-done.g_ref.got_ref), custom_call_target="tpu_custom_call" | custom-call | flops 352321536 | bytes 3670016 | tf_op jit(solution)/shard_map/pallas_call | solution.py:106
  103.8 2.1 %collective-permute-start.10 = (f32[16,40,128]{2,1,0:T(8,128)S(1)}, f32[16,40,128]{2,1,0:T(8,128)S(1)}, u32[]{:S(2)}, u32[]{:S(2)}) collective-permute-start(f32[16,40,128]{2,1,0:T(8,128)S(1)} %get-tuple-element.21), channel_id=1, source_target_pairs={{0,1},{1,0},{2,3},{3,2},{4,5},{5,4},{6,7},{7,6},{8,9},{9,8},{10,11... | collective-permute-start | bytes 983048 | tf_op jit(solution)/shard_map/ppermute | solution.py:40
  105.9 1.7 collective-permute-done.10
  107.6 0.8 add.101
  108.3 6.0 %all-to-all-start.1 = ((f32[16,40,128]{2,1,0:T(8,128)}), f32[16,40,128]{2,1,0:T(8,128)S(1)}, u32[]{:S(2)}, u32[]{:S(2)}) async-start(f32[16,40,128]{2,1,0:T(8,128)} %add.101), calls=%async_computation.1 | async-start | bytes 655360 | tf_op jit(solution)/shard_map/all_to_all | solution.py:264
  114.3 2.8 %fusion.3 = f32[96,4096]{1,0:T(8,128)S(1)} fusion(bf16[1,4096,448]{1,2,0:T(8,128)(2,1)} %param.10, bf16[32,448]{1,0:T(8,128)(2,1)S(1)} %get-tuple-element.46, bf16[32,448]{1,0:T(8,128)(2,1)S(1)} %get-tuple-element.45, bf16[32,448]{1,0:T(8,128)(2,1)S(1)} %get-tuple-element.27), kind=kOutput, calls=%fused_computation.3 | convolution fusion | flops 352579584 | bytes 5328896 | tf_op jit(solution)/shard_map/dot_general | solution.py:30
  117.1 10.0 %all-to-all-done.1 = f32[16,40,128]{2,1,0:T(8,128)S(1)} async-done(((f32[16,40,128]{2,1,0:T(8,128)}), f32[16,40,128]{2,1,0:T(8,128)S(1)}, u32[]{:S(2)}, u32[]{:S(2)}) %all-to-all-start.1) | async-done | bytes 327712 | tf_op jit(solution)/shard_map/all_to_all | solution.py:264
  127.8 1.9 collective-permute-start.11
  130.0 0.8 collective-permute-done.11
  130.9 1.4 collective-permute-start.14
  132.3 0.7 collective-permute-start.13
  133.0 1.2 collective-permute-start.12
  134.3 1.4 collective-permute-done.14
  135.7 1.3 collective-permute-done.13
  137.2 0.6 fusion.26
  137.9 3.5 %all-to-all-start.2 = ((f32[16,8,128]{2,1,0:T(8,128)}), f32[16,8,128]{2,1,0:T(8,128)S(1)}, u32[]{:S(2)}, u32[]{:S(2)}) async-start(f32[16,8,128]{2,1,0:T(8,128)} %bitcast.32), calls=%async_computation.2 | async-start | bytes 131072 | tf_op jit(solution)/shard_map/all_to_all | solution.py:274
  141.5 2.9 %cholesky.17 = f32[32,32]{1,0:T(8,128)S(1)} custom-call(f32[32,32]{1,0:T(8,128)S(1)} %fusion.40), custom_call_target="Cholesky" | custom-call | tf_op jit(solution)/shard_map/jit(cholesky)/cholesky | solution.py:281
  144.4 0.6 compare_reduce_fusion
  145.1 3.5 %all-to-all-done.2 = f32[16,8,128]{2,1,0:T(8,128)S(1)} async-done(((f32[16,8,128]{2,1,0:T(8,128)}), f32[16,8,128]{2,1,0:T(8,128)S(1)}, u32[]{:S(2)}, u32[]{:S(2)}) %all-to-all-start.2) | async-done | bytes 65568 | tf_op jit(solution)/shard_map/all_to_all | solution.py:274
  148.6 0.7 broadcast_in_dim.6
  149.3 6.0 %all-to-all-start.3 = ((f32[64,8,128]{2,1,0:T(8,128)}), f32[64,8,128]{2,1,0:T(8,128)S(1)}, u32[]{:S(2)}, u32[]{:S(2)}) async-start(f32[64,8,128]{2,1,0:T(8,128)} %broadcast_in_dim.6), calls=%async_computation.3 | async-start | bytes 524288 | tf_op jit(solution)/shard_map/all_to_all | solution.py:275
  155.3 0.7 fusion.35
  156.0 2.4 %custom-call.7 = f32[1,32,32]{1,2,0:T(8,128)S(1)} custom-call(f32[1,32,32]{2,1,0:T(8,128)S(1)} %fusion.35), custom_call_target="InvertDiagBlocksLowerTriangular" | custom-call | tf_op jit(solution)/shard_map/jit(_solve_triangular)/triangular_solve | solution.py:282
  158.6 5.8 %all-to-all-done.3 = f32[64,8,128]{2,1,0:T(8,128)S(1)} async-done(((f32[64,8,128]{2,1,0:T(8,128)}), f32[64,8,128]{2,1,0:T(8,128)S(1)}, u32[]{:S(2)}, u32[]{:S(2)}) %all-to-all-start.3) | async-done | bytes 262176 | tf_op jit(solution)/shard_map/all_to_all | solution.py:275
  164.4 3.5 %collective-permute-start.15 = (f32[4,16,8,128]{3,2,1,0:T(8,128)S(1)}, f32[4,16,8,128]{3,2,1,0:T(8,128)S(1)}, u32[]{:S(2)}, u32[]{:S(2)}) collective-permute-start(f32[4,16,8,128]{3,2,1,0:T(8,128)S(1)} %bitcast.102), channel_id=1, source_target_pairs={{0,1},{1,0},{2,3},{3,2},{4,5},{5,4},{6,7},{7,6},{8,9},{9,8},{10,11... | collective-permute-start | bytes 786440 | tf_op jit(solution)/shard_map/ppermute | solution.py:40
  169.1 0.6 constant_dynamic-update-slice_fusion.2
  170.0 0.5 copy-done.2
  170.6 0.9 copy-done.1
  171.4 0.6 copy-done
  172.0 5.5 %shard_map.112 = (f32[448,1024]{1,0:T(8,128)}, f32[448,1024]{1,0:T(8,128)}, f32[448,1024]{1,0:T(8,128)}) custom-call(s32[1]{0:T(128)} %bitcast.40.p, bf16[448,192]{1,0:T(8,128)(2,1)S(1)} %bitcast.95, bf16[192,4096]{1,0:T(8,128)(2,1)S(1)} %fusion.28.basis_ref, f32[448,1024]{1,0:T(8,128)S(1)} %bitcast.93, f32[448,1024]{1,0:T(8,128)S(1)} %bitcast.94, ...), custom_call_target="tpu_custom_call" | custom-call | flops 176160768 | bytes 11010048 | tf_op jit(solution)/shard_map/pallas_call | solution.py:218
  177.5 23.3 %shard_map.111 = bf16[448,4096]{1,0:T(8,128)(2,1)} custom-call(bf16[32,448,128]{2,1,0:T(8,128)(2,1)} %all-to-all-done.g_ref.got_ref, bf16[4096,4096]{1,0:T(8,128)(2,1)} %all-gather.2.cloned.1.call-done.acts_ref, bf16[448,4096]{1,0:T(8,128)(2,1)} %bitcast.99, bf16[448,192]{1,0:T(8,128)(2,1)S(1)} %bitcast.96, bf16[192,4096]{1,0:T(8,128)(2,1)S(1)} %fusion.28.basis_ref), custom_call_target="tpu_custom_call" | custom-call | flops 15737028608 | bytes 44564480 | tf_op jit(solution)/shard_map/pallas_call | solution.py:176
  (68 shorter events, 6.9 us)
Async XLA Ops:
  7.2 1.9 copy-start.3
  7.2 170.3 %all-gather.2.cloned.1.call-start = ((), (), s32[]{:S(2)}) async-start(), calls=%async_computation.4 | async-start | bytes 34603008 | tf_op jit(solution)/shard_map/all_gather | solution.py:249
  9.6 10.7 %collective-permute-start.1 = (f32[32,128]{1,0:T(8,128)S(1)}, f32[32,128]{1,0:T(8,128)S(1)}, u32[]{:S(2)}, u32[]{:S(2)}) collective-permute-start(f32[32,128]{1,0:T(8,128)S(1)} %fusion.37), channel_id=1, source_target_pairs={{0,4},{2,6},{4,0},{6,2},{1,5},{3,7},{5,1},{7,3},{8,12},{10,14},{12... | collective-permute-start | bytes 49160 | tf_op jit(solution)/shard_map/ppermute | solution.py:40
  13.4 6.8 %collective-permute-start = (f32[32,128]{1,0:T(8,128)S(1)}, f32[32,128]{1,0:T(8,128)S(1)}, u32[]{:S(2)}, u32[]{:S(2)}) collective-permute-start(f32[32,128]{1,0:T(8,128)S(1)} %fusion.37), channel_id=1, source_target_pairs={{0,2},{2,0},{4,6},{6,4},{1,3},{3,1},{5,7},{7,5},{8,10},{10,8},{12,... | collective-permute-start | bytes 49160 | tf_op jit(solution)/shard_map/ppermute | solution.py:40
  13.8 6.4 %collective-permute-start.2 = (f32[32,128]{1,0:T(8,128)S(1)}, f32[32,128]{1,0:T(8,128)S(1)}, u32[]{:S(2)}, u32[]{:S(2)}) collective-permute-start(f32[32,128]{1,0:T(8,128)S(1)} %fusion.37), channel_id=1, source_target_pairs={{0,6},{2,4},{4,2},{6,0},{1,7},{3,5},{5,3},{7,1},{8,14},{10,12},{12... | collective-permute-start | bytes 49160 | tf_op jit(solution)/shard_map/ppermute | solution.py:40
  20.3 69.4 %all-to-all-start = ((bf16[32,448,128]{2,1,0:T(8,128)(2,1)}), bf16[32,448,128]{2,1,0:T(8,128)(2,1)}, u32[]{:S(2)}, u32[]{:S(2)}) async-start(bf16[32,448,128]{2,1,0:T(8,128)(2,1)} %bitcast.97), calls=%async_computation | async-start | bytes 7340032 | tf_op jit(solution)/shard_map/all_to_all | solution.py:253
  32.8 29.9 %collective-permute-start.5 = (f32[4,32,128]{2,1,0:T(8,128)S(1)}, f32[4,32,128]{2,1,0:T(8,128)S(1)}, u32[]{:S(2)}, u32[]{:S(2)}) collective-permute-start(f32[4,32,128]{2,1,0:T(8,128)S(1)} %bitcast.110), channel_id=1, source_target_pairs={{0,24},{8,16},{16,8},{24,0},{1,25},{9,17},{17,9},{25,1},{2,26},{10... | collective-permute-start | bytes 196616 | tf_op jit(solution)/shard_map/ppermute | solution.py:40
  35.6 47.9 %collective-permute-start.4 = (f32[4,32,128]{2,1,0:T(8,128)S(1)}, f32[4,32,128]{2,1,0:T(8,128)S(1)}, u32[]{:S(2)}, u32[]{:S(2)}) collective-permute-start(f32[4,32,128]{2,1,0:T(8,128)S(1)} %bitcast.111), channel_id=1, source_target_pairs={{0,16},{8,24},{16,0},{24,8},{1,17},{9,25},{17,1},{25,9},{2,18},{10... | collective-permute-start | bytes 196616 | tf_op jit(solution)/shard_map/ppermute | solution.py:40
  36.1 50.5 %collective-permute-start.3 = (f32[4,32,128]{2,1,0:T(8,128)S(1)}, f32[4,32,128]{2,1,0:T(8,128)S(1)}, u32[]{:S(2)}, u32[]{:S(2)}) collective-permute-start(f32[4,32,128]{2,1,0:T(8,128)S(1)} %bitcast.112), channel_id=1, source_target_pairs={{0,8},{8,0},{16,24},{24,16},{1,9},{9,1},{17,25},{25,17},{2,10},{10... | collective-permute-start | bytes 196616 | tf_op jit(solution)/shard_map/ppermute | solution.py:40
  86.9 1.7 collective-permute-start.6
  93.0 4.4 %collective-permute-start.9 = (f32[32,448]{1,0:T(8,128)S(1)}, f32[32,448]{1,0:T(8,128)S(1)}, u32[]{:S(2)}, u32[]{:S(2)}) collective-permute-start(f32[32,448]{1,0:T(8,128)S(1)} %fusion.25), channel_id=1, source_target_pairs={{0,96},{32,64},{64,32},{96,0},{1,97},{33,65},{65,33},{97,1},{2,98}... | collective-permute-start | bytes 172040 | tf_op jit(solution)/shard_map/ppermute | solution.py:40
  95.4 4.7 %collective-permute-start.8 = (f32[32,448]{1,0:T(8,128)S(1)}, f32[32,448]{1,0:T(8,128)S(1)}, u32[]{:S(2)}, u32[]{:S(2)}) collective-permute-start(f32[32,448]{1,0:T(8,128)S(1)} %fusion.25), channel_id=1, source_target_pairs={{0,64},{32,96},{64,0},{96,32},{1,65},{33,97},{65,1},{97,33},{2,66}... | collective-permute-start | bytes 172040 | tf_op jit(solution)/shard_map/ppermute | solution.py:40
  96.0 4.1 %collective-permute-start.7 = (f32[32,448]{1,0:T(8,128)S(1)}, f32[32,448]{1,0:T(8,128)S(1)}, u32[]{:S(2)}, u32[]{:S(2)}) collective-permute-start(f32[32,448]{1,0:T(8,128)S(1)} %fusion.25), channel_id=1, source_target_pairs={{0,32},{32,0},{64,96},{96,64},{1,33},{33,1},{65,97},{97,65},{2,34}... | collective-permute-start | bytes 172040 | tf_op jit(solution)/shard_map/ppermute | solution.py:40
  103.8 3.8 %collective-permute-start.10 = (f32[16,40,128]{2,1,0:T(8,128)S(1)}, f32[16,40,128]{2,1,0:T(8,128)S(1)}, u32[]{:S(2)}, u32[]{:S(2)}) collective-permute-start(f32[16,40,128]{2,1,0:T(8,128)S(1)} %get-tuple-element.21), channel_id=1, source_target_pairs={{0,1},{1,0},{2,3},{3,2},{4,5},{5,4},{6,7},{7,6},{8,9},{9,8},{10,11... | collective-permute-start | bytes 983048 | tf_op jit(solution)/shard_map/ppermute | solution.py:40
  108.3 18.8 %all-to-all-start.1 = ((f32[16,40,128]{2,1,0:T(8,128)}), f32[16,40,128]{2,1,0:T(8,128)S(1)}, u32[]{:S(2)}, u32[]{:S(2)}) async-start(f32[16,40,128]{2,1,0:T(8,128)} %add.101), calls=%async_computation.1 | async-start | bytes 655360 | tf_op jit(solution)/shard_map/all_to_all | solution.py:264
  127.8 3.0 %collective-permute-start.11 = (f32[32,2048]{1,0:T(8,128)S(1)}, f32[32,2048]{1,0:T(8,128)S(1)}, u32[]{:S(2)}, u32[]{:S(2)}) collective-permute-start(f32[32,2048]{1,0:T(8,128)S(1)} %constant_dynamic-slice_fusion), channel_id=1, source_target_pairs={{0,1},{1,0},{2,3},{3,2},{4,5},{5,4},{6,7},{7,6},{8,9},{9,8},{10,11... | collective-permute-start | bytes 786440 | tf_op jit(solution)/shard_map/ppermute | solution.py:40
  130.9 4.8 %collective-permute-start.14 = (f32[8,2048]{1,0:T(8,128)S(1)}, f32[8,2048]{1,0:T(8,128)S(1)}, u32[]{:S(2)}, u32[]{:S(2)}) collective-permute-start(f32[8,2048]{1,0:T(8,128)S(1)} %get-tuple-element.41), channel_id=1, source_target_pairs={{0,96},{32,64},{64,32},{96,0},{1,97},{33,65},{65,33},{97,1},{2,98}... | collective-permute-start | bytes 196616 | tf_op jit(solution)/shard_map/ppermute | solution.py:40
  132.3 4.7 %collective-permute-start.13 = (f32[8,2048]{1,0:T(8,128)S(1)}, f32[8,2048]{1,0:T(8,128)S(1)}, u32[]{:S(2)}, u32[]{:S(2)}) collective-permute-start(f32[8,2048]{1,0:T(8,128)S(1)} %get-tuple-element.42), channel_id=1, source_target_pairs={{0,64},{32,96},{64,0},{96,32},{1,65},{33,97},{65,1},{97,33},{2,66}... | collective-permute-start | bytes 196616 | tf_op jit(solution)/shard_map/ppermute | solution.py:40
  133.0 4.2 %collective-permute-start.12 = (f32[8,2048]{1,0:T(8,128)S(1)}, f32[8,2048]{1,0:T(8,128)S(1)}, u32[]{:S(2)}, u32[]{:S(2)}) collective-permute-start(f32[8,2048]{1,0:T(8,128)S(1)} %get-tuple-element.43), channel_id=1, source_target_pairs={{0,32},{32,0},{64,96},{96,64},{1,33},{33,1},{65,97},{97,65},{2,34}... | collective-permute-start | bytes 196616 | tf_op jit(solution)/shard_map/ppermute | solution.py:40
  137.9 10.6 %all-to-all-start.2 = ((f32[16,8,128]{2,1,0:T(8,128)}), f32[16,8,128]{2,1,0:T(8,128)S(1)}, u32[]{:S(2)}, u32[]{:S(2)}) async-start(f32[16,8,128]{2,1,0:T(8,128)} %bitcast.32), calls=%async_computation.2 | async-start | bytes 131072 | tf_op jit(solution)/shard_map/all_to_all | solution.py:274
  149.3 15.1 %all-to-all-start.3 = ((f32[64,8,128]{2,1,0:T(8,128)}), f32[64,8,128]{2,1,0:T(8,128)S(1)}, u32[]{:S(2)}, u32[]{:S(2)}) async-start(f32[64,8,128]{2,1,0:T(8,128)} %broadcast_in_dim.6), calls=%async_computation.3 | async-start | bytes 524288 | tf_op jit(solution)/shard_map/all_to_all | solution.py:275
  164.4 4.7 %collective-permute-start.15 = (f32[4,16,8,128]{3,2,1,0:T(8,128)S(1)}, f32[4,16,8,128]{3,2,1,0:T(8,128)S(1)}, u32[]{:S(2)}, u32[]{:S(2)}) collective-permute-start(f32[4,16,8,128]{3,2,1,0:T(8,128)S(1)} %bitcast.102), channel_id=1, source_target_pairs={{0,1},{1,0},{2,3},{3,2},{4,5},{5,4},{6,7},{7,6},{8,9},{9,8},{10,11... | collective-permute-start | bytes 786440 | tf_op jit(solution)/shard_map/ppermute | solution.py:40
  169.7 0.8 copy-start.2
  169.7 1.7 copy-start.1
  169.8 2.2 %copy-start = (f32[1024,448]{0,1:T(8,128)S(1)}, f32[1024,448]{0,1:T(8,128)}, u32[]{:S(2)}) copy-start(f32[1024,448]{0,1:T(8,128)} %param.11) | copy-start | bytes 5505028
Sparse Core Ops, SparseCore 0:
  10.3 166.5 all-gather.1

commit v6 on v5

--- a/solution.py
+++ b/solution.py
@@ -79,7 +79,7 @@
     shards, cols, tok = got.shape
     rank = factor.shape[0]
     chips = shards // 2
-    step = min(4, chips)
+    step = min(8, chips)
     extra = rank * rank // tok
 
     def body(c, f_ref, f3_ref, g_ref, keep_ref, send_ref, gram_ref):
@@ -128,10 +128,10 @@
     block = min(1024, width)
     steps = width // block
     depth6 = ortho6.shape[1]
-    parts = 4
+    parts = 8
     rows = tokens // parts
 
-    def body(got_ref, acts_ref, error_ref, ortho_ref, basis_ref, out_ref, columns, held, gradient, sems):
+    def body(got_ref, acts_ref, error_ref, ortho_ref, basis_ref, out_ref, columns, held, sems):
         n = pl.program_id(0)
         slot = lax.rem(n, 2)
 
@@ -139,6 +139,11 @@
             piece = pl.ds(k * rows, rows)
             place = pl.ds(pl.multiple_of(m * block, block), block)
             return pltpu.make_async_copy(acts_ref.at[piece, place], held.at[s, piece], sems.at[s, k])
+
+        def close(gradient):
+            approx = jnp.dot(ortho_ref[...], basis_ref[...], preferred_element_type=jnp.float32)
+            matrix = gradient * scale + error_ref[...].astype(jnp.float32)
+            out_ref[...] = (matrix - approx).astype(jnp.bfloat16)
 
         @pl.when(n == 0)
         def _():
@@ -155,22 +160,18 @@
                 piece = slice(k * rows, (k + 1) * rows)
                 d = jnp.dot(columns[:, piece], held[0, piece], preferred_element_type=jnp.float32)
                 total = d if total is None else total + d
-            gradient[...] = total
+            close(total)
 
         @pl.when(n > 0)
         def _():
             for k in range(parts):
                 copy(n, slot, k).wait()
-            gradient[...] = jnp.dot(columns[...], held[slot], preferred_element_type=jnp.float32)
+            close(jnp.dot(columns[...], held[slot], preferred_element_type=jnp.float32))
 
         @pl.when(n + 2 < steps)
         def _():
             for k in range(parts):
                 copy(n + 2, slot, k).start()
-
-        approx = jnp.dot(ortho_ref[...], basis_ref[...], preferred_element_type=jnp.float32)
-        matrix = gradient[...] * scale + error_ref[...].astype(jnp.float32)
-        out_ref[...] = (matrix - approx).astype(jnp.bfloat16)
 
     wide = pl.BlockSpec((cols, block), lambda n: (0, n))
     return pl.pallas_call(
@@ -188,7 +189,6 @@
         scratch_shapes=[
             pltpu.VMEM((cols, tokens), got.dtype),
             pltpu.VMEM((2, tokens, block), gathered.dtype),
-            pltpu.VMEM((cols, block), jnp.float32),
             pltpu.SemaphoreType.DMA((2, parts)),
         ],
         compiler_params=pltpu.CompilerParams(vmem_limit_bytes=VMEM_LIMIT),
@@ -200,7 +200,7 @@
 
 def adam(place, ortho6, basis6, weight, moment_one, moment_two):
     cols, rows = weight.shape
-    block = min(256, rows)
+    block = min(512, rows)
     steps = rows // block
     depth6 = ortho6.shape[1]
 

time: 208 us -> 207 us (level)
  Pallas kernels: 32.3 us -> 29.7 us
  transfers between devices with their start and end apart: 21 -> 21, of which waited for: 15 -> 16; matrix products, arithmetic and copies ran while one was open for 15% -> 15% of each run, Pallas kernels for 4% -> 3%
where the time goes in v6:
time: 207 us; the launch traced here: 206 us
  waiting for transfers between devices  82.2 us (40%)
  starting transfers between devices  47.7 us (23%)
  Pallas kernels  29.7 us (14%)
  between operations  14.4 us (7%)
  matrix products  11.1 us (5%)
  other arithmetic  10.8 us (5%)
  local copies, waits for them, and re-layouts  10.3 us (5%)
    ppermute x16, waiting for transfers between devices, swap(): lax.ppermute(x, axis, [(i, i ^ k) for i in range(lax.axis_size(axis))])  60.8 us
    ppermute x16, starting transfers between devices, swap(): lax.ppermute(x, axis, [(i, i ^ k) for i in range(lax.axis_size(axis))])  22.6 us
    pallas_call x1, Pallas kernels, finish_error(): pl.pallas_call(body, out_shape=jax.ShapeDtypeStruct(error_t.shape, jnp.bf...  22.5 us
    dot_general x5, matrix products, dot(): lax.dot_general(a, b, (((ca,), (cb,)), ((), ())), preferred_element_type=...  10.1 us
    all_to_all x1, waiting for transfers between devices, per_device(): lax.all_to_all(keep + twin(send), ('z', 'y'), 0, 0, tiled=True).sum(0)  10.1 us
    all_to_all x1, starting transfers between devices, per_device(): got = lax.all_to_all(grads_t, SHARD, 0, 0)  9.23 us
    all_to_all x1, starting transfers between devices, per_device(): lax.all_to_all(keep + twin(send), ('z', 'y'), 0, 0, tiled=True).sum(0)  6.75 us
    transpose x1, local copies, waits for them, and re-layouts, per_device(): grads.T.reshape(shards, cols, tok)  6.04 us
  transfers between devices with their start and end apart: 21, of which 16 were waited for; matrix products, arithmetic and copies ran while one was open for 15% of the time, Pallas kernels for 3%

profile of v6, /device:TPU:1, one launch (start us, length us, event | category | flops | bytes accessed | tf_op | source)
XLA Modules:
  0.0 206.2 jit_solution(17931086667737745929)
XLA Ops:
  7.2 0.7 all-gather.2.cloned.1.call-update
  7.9 1.2 reduce-precision_convert_fusion.5
  9.6 3.8 %collective-permute-start.1 = (f32[32,128]{1,0:T(8,128)S(1)}, f32[32,128]{1,0:T(8,128)S(1)}, u32[]{:S(2)}, u32[]{:S(2)}) collective-permute-start(f32[32,128]{1,0:T(8,128)S(1)} %fusion.37), channel_id=1, source_target_pairs={{0,4},{2,6},{4,0},{6,2},{1,5},{3,7},{5,1},{7,3},{8,12},{10,14},{12... | collective-permute-start | bytes 49160 | tf_op jit(solution)/shard_map/ppermute | solution.py:40
  14.2 6.0 %copy.40 = bf16[14336,128]{1,0:T(8,128)(2,1)} copy(bf16[14336,128]{0,1:T(8,128)(2,1)} %bitcast.98) | data formatting | bytes 7340032 | tf_op jit(solution)/shard_map/transpose | solution.py:252
  20.3 9.2 %all-to-all-start = ((bf16[32,448,128]{2,1,0:T(8,128)(2,1)}), bf16[32,448,128]{2,1,0:T(8,128)(2,1)}, u32[]{:S(2)}, u32[]{:S(2)}) async-start(bf16[32,448,128]{2,1,0:T(8,128)(2,1)} %bitcast.97), calls=%async_computation | async-start | bytes 7340032 | tf_op jit(solution)/shard_map/all_to_all | solution.py:253
  29.5 3.3 %fusion.5 = f32[96,448]{1,0:T(8,128)S(1)} fusion(bf16[1,4096,448]{1,2,0:T(8,128)(2,1)} %param.10, bf16[32,4096]{1,0:T(8,128)(2,1)S(1)} %get-tuple-element.37, bf16[32,4096]{1,0:T(8,128)(2,1)S(1)} %get-tuple-element.38, bf16[32,4096]{1,0:T(8,128)(2,1)S(1)} %get-tuple-element.36), kind=kOutput, calls=%fused_computation.5 | convolution fusion | flops 354680832 | bytes 4628480 | tf_op jit(solution)/shard_map/dot_general | solution.py:30
  32.8 2.7 %collective-permute-start.5 = (f32[4,32,128]{2,1,0:T(8,128)S(1)}, f32[4,32,128]{2,1,0:T(8,128)S(1)}, u32[]{:S(2)}, u32[]{:S(2)}) collective-permute-start(f32[4,32,128]{2,1,0:T(8,128)S(1)} %bitcast.110), channel_id=1, source_target_pairs={{0,24},{8,16},{16,8},{24,0},{1,25},{9,17},{17,9},{25,1},{2,26},{10... | collective-permute-start | bytes 196616 | tf_op jit(solution)/shard_map/ppermute | solution.py:40
  36.3 26.5 %collective-permute-done.5 = f32[4,32,128]{2,1,0:T(8,128)S(1)} collective-permute-done((f32[4,32,128]{2,1,0:T(8,128)S(1)}, f32[4,32,128]{2,1,0:T(8,128)S(1)}, u32[]{:S(2)}, u32[]{:S(2)}) %collective-permute-start.5) | collective-permute-done | bytes 65568 | tf_op jit(solution)/shard_map/ppermute | solution.py:40
  62.7 20.8 %collective-permute-done.4 = f32[4,32,128]{2,1,0:T(8,128)S(1)} collective-permute-done((f32[4,32,128]{2,1,0:T(8,128)S(1)}, f32[4,32,128]{2,1,0:T(8,128)S(1)}, u32[]{:S(2)}, u32[]{:S(2)}) %collective-permute-start.4) | collective-permute-done | bytes 65568 | tf_op jit(solution)/shard_map/ppermute | solution.py:40
  83.5 3.1 %collective-permute-done.3 = f32[4,32,128]{2,1,0:T(8,128)S(1)} collective-permute-done((f32[4,32,128]{2,1,0:T(8,128)S(1)}, f32[4,32,128]{2,1,0:T(8,128)S(1)}, u32[]{:S(2)}, u32[]{:S(2)}) %collective-permute-start.3) | collective-permute-done | bytes 65568 | tf_op jit(solution)/shard_map/ppermute | solution.py:40
  86.9 0.6 collective-permute-start.6
  87.5 1.2 collective-permute-done.6
  89.7 3.2 %fusion = f32[96,448]{1,0:T(8,128)S(1)} fusion(bf16[32,4096]{1,0:T(8,128)(2,1)S(1)} %get-tuple-element.32, bf16[32,4096]{1,0:T(8,128)(2,1)S(1)} %get-tuple-element.33, bf16[32,4096]{1,0:T(8,128)(2,1)S(1)} %get-tuple-element.31, bf16[32,448,128]{2,1,0:T(8,128)(2,1)} %all-to-all-done.g_ref.got_ref), kind=kOutput, calls=%fused_computation | convolution fusion | flops 354680832 | bytes 4628480 | tf_op jit(solution)/shard_map/dot_general | solution.py:30
  93.0 2.5 %collective-permute-start.9 = (f32[32,448]{1,0:T(8,128)S(1)}, f32[32,448]{1,0:T(8,128)S(1)}, u32[]{:S(2)}, u32[]{:S(2)}) collective-permute-start(f32[32,448]{1,0:T(8,128)S(1)} %fusion.25), channel_id=1, source_target_pairs={{0,96},{32,64},{64,32},{96,0},{1,97},{33,65},{65,33},{97,1},{2,98}... | collective-permute-start | bytes 172040 | tf_op jit(solution)/shard_map/ppermute | solution.py:40
  95.4 0.6 collective-permute-start.8
  96.3 1.1 collective-permute-done.9
  97.4 2.7 %collective-permute-done.8 = f32[32,448]{1,0:T(8,128)S(1)} collective-permute-done((f32[32,448]{1,0:T(8,128)S(1)}, f32[32,448]{1,0:T(8,128)S(1)}, u32[]{:S(2)}, u32[]{:S(2)}) %collective-permute-start.8) | collective-permute-done | bytes 57376 | tf_op jit(solution)/shard_map/ppermute | solution.py:40
  100.2 2.6 %shard_map.110 = (f32[16,40,128]{2,1,0:T(8,128)S(1)}, f32[16,40,128]{2,1,0:T(8,128)S(1)}) custom-call(s32[1]{0:T(128)} %bitcast.c, f32[32,448]{1,0:T(8,128)S(1)} %get-tuple-element.28.f_ref, bf16[96,448]{1,0:T(8,128)(2,1)S(1)} %pad_maximum_fusion.4.f3_ref, bf16[32,448,128]{2,1,0:T(8,128)(2,1)} %all-to-all-done.g_ref.got_ref), custom_call_target="tpu_custom_call" | custom-call | flops 352321536 | bytes 3670016 | tf_op jit(solution)/shard_map/pallas_call | solution.py:106
  102.9 2.1 %collective-permute-start.10 = (f32[16,40,128]{2,1,0:T(8,128)S(1)}, f32[16,40,128]{2,1,0:T(8,128)S(1)}, u32[]{:S(2)}, u32[]{:S(2)}) collective-permute-start(f32[16,40,128]{2,1,0:T(8,128)S(1)} %get-tuple-element.21), channel_id=1, source_target_pairs={{0,1},{1,0},{2,3},{3,2},{4,5},{5,4},{6,7},{7,6},{8,9},{9,8},{10,11... | collective-permute-start | bytes 983048 | tf_op jit(solution)/shard_map/ppermute | solution.py:40
  105.0 1.3 collective-permute-done.10
  106.2 0.8 add.101
  107.0 6.7 %all-to-all-start.1 = ((f32[16,40,128]{2,1,0:T(8,128)}), f32[16,40,128]{2,1,0:T(8,128)S(1)}, u32[]{:S(2)}, u32[]{:S(2)}) async-start(f32[16,40,128]{2,1,0:T(8,128)} %add.101), calls=%async_computation.1 | async-start | bytes 655360 | tf_op jit(solution)/shard_map/all_to_all | solution.py:264
  113.7 2.8 %fusion.3 = f32[96,4096]{1,0:T(8,128)S(1)} fusion(bf16[1,4096,448]{1,2,0:T(8,128)(2,1)} %param.10, bf16[32,448]{1,0:T(8,128)(2,1)S(1)} %get-tuple-element.46, bf16[32,448]{1,0:T(8,128)(2,1)S(1)} %get-tuple-element.45, bf16[32,448]{1,0:T(8,128)(2,1)S(1)} %get-tuple-element.27), kind=kOutput, calls=%fused_computation.3 | convolution fusion | flops 352579584 | bytes 5328896 | tf_op jit(solution)/shard_map/dot_general | solution.py:30
  116.5 10.1 %all-to-all-done.1 = f32[16,40,128]{2,1,0:T(8,128)S(1)} async-done(((f32[16,40,128]{2,1,0:T(8,128)}), f32[16,40,128]{2,1,0:T(8,128)S(1)}, u32[]{:S(2)}, u32[]{:S(2)}) %all-to-all-start.1) | async-done | bytes 327712 | tf_op jit(solution)/shard_map/all_to_all | solution.py:264
  127.2 1.6 collective-permute-start.11
  129.3 0.8 collective-permute-done.11
  130.1 1.1 collective-permute-start.14
  131.2 1.2 collective-permute-start.13
  132.4 1.0 collective-permute-start.12
  133.5 1.4 collective-permute-done.14
  134.9 1.0 collective-permute-done.13
  136.5 0.6 fusion.26
  137.1 3.5 %all-to-all-start.2 = ((f32[16,8,128]{2,1,0:T(8,128)}), f32[16,8,128]{2,1,0:T(8,128)S(1)}, u32[]{:S(2)}, u32[]{:S(2)}) async-start(f32[16,8,128]{2,1,0:T(8,128)} %bitcast.32), calls=%async_computation.2 | async-start | bytes 131072 | tf_op jit(solution)/shard_map/all_to_all | solution.py:274
  140.7 2.9 %cholesky.17 = f32[32,32]{1,0:T(8,128)S(1)} custom-call(f32[32,32]{1,0:T(8,128)S(1)} %fusion.40), custom_call_target="Cholesky" | custom-call | tf_op jit(solution)/shard_map/jit(cholesky)/cholesky | solution.py:281
  143.7 0.6 compare_reduce_fusion
  144.3 3.5 %all-to-all-done.2 = f32[16,8,128]{2,1,0:T(8,128)S(1)} async-done(((f32[16,8,128]{2,1,0:T(8,128)}), f32[16,8,128]{2,1,0:T(8,128)S(1)}, u32[]{:S(2)}, u32[]{:S(2)}) %all-to-all-start.2) | async-done | bytes 65568 | tf_op jit(solution)/shard_map/all_to_all | solution.py:274
  147.8 0.7 broadcast_in_dim.6
  148.5 5.5 %all-to-all-start.3 = ((f32[64,8,128]{2,1,0:T(8,128)}), f32[64,8,128]{2,1,0:T(8,128)S(1)}, u32[]{:S(2)}, u32[]{:S(2)}) async-start(f32[64,8,128]{2,1,0:T(8,128)} %broadcast_in_dim.6), calls=%async_computation.3 | async-start | bytes 524288 | tf_op jit(solution)/shard_map/all_to_all | solution.py:275
  154.1 0.7 fusion.35
  154.7 2.4 %custom-call.7 = f32[1,32,32]{1,2,0:T(8,128)S(1)} custom-call(f32[1,32,32]{2,1,0:T(8,128)S(1)} %fusion.35), custom_call_target="InvertDiagBlocksLowerTriangular" | custom-call | tf_op jit(solution)/shard_map/jit(_solve_triangular)/triangular_solve | solution.py:282
  157.4 6.0 %all-to-all-done.3 = f32[64,8,128]{2,1,0:T(8,128)S(1)} async-done(((f32[64,8,128]{2,1,0:T(8,128)}), f32[64,8,128]{2,1,0:T(8,128)S(1)}, u32[]{:S(2)}, u32[]{:S(2)}) %all-to-all-start.3) | async-done | bytes 262176 | tf_op jit(solution)/shard_map/all_to_all | solution.py:275
  163.4 3.7 %collective-permute-start.15 = (f32[4,16,8,128]{3,2,1,0:T(8,128)S(1)}, f32[4,16,8,128]{3,2,1,0:T(8,128)S(1)}, u32[]{:S(2)}, u32[]{:S(2)}) collective-permute-start(f32[4,16,8,128]{3,2,1,0:T(8,128)S(1)} %bitcast.102), channel_id=1, source_target_pairs={{0,1},{1,0},{2,3},{3,2},{4,5},{5,4},{6,7},{7,6},{8,9},{9,8},{10,11... | collective-permute-start | bytes 786440 | tf_op jit(solution)/shard_map/ppermute | solution.py:40
  168.3 0.6 constant_dynamic-update-slice_fusion.2
  169.7 0.9 copy-done.1
  170.6 0.6 copy-done
  171.1 4.5 %shard_map.112 = (f32[448,1024]{1,0:T(8,128)}, f32[448,1024]{1,0:T(8,128)}, f32[448,1024]{1,0:T(8,128)}) custom-call(s32[1]{0:T(128)} %bitcast.40.p, bf16[448,192]{1,0:T(8,128)(2,1)S(1)} %bitcast.95, bf16[192,4096]{1,0:T(8,128)(2,1)S(1)} %fusion.28.basis_ref, f32[448,1024]{1,0:T(8,128)S(1)} %bitcast.93, f32[448,1024]{1,0:T(8,128)S(1)} %bitcast.94, ...), custom_call_target="tpu_custom_call" | custom-call | flops 176160768 | bytes 11010048 | tf_op jit(solution)/shard_map/pallas_call | solution.py:218
  175.6 1.2 all-gather.2.cloned.1.call-done.acts_ref
  176.9 22.5 %shard_map.111 = bf16[448,4096]{1,0:T(8,128)(2,1)} custom-call(bf16[32,448,128]{2,1,0:T(8,128)(2,1)} %all-to-all-done.g_ref.got_ref, bf16[4096,4096]{1,0:T(8,128)(2,1)} %all-gather.2.cloned.1.call-done.acts_ref, bf16[448,4096]{1,0:T(8,128)(2,1)} %bitcast.99, bf16[448,192]{1,0:T(8,128)(2,1)S(1)} %bitcast.96, bf16[192,4096]{1,0:T(8,128)(2,1)S(1)} %fusion.28.basis_ref), custom_call_target="tpu_custom_call" | custom-call | flops 15737028608 | bytes 44564480 | tf_op jit(solution)/shard_map/pallas_call | solution.py:177
  (68 shorter events, 7.7 us)
Async XLA Ops:
  7.2 1.9 copy-start.3
  7.2 169.7 %all-gather.2.cloned.1.call-start = ((), (), s32[]{:S(2)}) async-start(), calls=%async_computation.4 | async-start | bytes 34603008 | tf_op jit(solution)/shard_map/all_gather | solution.py:249
  9.6 10.7 %collective-permute-start.1 = (f32[32,128]{1,0:T(8,128)S(1)}, f32[32,128]{1,0:T(8,128)S(1)}, u32[]{:S(2)}, u32[]{:S(2)}) collective-permute-start(f32[32,128]{1,0:T(8,128)S(1)} %fusion.37), channel_id=1, source_target_pairs={{0,4},{2,6},{4,0},{6,2},{1,5},{3,7},{5,1},{7,3},{8,12},{10,14},{12... | collective-permute-start | bytes 49160 | tf_op jit(solution)/shard_map/ppermute | solution.py:40
  13.4 6.8 %collective-permute-start = (f32[32,128]{1,0:T(8,128)S(1)}, f32[32,128]{1,0:T(8,128)S(1)}, u32[]{:S(2)}, u32[]{:S(2)}) collective-permute-start(f32[32,128]{1,0:T(8,128)S(1)} %fusion.37), channel_id=1, source_target_pairs={{0,2},{2,0},{4,6},{6,4},{1,3},{3,1},{5,7},{7,5},{8,10},{10,8},{12,... | collective-permute-start | bytes 49160 | tf_op jit(solution)/shard_map/ppermute | solution.py:40
  13.8 6.4 %collective-permute-start.2 = (f32[32,128]{1,0:T(8,128)S(1)}, f32[32,128]{1,0:T(8,128)S(1)}, u32[]{:S(2)}, u32[]{:S(2)}) collective-permute-start(f32[32,128]{1,0:T(8,128)S(1)} %fusion.37), channel_id=1, source_target_pairs={{0,6},{2,4},{4,2},{6,0},{1,7},{3,5},{5,3},{7,1},{8,14},{10,12},{12... | collective-permute-start | bytes 49160 | tf_op jit(solution)/shard_map/ppermute | solution.py:40
  20.3 69.4 %all-to-all-start = ((bf16[32,448,128]{2,1,0:T(8,128)(2,1)}), bf16[32,448,128]{2,1,0:T(8,128)(2,1)}, u32[]{:S(2)}, u32[]{:S(2)}) async-start(bf16[32,448,128]{2,1,0:T(8,128)(2,1)} %bitcast.97), calls=%async_computation | async-start | bytes 7340032 | tf_op jit(solution)/shard_map/all_to_all | solution.py:253
  32.8 29.9 %collective-permute-start.5 = (f32[4,32,128]{2,1,0:T(8,128)S(1)}, f32[4,32,128]{2,1,0:T(8,128)S(1)}, u32[]{:S(2)}, u32[]{:S(2)}) collective-permute-start(f32[4,32,128]{2,1,0:T(8,128)S(1)} %bitcast.110), channel_id=1, source_target_pairs={{0,24},{8,16},{16,8},{24,0},{1,25},{9,17},{17,9},{25,1},{2,26},{10... | collective-permute-start | bytes 196616 | tf_op jit(solution)/shard_map/ppermute | solution.py:40
  35.6 47.9 %collective-permute-start.4 = (f32[4,32,128]{2,1,0:T(8,128)S(1)}, f32[4,32,128]{2,1,0:T(8,128)S(1)}, u32[]{:S(2)}, u32[]{:S(2)}) collective-permute-start(f32[4,32,128]{2,1,0:T(8,128)S(1)} %bitcast.111), channel_id=1, source_target_pairs={{0,16},{8,24},{16,0},{24,8},{1,17},{9,25},{17,1},{25,9},{2,18},{10... | collective-permute-start | bytes 196616 | tf_op jit(solution)/shard_map/ppermute | solution.py:40
  36.1 50.5 %collective-permute-start.3 = (f32[4,32,128]{2,1,0:T(8,128)S(1)}, f32[4,32,128]{2,1,0:T(8,128)S(1)}, u32[]{:S(2)}, u32[]{:S(2)}) collective-permute-start(f32[4,32,128]{2,1,0:T(8,128)S(1)} %bitcast.112), channel_id=1, source_target_pairs={{0,8},{8,0},{16,24},{24,16},{1,9},{9,1},{17,25},{25,17},{2,10},{10... | collective-permute-start | bytes 196616 | tf_op jit(solution)/shard_map/ppermute | solution.py:40
  86.9 1.7 collective-permute-start.6
  93.0 4.4 %collective-permute-start.9 = (f32[32,448]{1,0:T(8,128)S(1)}, f32[32,448]{1,0:T(8,128)S(1)}, u32[]{:S(2)}, u32[]{:S(2)}) collective-permute-start(f32[32,448]{1,0:T(8,128)S(1)} %fusion.25), channel_id=1, source_target_pairs={{0,96},{32,64},{64,32},{96,0},{1,97},{33,65},{65,33},{97,1},{2,98}... | collective-permute-start | bytes 172040 | tf_op jit(solution)/shard_map/ppermute | solution.py:40
  95.4 4.7 %collective-permute-start.8 = (f32[32,448]{1,0:T(8,128)S(1)}, f32[32,448]{1,0:T(8,128)S(1)}, u32[]{:S(2)}, u32[]{:S(2)}) collective-permute-start(f32[32,448]{1,0:T(8,128)S(1)} %fusion.25), channel_id=1, source_target_pairs={{0,64},{32,96},{64,0},{96,32},{1,65},{33,97},{65,1},{97,33},{2,66}... | collective-permute-start | bytes 172040 | tf_op jit(solution)/shard_map/ppermute | solution.py:40
  96.0 4.1 %collective-permute-start.7 = (f32[32,448]{1,0:T(8,128)S(1)}, f32[32,448]{1,0:T(8,128)S(1)}, u32[]{:S(2)}, u32[]{:S(2)}) collective-permute-start(f32[32,448]{1,0:T(8,128)S(1)} %fusion.25), channel_id=1, source_target_pairs={{0,32},{32,0},{64,96},{96,64},{1,33},{33,1},{65,97},{97,65},{2,34}... | collective-permute-start | bytes 172040 | tf_op jit(solution)/shard_map/ppermute | solution.py:40
  102.9 3.3 %collective-permute-start.10 = (f32[16,40,128]{2,1,0:T(8,128)S(1)}, f32[16,40,128]{2,1,0:T(8,128)S(1)}, u32[]{:S(2)}, u32[]{:S(2)}) collective-permute-start(f32[16,40,128]{2,1,0:T(8,128)S(1)} %get-tuple-element.21), channel_id=1, source_target_pairs={{0,1},{1,0},{2,3},{3,2},{4,5},{5,4},{6,7},{7,6},{8,9},{9,8},{10,11... | collective-permute-start | bytes 983048 | tf_op jit(solution)/shard_map/ppermute | solution.py:40
  107.0 19.6 %all-to-all-start.1 = ((f32[16,40,128]{2,1,0:T(8,128)}), f32[16,40,128]{2,1,0:T(8,128)S(1)}, u32[]{:S(2)}, u32[]{:S(2)}) async-start(f32[16,40,128]{2,1,0:T(8,128)} %add.101), calls=%async_computation.1 | async-start | bytes 655360 | tf_op jit(solution)/shard_map/all_to_all | solution.py:264
  127.2 2.8 %collective-permute-start.11 = (f32[32,2048]{1,0:T(8,128)S(1)}, f32[32,2048]{1,0:T(8,128)S(1)}, u32[]{:S(2)}, u32[]{:S(2)}) collective-permute-start(f32[32,2048]{1,0:T(8,128)S(1)} %constant_dynamic-slice_fusion), channel_id=1, source_target_pairs={{0,1},{1,0},{2,3},{3,2},{4,5},{5,4},{6,7},{7,6},{8,9},{9,8},{10,11... | collective-permute-start | bytes 786440 | tf_op jit(solution)/shard_map/ppermute | solution.py:40
  130.1 4.8 %collective-permute-start.14 = (f32[8,2048]{1,0:T(8,128)S(1)}, f32[8,2048]{1,0:T(8,128)S(1)}, u32[]{:S(2)}, u32[]{:S(2)}) collective-permute-start(f32[8,2048]{1,0:T(8,128)S(1)} %get-tuple-element.41), channel_id=1, source_target_pairs={{0,96},{32,64},{64,32},{96,0},{1,97},{33,65},{65,33},{97,1},{2,98}... | collective-permute-start | bytes 196616 | tf_op jit(solution)/shard_map/ppermute | solution.py:40
  131.2 4.7 %collective-permute-start.13 = (f32[8,2048]{1,0:T(8,128)S(1)}, f32[8,2048]{1,0:T(8,128)S(1)}, u32[]{:S(2)}, u32[]{:S(2)}) collective-permute-start(f32[8,2048]{1,0:T(8,128)S(1)} %get-tuple-element.42), channel_id=1, source_target_pairs={{0,64},{32,96},{64,0},{96,32},{1,65},{33,97},{65,1},{97,33},{2,66}... | collective-permute-start | bytes 196616 | tf_op jit(solution)/shard_map/ppermute | solution.py:40
  132.4 4.1 %collective-permute-start.12 = (f32[8,2048]{1,0:T(8,128)S(1)}, f32[8,2048]{1,0:T(8,128)S(1)}, u32[]{:S(2)}, u32[]{:S(2)}) collective-permute-start(f32[8,2048]{1,0:T(8,128)S(1)} %get-tuple-element.43), channel_id=1, source_target_pairs={{0,32},{32,0},{64,96},{96,64},{1,33},{33,1},{65,97},{97,65},{2,34}... | collective-permute-start | bytes 196616 | tf_op jit(solution)/shard_map/ppermute | solution.py:40
  137.1 10.6 %all-to-all-start.2 = ((f32[16,8,128]{2,1,0:T(8,128)}), f32[16,8,128]{2,1,0:T(8,128)S(1)}, u32[]{:S(2)}, u32[]{:S(2)}) async-start(f32[16,8,128]{2,1,0:T(8,128)} %bitcast.32), calls=%async_computation.2 | async-start | bytes 131072 | tf_op jit(solution)/shard_map/all_to_all | solution.py:274
  148.5 14.9 %all-to-all-start.3 = ((f32[64,8,128]{2,1,0:T(8,128)}), f32[64,8,128]{2,1,0:T(8,128)S(1)}, u32[]{:S(2)}, u32[]{:S(2)}) async-start(f32[64,8,128]{2,1,0:T(8,128)} %broadcast_in_dim.6), calls=%async_computation.3 | async-start | bytes 524288 | tf_op jit(solution)/shard_map/all_to_all | solution.py:275
  163.4 4.8 %collective-permute-start.15 = (f32[4,16,8,128]{3,2,1,0:T(8,128)S(1)}, f32[4,16,8,128]{3,2,1,0:T(8,128)S(1)}, u32[]{:S(2)}, u32[]{:S(2)}) collective-permute-start(f32[4,16,8,128]{3,2,1,0:T(8,128)S(1)} %bitcast.102), channel_id=1, source_target_pairs={{0,1},{1,0},{2,3},{3,2},{4,5},{5,4},{6,7},{7,6},{8,9},{9,8},{10,11... | collective-permute-start | bytes 786440 | tf_op jit(solution)/shard_map/ppermute | solution.py:40
  168.8 0.8 copy-start.2
  168.9 1.7 copy-start.1
  168.9 2.2 %copy-start = (f32[1024,448]{0,1:T(8,128)S(1)}, f32[1024,448]{0,1:T(8,128)}, u32[]{:S(2)}) copy-start(f32[1024,448]{0,1:T(8,128)} %param.11) | copy-start | bytes 5505028
Sparse Core Ops, SparseCore 0:
  10.3 166.5 all-gather.1

commit v7 on v6

--- a/solution.py
+++ b/solution.py
@@ -135,43 +135,42 @@
         n = pl.program_id(0)
         slot = lax.rem(n, 2)
 
-        def copy(m, s, k):
-            piece = pl.ds(k * rows, rows)
+        def copies(m, s):
             place = pl.ds(pl.multiple_of(m * block, block), block)
-            return pltpu.make_async_copy(acts_ref.at[piece, place], held.at[s, piece], sems.at[s, k])
-
-        def close(gradient):
-            approx = jnp.dot(ortho_ref[...], basis_ref[...], preferred_element_type=jnp.float32)
-            matrix = gradient * scale + error_ref[...].astype(jnp.float32)
-            out_ref[...] = (matrix - approx).astype(jnp.bfloat16)
+            pieces = [pl.ds(k * rows, rows) for k in range(parts)]
+            return [pltpu.make_async_copy(acts_ref.at[p, place], held.at[s, p], sems.at[s, k]) for k, p in enumerate(pieces)]
+
+        def close(total):
+            out_ref[...] = (total * scale + error_ref[...].astype(jnp.float32)).astype(jnp.bfloat16)
 
         @pl.when(n == 0)
         def _():
-            for k in range(parts):
-                copy(0, 0, k).start()
+            for c in copies(0, 0):
+                c.start()
             if steps > 1:
-                for k in range(parts):
-                    copy(1, 1, k).start()
+                for c in copies(1, 1):
+                    c.start()
+            columns[:, tokens:] = ortho_ref[...]
             for s in range(shards):
                 columns[:, s * tok : (s + 1) * tok] = got_ref[s]
-            total = None
-            for k in range(parts):
-                copy(0, 0, k).wait()
+            total = jnp.dot(ortho_ref[...], basis_ref[...], preferred_element_type=jnp.float32)
+            for k, c in enumerate(copies(0, 0)):
+                c.wait()
                 piece = slice(k * rows, (k + 1) * rows)
-                d = jnp.dot(columns[:, piece], held[0, piece], preferred_element_type=jnp.float32)
-                total = d if total is None else total + d
+                total = total + jnp.dot(columns[:, piece], held[0, piece], preferred_element_type=jnp.float32)
             close(total)
 
         @pl.when(n > 0)
         def _():
-            for k in range(parts):
-                copy(n, slot, k).wait()
+            held[slot, tokens:] = basis_ref[...]
+            for c in copies(n, slot):
+                c.wait()
             close(jnp.dot(columns[...], held[slot], preferred_element_type=jnp.float32))
 
         @pl.when(n + 2 < steps)
         def _():
-            for k in range(parts):
-                copy(n + 2, slot, k).start()
+            for c in copies(n + 2, slot):
+                c.start()
 
     wide = pl.BlockSpec((cols, block), lambda n: (0, n))
     return pl.pallas_call(
@@ -187,8 +186,8 @@
         ],
         out_specs=wide,
         scratch_shapes=[
-            pltpu.VMEM((cols, tokens), got.dtype),
-            pltpu.VMEM((2, tokens, block), gathered.dtype),
+            pltpu.VMEM((cols, tokens + depth6), got.dtype),
+            pltpu.VMEM((2, tokens + depth6, block), gathered.dtype),
             pltpu.SemaphoreType.DMA((2, parts)),
         ],
         compiler_params=pltpu.CompilerParams(vmem_limit_bytes=VMEM_LIMIT),
@@ -198,14 +197,14 @@
     )(got, gathered, error_t, ortho6, basis6)
 
 
-def adam(place, ortho6, basis6, weight, moment_one, moment_two):
+def adam(place, ortho6, basis6, weight, moment_one, moment_two, scale):
     cols, rows = weight.shape
     block = min(512, rows)
     steps = rows // block
     depth6 = ortho6.shape[1]
 
     def body(p, ortho_ref, basis_ref, w_ref, one_ref, two_ref, w_out, one_out, two_out):
-        update = jnp.dot(ortho_ref[...], basis_ref[...], preferred_element_type=jnp.float32)
+        update = jnp.dot(ortho_ref[...], basis_ref[...], preferred_element_type=jnp.float32) * (-scale)
         one = beta_one * one_ref[...] + (1.0 - beta_one) * update
         two = beta_two * two_ref[...] + (1.0 - beta_two) * update * update
         root = jnp.sqrt(two * (1.0 / second_fix)) + adam_epsilon
@@ -230,7 +229,7 @@
             ],
             out_specs=[own, own, own],
         ),
-        compiler_params=pltpu.CompilerParams(vmem_limit_bytes=VMEM_LIMIT),
+        compiler_params=pltpu.CompilerParams(vmem_limit_bytes=20 * 1024 * 1024),
         cost_estimate=pl.CostEstimate(flops=2 * cols * rows * depth6, bytes_accessed=24 * cols * rows, transcendentals=cols * rows),
     )(place, ortho6, basis6, weight, moment_one, moment_two)
 
@@ -284,12 +283,13 @@
     basis_out = jnp.dot(inverse, terms, precision=highest)
 
     oh, om, ol = split3(ortho)
-    bh, bm, bl = split3(basis_out)
-    ortho6 = jnp.concatenate([oh, oh, om, oh, ol, om], 0).T
-    basis6 = jnp.concatenate([bh, bm, bh, bl, bh, bm], 0)
+    bh, bm, bl = split3(basis_out * (-1.0 / scale))
+    zero = jnp.zeros_like(bh)
+    ortho6 = jnp.concatenate([oh, oh, om, oh, ol, om, jnp.zeros_like(oh), jnp.zeros_like(oh)], 0).T
+    basis6 = jnp.concatenate([bh, bm, bh, bl, bh, bm, zero, zero], 0)
 
     place = lax.axis_index("outer").astype(jnp.int32).reshape(1)
-    state = adam(place, ortho6, basis6, weight.T, moment_one.T, moment_two.T)
+    state = adam(place, ortho6, basis6, weight.T, moment_one.T, moment_two.T, scale)
     error_out = finish_error(got, gathered, error_t, ortho6, basis6, scale)
     return (basis_out, error_out.T[None], state[0].T, state[1].T, state[2].T)
 

time: 207 us -> 207 us (level)
  no operation moved by 1% of the time
where the time goes in v7:
time: 207 us; the launch traced here: 206 us
  waiting for transfers between devices  82.7 us (40%)
  starting transfers between devices  47.7 us (23%)
  Pallas kernels  28.5 us (14%)
  between operations  14.5 us (7%)
  matrix products  11.1 us (5%)
  other arithmetic  10.9 us (5%)
  local copies, waits for them, and re-layouts  10.6 us (5%)
    ppermute x16, waiting for transfers between devices, swap(): lax.ppermute(x, axis, [(i, i ^ k) for i in range(lax.axis_size(axis))])  60.7 us
    ppermute x16, starting transfers between devices, swap(): lax.ppermute(x, axis, [(i, i ^ k) for i in range(lax.axis_size(axis))])  22.6 us
    pallas_call x1, Pallas kernels, finish_error(): pl.pallas_call(body, out_shape=jax.ShapeDtypeStruct(error_t.shape, jnp.bf...  22.2 us
    dot_general x5, matrix products, dot(): lax.dot_general(a, b, (((ca,), (cb,)), ((), ())), preferred_element_type=...  10.1 us
    all_to_all x1, waiting for transfers between devices, per_device(): lax.all_to_all(keep + twin(send), ('z', 'y'), 0, 0, tiled=True).sum(0)  10.1 us
    all_to_all x1, starting transfers between devices, per_device(): got = lax.all_to_all(grads_t, SHARD, 0, 0)  9.23 us
    all_to_all x1, starting transfers between devices, per_device(): lax.all_to_all(keep + twin(send), ('z', 'y'), 0, 0, tiled=True).sum(0)  6.75 us
    transpose x1, local copies, waits for them, and re-layouts, per_device(): grads.T.reshape(shards, cols, tok)  6.04 us
  transfers between devices with their start and end apart: 21, of which 16 were waited for; matrix products, arithmetic and copies ran while one was open for 15% of the time, Pallas kernels for 3%

profile of v7, /device:TPU:1, one launch (start us, length us, event | category | flops | bytes accessed | tf_op | source)
XLA Modules:
  0.0 205.9 jit_solution(13226564655312417286)
XLA Ops:
  7.2 0.7 all-gather.2.cloned.1.call-update
  7.9 1.2 reduce-precision_convert_fusion.5
  9.6 3.8 %collective-permute-start.1 = (f32[32,128]{1,0:T(8,128)S(1)}, f32[32,128]{1,0:T(8,128)S(1)}, u32[]{:S(2)}, u32[]{:S(2)}) collective-permute-start(f32[32,128]{1,0:T(8,128)S(1)} %fusion.35), channel_id=1, source_target_pairs={{0,4},{2,6},{4,0},{6,2},{1,5},{3,7},{5,1},{7,3},{8,12},{10,14},{12... | collective-permute-start | bytes 49160 | tf_op jit(solution)/shard_map/ppermute | solution.py:40
  14.2 6.0 %copy.40 = bf16[14336,128]{1,0:T(8,128)(2,1)} copy(bf16[14336,128]{0,1:T(8,128)(2,1)} %bitcast.99) | data formatting | bytes 7340032 | tf_op jit(solution)/shard_map/transpose | solution.py:251
  20.3 9.2 %all-to-all-start = ((bf16[32,448,128]{2,1,0:T(8,128)(2,1)}), bf16[32,448,128]{2,1,0:T(8,128)(2,1)}, u32[]{:S(2)}, u32[]{:S(2)}) async-start(bf16[32,448,128]{2,1,0:T(8,128)(2,1)} %bitcast.98), calls=%async_computation | async-start | bytes 7340032 | tf_op jit(solution)/shard_map/all_to_all | solution.py:252
  29.5 3.3 %fusion.5 = f32[96,448]{1,0:T(8,128)S(1)} fusion(bf16[1,4096,448]{1,2,0:T(8,128)(2,1)} %param.10, bf16[32,4096]{1,0:T(8,128)(2,1)S(1)} %get-tuple-element.37, bf16[32,4096]{1,0:T(8,128)(2,1)S(1)} %get-tuple-element.38, bf16[32,4096]{1,0:T(8,128)(2,1)S(1)} %get-tuple-element.36), kind=kOutput, calls=%fused_computation.5 | convolution fusion | flops 354680832 | bytes 4628480 | tf_op jit(solution)/shard_map/dot_general | solution.py:30
  32.8 2.7 %collective-permute-start.5 = (f32[4,32,128]{2,1,0:T(8,128)S(1)}, f32[4,32,128]{2,1,0:T(8,128)S(1)}, u32[]{:S(2)}, u32[]{:S(2)}) collective-permute-start(f32[4,32,128]{2,1,0:T(8,128)S(1)} %bitcast.110), channel_id=1, source_target_pairs={{0,24},{8,16},{16,8},{24,0},{1,25},{9,17},{17,9},{25,1},{2,26},{10... | collective-permute-start | bytes 196616 | tf_op jit(solution)/shard_map/ppermute | solution.py:40
  36.3 26.5 %collective-permute-done.5 = f32[4,32,128]{2,1,0:T(8,128)S(1)} collective-permute-done((f32[4,32,128]{2,1,0:T(8,128)S(1)}, f32[4,32,128]{2,1,0:T(8,128)S(1)}, u32[]{:S(2)}, u32[]{:S(2)}) %collective-permute-start.5) | collective-permute-done | bytes 65568 | tf_op jit(solution)/shard_map/ppermute | solution.py:40
  62.7 20.8 %collective-permute-done.4 = f32[4,32,128]{2,1,0:T(8,128)S(1)} collective-permute-done((f32[4,32,128]{2,1,0:T(8,128)S(1)}, f32[4,32,128]{2,1,0:T(8,128)S(1)}, u32[]{:S(2)}, u32[]{:S(2)}) %collective-permute-start.4) | collective-permute-done | bytes 65568 | tf_op jit(solution)/shard_map/ppermute | solution.py:40
  83.5 3.1 %collective-permute-done.3 = f32[4,32,128]{2,1,0:T(8,128)S(1)} collective-permute-done((f32[4,32,128]{2,1,0:T(8,128)S(1)}, f32[4,32,128]{2,1,0:T(8,128)S(1)}, u32[]{:S(2)}, u32[]{:S(2)}) %collective-permute-start.3) | collective-permute-done | bytes 65568 | tf_op jit(solution)/shard_map/ppermute | solution.py:40
  87.5 1.2 collective-permute-done.6
  89.7 3.2 %fusion = f32[96,448]{1,0:T(8,128)S(1)} fusion(bf16[32,4096]{1,0:T(8,128)(2,1)S(1)} %get-tuple-element.32, bf16[32,4096]{1,0:T(8,128)(2,1)S(1)} %get-tuple-element.33, bf16[32,4096]{1,0:T(8,128)(2,1)S(1)} %get-tuple-element.31, bf16[32,448,128]{2,1,0:T(8,128)(2,1)} %all-to-all-done.g_ref.got_ref), kind=kOutput, calls=%fused_computation | convolution fusion | flops 354680832 | bytes 4628480 | tf_op jit(solution)/shard_map/dot_general | solution.py:30
  93.0 2.5 %collective-permute-start.9 = (f32[32,448]{1,0:T(8,128)S(1)}, f32[32,448]{1,0:T(8,128)S(1)}, u32[]{:S(2)}, u32[]{:S(2)}) collective-permute-start(f32[32,448]{1,0:T(8,128)S(1)} %fusion.25), channel_id=1, source_target_pairs={{0,96},{32,64},{64,32},{96,0},{1,97},{33,65},{65,33},{97,1},{2,98}... | collective-permute-start | bytes 172040 | tf_op jit(solution)/shard_map/ppermute | solution.py:40
  95.4 0.6 collective-permute-start.8
  96.3 1.1 collective-permute-done.9
  97.4 2.7 %collective-permute-done.8 = f32[32,448]{1,0:T(8,128)S(1)} collective-permute-done((f32[32,448]{1,0:T(8,128)S(1)}, f32[32,448]{1,0:T(8,128)S(1)}, u32[]{:S(2)}, u32[]{:S(2)}) %collective-permute-start.8) | collective-permute-done | bytes 57376 | tf_op jit(solution)/shard_map/ppermute | solution.py:40
  100.2 2.6 %shard_map.110 = (f32[16,40,128]{2,1,0:T(8,128)S(1)}, f32[16,40,128]{2,1,0:T(8,128)S(1)}) custom-call(s32[1]{0:T(128)} %bitcast.c, f32[32,448]{1,0:T(8,128)S(1)} %get-tuple-element.28.f_ref, bf16[96,448]{1,0:T(8,128)(2,1)S(1)} %pad_maximum_fusion.4.f3_ref, bf16[32,448,128]{2,1,0:T(8,128)(2,1)} %all-to-all-done.g_ref.got_ref), custom_call_target="tpu_custom_call" | custom-call | flops 352321536 | bytes 3670016 | tf_op jit(solution)/shard_map/pallas_call | solution.py:106
  102.9 2.1 %collective-permute-start.10 = (f32[16,40,128]{2,1,0:T(8,128)S(1)}, f32[16,40,128]{2,1,0:T(8,128)S(1)}, u32[]{:S(2)}, u32[]{:S(2)}) collective-permute-start(f32[16,40,128]{2,1,0:T(8,128)S(1)} %get-tuple-element.21), channel_id=1, source_target_pairs={{0,1},{1,0},{2,3},{3,2},{4,5},{5,4},{6,7},{7,6},{8,9},{9,8},{10,11... | collective-permute-start | bytes 983048 | tf_op jit(solution)/shard_map/ppermute | solution.py:40
  105.0 1.3 collective-permute-done.10
  106.2 0.8 add.101
  107.0 6.7 %all-to-all-start.1 = ((f32[16,40,128]{2,1,0:T(8,128)}), f32[16,40,128]{2,1,0:T(8,128)S(1)}, u32[]{:S(2)}, u32[]{:S(2)}) async-start(f32[16,40,128]{2,1,0:T(8,128)} %add.101), calls=%async_computation.1 | async-start | bytes 655360 | tf_op jit(solution)/shard_map/all_to_all | solution.py:263
  113.7 2.8 %fusion.3 = f32[96,4096]{1,0:T(8,128)S(1)} fusion(bf16[1,4096,448]{1,2,0:T(8,128)(2,1)} %param.10, bf16[32,448]{1,0:T(8,128)(2,1)S(1)} %get-tuple-element.46, bf16[32,448]{1,0:T(8,128)(2,1)S(1)} %get-tuple-element.45, bf16[32,448]{1,0:T(8,128)(2,1)S(1)} %get-tuple-element.27), kind=kOutput, calls=%fused_computation.3 | convolution fusion | flops 352579584 | bytes 5328896 | tf_op jit(solution)/shard_map/dot_general | solution.py:30
  116.5 10.1 %all-to-all-done.1 = f32[16,40,128]{2,1,0:T(8,128)S(1)} async-done(((f32[16,40,128]{2,1,0:T(8,128)}), f32[16,40,128]{2,1,0:T(8,128)S(1)}, u32[]{:S(2)}, u32[]{:S(2)}) %all-to-all-start.1) | async-done | bytes 327712 | tf_op jit(solution)/shard_map/all_to_all | solution.py:263
  127.2 1.6 collective-permute-start.11
  129.3 0.8 collective-permute-done.11
  130.1 1.1 collective-permute-start.14
  131.2 1.2 collective-permute-start.13
  132.4 1.0 collective-permute-start.12
  133.5 1.4 collective-permute-done.14
  134.9 1.0 collective-permute-done.13
  136.5 0.6 fusion.26
  137.1 3.5 %all-to-all-start.2 = ((f32[16,8,128]{2,1,0:T(8,128)}), f32[16,8,128]{2,1,0:T(8,128)S(1)}, u32[]{:S(2)}, u32[]{:S(2)}) async-start(f32[16,8,128]{2,1,0:T(8,128)} %bitcast.32), calls=%async_computation.2 | async-start | bytes 131072 | tf_op jit(solution)/shard_map/all_to_all | solution.py:273
  140.7 2.9 %cholesky.17 = f32[32,32]{1,0:T(8,128)S(1)} custom-call(f32[32,32]{1,0:T(8,128)S(1)} %fusion.38), custom_call_target="Cholesky" | custom-call | tf_op jit(solution)/shard_map/jit(cholesky)/cholesky | solution.py:280
  143.7 0.6 compare_reduce_fusion
  144.3 3.5 %all-to-all-done.2 = f32[16,8,128]{2,1,0:T(8,128)S(1)} async-done(((f32[16,8,128]{2,1,0:T(8,128)}), f32[16,8,128]{2,1,0:T(8,128)S(1)}, u32[]{:S(2)}, u32[]{:S(2)}) %all-to-all-start.2) | async-done | bytes 65568 | tf_op jit(solution)/shard_map/all_to_all | solution.py:273
  147.8 0.7 broadcast_in_dim.6
  148.5 5.5 %all-to-all-start.3 = ((f32[64,8,128]{2,1,0:T(8,128)}), f32[64,8,128]{2,1,0:T(8,128)S(1)}, u32[]{:S(2)}, u32[]{:S(2)}) async-start(f32[64,8,128]{2,1,0:T(8,128)} %broadcast_in_dim.6), calls=%async_computation.3 | async-start | bytes 524288 | tf_op jit(solution)/shard_map/all_to_all | solution.py:274
  154.1 0.7 fusion.33
  154.7 2.4 %custom-call.7 = f32[1,32,32]{1,2,0:T(8,128)S(1)} custom-call(f32[1,32,32]{2,1,0:T(8,128)S(1)} %fusion.33), custom_call_target="InvertDiagBlocksLowerTriangular" | custom-call | tf_op jit(solution)/shard_map/jit(_solve_triangular)/triangular_solve | solution.py:281
  157.4 6.0 %all-to-all-done.3 = f32[64,8,128]{2,1,0:T(8,128)S(1)} async-done(((f32[64,8,128]{2,1,0:T(8,128)}), f32[64,8,128]{2,1,0:T(8,128)S(1)}, u32[]{:S(2)}, u32[]{:S(2)}) %all-to-all-start.3) | async-done | bytes 262176 | tf_op jit(solution)/shard_map/all_to_all | solution.py:274
  163.4 3.7 %collective-permute-start.15 = (f32[4,16,8,128]{3,2,1,0:T(8,128)S(1)}, f32[4,16,8,128]{3,2,1,0:T(8,128)S(1)}, u32[]{:S(2)}, u32[]{:S(2)}) collective-permute-start(f32[4,16,8,128]{3,2,1,0:T(8,128)S(1)} %bitcast.102), channel_id=1, source_target_pairs={{0,1},{1,0},{2,3},{3,2},{4,5},{5,4},{6,7},{7,6},{8,9},{9,8},{10,11... | collective-permute-start | bytes 786440 | tf_op jit(solution)/shard_map/ppermute | solution.py:40
  168.3 0.6 constant_dynamic-update-slice_fusion.4
  169.7 0.6 copy-done.2
  170.3 0.6 copy-done
  170.8 0.6 copy-done.1
  171.4 3.7 %shard_map.112 = (f32[448,1024]{1,0:T(8,128)}, f32[448,1024]{1,0:T(8,128)}, f32[448,1024]{1,0:T(8,128)}) custom-call(s32[1]{0:T(128)} %bitcast.40.p, bf16[448,256]{1,0:T(8,128)(2,1)S(1)} %bitcast.96, bf16[256,4096]{1,0:T(8,128)(2,1)S(1)} %broadcast_dynamic-update-slice_fusion.basis_ref, f32[448,1024]{1,0:T(8,128)S(1)} %bitcast.93, f32[448,1024]{1,0:T(8,128)S(1)} %bitcast.94, ...), custom_call_target="tpu_custom_call" | custom-call | flops 234881024 | bytes 11010048 | tf_op jit(solution)/shard_map/pallas_call | solution.py:217
  175.1 1.8 all-gather.2.cloned.1.call-done.acts_ref
  176.9 22.2 %shard_map.111 = bf16[448,4096]{1,0:T(8,128)(2,1)} custom-call(bf16[32,448,128]{2,1,0:T(8,128)(2,1)} %all-to-all-done.g_ref.got_ref, bf16[4096,4096]{1,0:T(8,128)(2,1)} %all-gather.2.cloned.1.call-done.acts_ref, bf16[448,4096]{1,0:T(8,128)(2,1)} %bitcast.100, bf16[448,256]{1,0:T(8,128)(2,1)S(1)} %bitcast.97, ...), custom_call_target="tpu_custom_call" | custom-call | flops 15971909632 | bytes 44564480 | tf_op jit(solution)/shard_map/pallas_call | solution.py:176
  (72 shorter events, 8.2 us)
Async XLA Ops:
  7.2 1.9 copy-start.4
  7.2 169.7 %all-gather.2.cloned.1.call-start = ((), (), s32[]{:S(2)}) async-start(), calls=%async_computation.4 | async-start | bytes 34603008 | tf_op jit(solution)/shard_map/all_gather | solution.py:248
  9.6 10.7 %collective-permute-start.1 = (f32[32,128]{1,0:T(8,128)S(1)}, f32[32,128]{1,0:T(8,128)S(1)}, u32[]{:S(2)}, u32[]{:S(2)}) collective-permute-start(f32[32,128]{1,0:T(8,128)S(1)} %fusion.35), channel_id=1, source_target_pairs={{0,4},{2,6},{4,0},{6,2},{1,5},{3,7},{5,1},{7,3},{8,12},{10,14},{12... | collective-permute-start | bytes 49160 | tf_op jit(solution)/shard_map/ppermute | solution.py:40
  13.4 6.8 %collective-permute-start = (f32[32,128]{1,0:T(8,128)S(1)}, f32[32,128]{1,0:T(8,128)S(1)}, u32[]{:S(2)}, u32[]{:S(2)}) collective-permute-start(f32[32,128]{1,0:T(8,128)S(1)} %fusion.35), channel_id=1, source_target_pairs={{0,2},{2,0},{4,6},{6,4},{1,3},{3,1},{5,7},{7,5},{8,10},{10,8},{12,... | collective-permute-start | bytes 49160 | tf_op jit(solution)/shard_map/ppermute | solution.py:40
  13.8 6.4 %collective-permute-start.2 = (f32[32,128]{1,0:T(8,128)S(1)}, f32[32,128]{1,0:T(8,128)S(1)}, u32[]{:S(2)}, u32[]{:S(2)}) collective-permute-start(f32[32,128]{1,0:T(8,128)S(1)} %fusion.35), channel_id=1, source_target_pairs={{0,6},{2,4},{4,2},{6,0},{1,7},{3,5},{5,3},{7,1},{8,14},{10,12},{12... | collective-permute-start | bytes 49160 | tf_op jit(solution)/shard_map/ppermute | solution.py:40
  20.3 69.4 %all-to-all-start = ((bf16[32,448,128]{2,1,0:T(8,128)(2,1)}), bf16[32,448,128]{2,1,0:T(8,128)(2,1)}, u32[]{:S(2)}, u32[]{:S(2)}) async-start(bf16[32,448,128]{2,1,0:T(8,128)(2,1)} %bitcast.98), calls=%async_computation | async-start | bytes 7340032 | tf_op jit(solution)/shard_map/all_to_all | solution.py:252
  32.8 29.9 %collective-permute-start.5 = (f32[4,32,128]{2,1,0:T(8,128)S(1)}, f32[4,32,128]{2,1,0:T(8,128)S(1)}, u32[]{:S(2)}, u32[]{:S(2)}) collective-permute-start(f32[4,32,128]{2,1,0:T(8,128)S(1)} %bitcast.110), channel_id=1, source_target_pairs={{0,24},{8,16},{16,8},{24,0},{1,25},{9,17},{17,9},{25,1},{2,26},{10... | collective-permute-start | bytes 196616 | tf_op jit(solution)/shard_map/ppermute | solution.py:40
  35.6 47.9 %collective-permute-start.4 = (f32[4,32,128]{2,1,0:T(8,128)S(1)}, f32[4,32,128]{2,1,0:T(8,128)S(1)}, u32[]{:S(2)}, u32[]{:S(2)}) collective-permute-start(f32[4,32,128]{2,1,0:T(8,128)S(1)} %bitcast.111), channel_id=1, source_target_pairs={{0,16},{8,24},{16,0},{24,8},{1,17},{9,25},{17,1},{25,9},{2,18},{10... | collective-permute-start | bytes 196616 | tf_op jit(solution)/shard_map/ppermute | solution.py:40
  36.1 50.5 %collective-permute-start.3 = (f32[4,32,128]{2,1,0:T(8,128)S(1)}, f32[4,32,128]{2,1,0:T(8,128)S(1)}, u32[]{:S(2)}, u32[]{:S(2)}) collective-permute-start(f32[4,32,128]{2,1,0:T(8,128)S(1)} %bitcast.112), channel_id=1, source_target_pairs={{0,8},{8,0},{16,24},{24,16},{1,9},{9,1},{17,25},{25,17},{2,10},{10... | collective-permute-start | bytes 196616 | tf_op jit(solution)/shard_map/ppermute | solution.py:40
  86.9 1.7 collective-permute-start.6
  93.0 4.4 %collective-permute-start.9 = (f32[32,448]{1,0:T(8,128)S(1)}, f32[32,448]{1,0:T(8,128)S(1)}, u32[]{:S(2)}, u32[]{:S(2)}) collective-permute-start(f32[32,448]{1,0:T(8,128)S(1)} %fusion.25), channel_id=1, source_target_pairs={{0,96},{32,64},{64,32},{96,0},{1,97},{33,65},{65,33},{97,1},{2,98}... | collective-permute-start | bytes 172040 | tf_op jit(solution)/shard_map/ppermute | solution.py:40
  95.4 4.7 %collective-permute-start.8 = (f32[32,448]{1,0:T(8,128)S(1)}, f32[32,448]{1,0:T(8,128)S(1)}, u32[]{:S(2)}, u32[]{:S(2)}) collective-permute-start(f32[32,448]{1,0:T(8,128)S(1)} %fusion.25), channel_id=1, source_target_pairs={{0,64},{32,96},{64,0},{96,32},{1,65},{33,97},{65,1},{97,33},{2,66}... | collective-permute-start | bytes 172040 | tf_op jit(solution)/shard_map/ppermute | solution.py:40
  96.0 4.1 %collective-permute-start.7 = (f32[32,448]{1,0:T(8,128)S(1)}, f32[32,448]{1,0:T(8,128)S(1)}, u32[]{:S(2)}, u32[]{:S(2)}) collective-permute-start(f32[32,448]{1,0:T(8,128)S(1)} %fusion.25), channel_id=1, source_target_pairs={{0,32},{32,0},{64,96},{96,64},{1,33},{33,1},{65,97},{97,65},{2,34}... | collective-permute-start | bytes 172040 | tf_op jit(solution)/shard_map/ppermute | solution.py:40
  102.9 3.3 %collective-permute-start.10 = (f32[16,40,128]{2,1,0:T(8,128)S(1)}, f32[16,40,128]{2,1,0:T(8,128)S(1)}, u32[]{:S(2)}, u32[]{:S(2)}) collective-permute-start(f32[16,40,128]{2,1,0:T(8,128)S(1)} %get-tuple-element.21), channel_id=1, source_target_pairs={{0,1},{1,0},{2,3},{3,2},{4,5},{5,4},{6,7},{7,6},{8,9},{9,8},{10,11... | collective-permute-start | bytes 983048 | tf_op jit(solution)/shard_map/ppermute | solution.py:40
  107.0 19.6 %all-to-all-start.1 = ((f32[16,40,128]{2,1,0:T(8,128)}), f32[16,40,128]{2,1,0:T(8,128)S(1)}, u32[]{:S(2)}, u32[]{:S(2)}) async-start(f32[16,40,128]{2,1,0:T(8,128)} %add.101), calls=%async_computation.1 | async-start | bytes 655360 | tf_op jit(solution)/shard_map/all_to_all | solution.py:263
  127.2 2.8 %collective-permute-start.11 = (f32[32,2048]{1,0:T(8,128)S(1)}, f32[32,2048]{1,0:T(8,128)S(1)}, u32[]{:S(2)}, u32[]{:S(2)}) collective-permute-start(f32[32,2048]{1,0:T(8,128)S(1)} %constant_dynamic-slice_fusion), channel_id=1, source_target_pairs={{0,1},{1,0},{2,3},{3,2},{4,5},{5,4},{6,7},{7,6},{8,9},{9,8},{10,11... | collective-permute-start | bytes 786440 | tf_op jit(solution)/shard_map/ppermute | solution.py:40
  130.1 4.8 %collective-permute-start.14 = (f32[8,2048]{1,0:T(8,128)S(1)}, f32[8,2048]{1,0:T(8,128)S(1)}, u32[]{:S(2)}, u32[]{:S(2)}) collective-permute-start(f32[8,2048]{1,0:T(8,128)S(1)} %get-tuple-element.41), channel_id=1, source_target_pairs={{0,96},{32,64},{64,32},{96,0},{1,97},{33,65},{65,33},{97,1},{2,98}... | collective-permute-start | bytes 196616 | tf_op jit(solution)/shard_map/ppermute | solution.py:40
  131.2 4.7 %collective-permute-start.13 = (f32[8,2048]{1,0:T(8,128)S(1)}, f32[8,2048]{1,0:T(8,128)S(1)}, u32[]{:S(2)}, u32[]{:S(2)}) collective-permute-start(f32[8,2048]{1,0:T(8,128)S(1)} %get-tuple-element.42), channel_id=1, source_target_pairs={{0,64},{32,96},{64,0},{96,32},{1,65},{33,97},{65,1},{97,33},{2,66}... | collective-permute-start | bytes 196616 | tf_op jit(solution)/shard_map/ppermute | solution.py:40
  132.4 4.1 %collective-permute-start.12 = (f32[8,2048]{1,0:T(8,128)S(1)}, f32[8,2048]{1,0:T(8,128)S(1)}, u32[]{:S(2)}, u32[]{:S(2)}) collective-permute-start(f32[8,2048]{1,0:T(8,128)S(1)} %get-tuple-element.43), channel_id=1, source_target_pairs={{0,32},{32,0},{64,96},{96,64},{1,33},{33,1},{65,97},{97,65},{2,34}... | collective-permute-start | bytes 196616 | tf_op jit(solution)/shard_map/ppermute | solution.py:40
  137.1 10.6 %all-to-all-start.2 = ((f32[16,8,128]{2,1,0:T(8,128)}), f32[16,8,128]{2,1,0:T(8,128)S(1)}, u32[]{:S(2)}, u32[]{:S(2)}) async-start(f32[16,8,128]{2,1,0:T(8,128)} %bitcast.32), calls=%async_computation.2 | async-start | bytes 131072 | tf_op jit(solution)/shard_map/all_to_all | solution.py:273
  148.5 14.9 %all-to-all-start.3 = ((f32[64,8,128]{2,1,0:T(8,128)}), f32[64,8,128]{2,1,0:T(8,128)S(1)}, u32[]{:S(2)}, u32[]{:S(2)}) async-start(f32[64,8,128]{2,1,0:T(8,128)} %broadcast_in_dim.6), calls=%async_computation.3 | async-start | bytes 524288 | tf_op jit(solution)/shard_map/all_to_all | solution.py:274
  163.4 4.8 %collective-permute-start.15 = (f32[4,16,8,128]{3,2,1,0:T(8,128)S(1)}, f32[4,16,8,128]{3,2,1,0:T(8,128)S(1)}, u32[]{:S(2)}, u32[]{:S(2)}) collective-permute-start(f32[4,16,8,128]{3,2,1,0:T(8,128)S(1)} %bitcast.102), channel_id=1, source_target_pairs={{0,1},{1,0},{2,3},{3,2},{4,5},{5,4},{6,7},{7,6},{8,9},{9,8},{10,11... | collective-permute-start | bytes 786440 | tf_op jit(solution)/shard_map/ppermute | solution.py:40
  168.3 2.0 copy-start.2
  168.9 0.8 copy-start.3
  168.9 2.0 copy-start
  168.9 2.5 %copy-start.1 = (f32[1024,448]{0,1:T(8,128)S(1)}, f32[1024,448]{0,1:T(8,128)}, u32[]{:S(2)}) copy-start(f32[1024,448]{0,1:T(8,128)} %param.12) | copy-start | bytes 5505028
Sparse Core Ops, SparseCore 0:
  10.3 166.5 all-gather.1

commit v8 on v6

--- a/solution.py
+++ b/solution.py
@@ -230,7 +230,7 @@
             ],
             out_specs=[own, own, own],
         ),
-        compiler_params=pltpu.CompilerParams(vmem_limit_bytes=VMEM_LIMIT),
+        compiler_params=pltpu.CompilerParams(vmem_limit_bytes=20 * 1024 * 1024),
         cost_estimate=pl.CostEstimate(flops=2 * cols * rows * depth6, bytes_accessed=24 * cols * rows, transcendentals=cols * rows),
     )(place, ortho6, basis6, weight, moment_one, moment_two)
 

time: 207 us -> 207 us (level)
  no operation moved by 1% of the time
where the time goes in v8:
time: 207 us; the launch traced here: 206 us
  waiting for transfers between devices  82.9 us (40%)
  starting transfers between devices  47.7 us (23%)
  Pallas kernels  28.8 us (14%)
  between operations  14.4 us (7%)
  matrix products  11.1 us (5%)
  other arithmetic  10.8 us (5%)
  local copies, waits for them, and re-layouts  10.6 us (5%)
    ppermute x16, waiting for transfers between devices, swap(): lax.ppermute(x, axis, [(i, i ^ k) for i in range(lax.axis_size(axis))])  60.8 us
    ppermute x16, starting transfers between devices, swap(): lax.ppermute(x, axis, [(i, i ^ k) for i in range(lax.axis_size(axis))])  22.6 us
    pallas_call x1, Pallas kernels, finish_error(): pl.pallas_call(body, out_shape=jax.ShapeDtypeStruct(error_t.shape, jnp.bf...  22.5 us
    dot_general x5, matrix products, dot(): lax.dot_general(a, b, (((ca,), (cb,)), ((), ())), preferred_element_type=...  10.1 us
    all_to_all x1, waiting for transfers between devices, per_device(): lax.all_to_all(keep + twin(send), ('z', 'y'), 0, 0, tiled=True).sum(0)  10.1 us
    all_to_all x1, starting transfers between devices, per_device(): got = lax.all_to_all(grads_t, SHARD, 0, 0)  9.23 us
    all_to_all x1, starting transfers between devices, per_device(): lax.all_to_all(keep + twin(send), ('z', 'y'), 0, 0, tiled=True).sum(0)  6.75 us
    transpose x1, local copies, waits for them, and re-layouts, per_device(): grads.T.reshape(shards, cols, tok)  6.04 us
  transfers between devices with their start and end apart: 21, of which 16 were waited for; matrix products, arithmetic and copies ran while one was open for 15% of the time, Pallas kernels for 3%

profile of v8, /device:TPU:1, one launch (start us, length us, event | category | flops | bytes accessed | tf_op | source)
XLA Modules:
  0.0 206.2 jit_solution(2884617488645268227)
XLA Ops:
  7.2 0.7 all-gather.2.cloned.1.call-update
  7.9 1.2 reduce-precision_convert_fusion.5
  9.6 3.8 %collective-permute-start.1 = (f32[32,128]{1,0:T(8,128)S(1)}, f32[32,128]{1,0:T(8,128)S(1)}, u32[]{:S(2)}, u32[]{:S(2)}) collective-permute-start(f32[32,128]{1,0:T(8,128)S(1)} %fusion.37), channel_id=1, source_target_pairs={{0,4},{2,6},{4,0},{6,2},{1,5},{3,7},{5,1},{7,3},{8,12},{10,14},{12... | collective-permute-start | bytes 49160 | tf_op jit(solution)/shard_map/ppermute | solution.py:40
  14.2 6.0 %copy.40 = bf16[14336,128]{1,0:T(8,128)(2,1)} copy(bf16[14336,128]{0,1:T(8,128)(2,1)} %bitcast.99) | data formatting | bytes 7340032 | tf_op jit(solution)/shard_map/transpose | solution.py:252
  20.3 9.2 %all-to-all-start = ((bf16[32,448,128]{2,1,0:T(8,128)(2,1)}), bf16[32,448,128]{2,1,0:T(8,128)(2,1)}, u32[]{:S(2)}, u32[]{:S(2)}) async-start(bf16[32,448,128]{2,1,0:T(8,128)(2,1)} %bitcast.98), calls=%async_computation | async-start | bytes 7340032 | tf_op jit(solution)/shard_map/all_to_all | solution.py:253
  29.5 3.3 %fusion.5 = f32[96,448]{1,0:T(8,128)S(1)} fusion(bf16[1,4096,448]{1,2,0:T(8,128)(2,1)} %param.10, bf16[32,4096]{1,0:T(8,128)(2,1)S(1)} %get-tuple-element.37, bf16[32,4096]{1,0:T(8,128)(2,1)S(1)} %get-tuple-element.38, bf16[32,4096]{1,0:T(8,128)(2,1)S(1)} %get-tuple-element.36), kind=kOutput, calls=%fused_computation.5 | convolution fusion | flops 354680832 | bytes 4628480 | tf_op jit(solution)/shard_map/dot_general | solution.py:30
  32.8 2.7 %collective-permute-start.5 = (f32[4,32,128]{2,1,0:T(8,128)S(1)}, f32[4,32,128]{2,1,0:T(8,128)S(1)}, u32[]{:S(2)}, u32[]{:S(2)}) collective-permute-start(f32[4,32,128]{2,1,0:T(8,128)S(1)} %bitcast.110), channel_id=1, source_target_pairs={{0,24},{8,16},{16,8},{24,0},{1,25},{9,17},{17,9},{25,1},{2,26},{10... | collective-permute-start | bytes 196616 | tf_op jit(solution)/shard_map/ppermute | solution.py:40
  36.3 26.5 %collective-permute-done.5 = f32[4,32,128]{2,1,0:T(8,128)S(1)} collective-permute-done((f32[4,32,128]{2,1,0:T(8,128)S(1)}, f32[4,32,128]{2,1,0:T(8,128)S(1)}, u32[]{:S(2)}, u32[]{:S(2)}) %collective-permute-start.5) | collective-permute-done | bytes 65568 | tf_op jit(solution)/shard_map/ppermute | solution.py:40
  62.7 20.8 %collective-permute-done.4 = f32[4,32,128]{2,1,0:T(8,128)S(1)} collective-permute-done((f32[4,32,128]{2,1,0:T(8,128)S(1)}, f32[4,32,128]{2,1,0:T(8,128)S(1)}, u32[]{:S(2)}, u32[]{:S(2)}) %collective-permute-start.4) | collective-permute-done | bytes 65568 | tf_op jit(solution)/shard_map/ppermute | solution.py:40
  83.5 3.1 %collective-permute-done.3 = f32[4,32,128]{2,1,0:T(8,128)S(1)} collective-permute-done((f32[4,32,128]{2,1,0:T(8,128)S(1)}, f32[4,32,128]{2,1,0:T(8,128)S(1)}, u32[]{:S(2)}, u32[]{:S(2)}) %collective-permute-start.3) | collective-permute-done | bytes 65568 | tf_op jit(solution)/shard_map/ppermute | solution.py:40
  86.9 0.6 collective-permute-start.6
  87.5 1.2 collective-permute-done.6
  89.7 3.2 %fusion = f32[96,448]{1,0:T(8,128)S(1)} fusion(bf16[32,4096]{1,0:T(8,128)(2,1)S(1)} %get-tuple-element.32, bf16[32,4096]{1,0:T(8,128)(2,1)S(1)} %get-tuple-element.33, bf16[32,4096]{1,0:T(8,128)(2,1)S(1)} %get-tuple-element.31, bf16[32,448,128]{2,1,0:T(8,128)(2,1)} %all-to-all-done.g_ref.got_ref), kind=kOutput, calls=%fused_computation | convolution fusion | flops 354680832 | bytes 4628480 | tf_op jit(solution)/shard_map/dot_general | solution.py:30
  93.0 2.5 %collective-permute-start.9 = (f32[32,448]{1,0:T(8,128)S(1)}, f32[32,448]{1,0:T(8,128)S(1)}, u32[]{:S(2)}, u32[]{:S(2)}) collective-permute-start(f32[32,448]{1,0:T(8,128)S(1)} %fusion.25), channel_id=1, source_target_pairs={{0,96},{32,64},{64,32},{96,0},{1,97},{33,65},{65,33},{97,1},{2,98}... | collective-permute-start | bytes 172040 | tf_op jit(solution)/shard_map/ppermute | solution.py:40
  95.4 0.6 collective-permute-start.8
  96.3 1.1 collective-permute-done.9
  97.4 2.7 %collective-permute-done.8 = f32[32,448]{1,0:T(8,128)S(1)} collective-permute-done((f32[32,448]{1,0:T(8,128)S(1)}, f32[32,448]{1,0:T(8,128)S(1)}, u32[]{:S(2)}, u32[]{:S(2)}) %collective-permute-start.8) | collective-permute-done | bytes 57376 | tf_op jit(solution)/shard_map/ppermute | solution.py:40
  100.2 2.6 %shard_map.110 = (f32[16,40,128]{2,1,0:T(8,128)S(1)}, f32[16,40,128]{2,1,0:T(8,128)S(1)}) custom-call(s32[1]{0:T(128)} %bitcast.c, f32[32,448]{1,0:T(8,128)S(1)} %get-tuple-element.28.f_ref, bf16[96,448]{1,0:T(8,128)(2,1)S(1)} %pad_maximum_fusion.4.f3_ref, bf16[32,448,128]{2,1,0:T(8,128)(2,1)} %all-to-all-done.g_ref.got_ref), custom_call_target="tpu_custom_call" | custom-call | flops 352321536 | bytes 3670016 | tf_op jit(solution)/shard_map/pallas_call | solution.py:106
  102.9 2.1 %collective-permute-start.10 = (f32[16,40,128]{2,1,0:T(8,128)S(1)}, f32[16,40,128]{2,1,0:T(8,128)S(1)}, u32[]{:S(2)}, u32[]{:S(2)}) collective-permute-start(f32[16,40,128]{2,1,0:T(8,128)S(1)} %get-tuple-element.21), channel_id=1, source_target_pairs={{0,1},{1,0},{2,3},{3,2},{4,5},{5,4},{6,7},{7,6},{8,9},{9,8},{10,11... | collective-permute-start | bytes 983048 | tf_op jit(solution)/shard_map/ppermute | solution.py:40
  105.0 1.3 collective-permute-done.10
  106.2 0.8 add.101
  107.0 6.7 %all-to-all-start.1 = ((f32[16,40,128]{2,1,0:T(8,128)}), f32[16,40,128]{2,1,0:T(8,128)S(1)}, u32[]{:S(2)}, u32[]{:S(2)}) async-start(f32[16,40,128]{2,1,0:T(8,128)} %add.101), calls=%async_computation.1 | async-start | bytes 655360 | tf_op jit(solution)/shard_map/all_to_all | solution.py:264
  113.7 2.8 %fusion.3 = f32[96,4096]{1,0:T(8,128)S(1)} fusion(bf16[1,4096,448]{1,2,0:T(8,128)(2,1)} %param.10, bf16[32,448]{1,0:T(8,128)(2,1)S(1)} %get-tuple-element.46, bf16[32,448]{1,0:T(8,128)(2,1)S(1)} %get-tuple-element.45, bf16[32,448]{1,0:T(8,128)(2,1)S(1)} %get-tuple-element.27), kind=kOutput, calls=%fused_computation.3 | convolution fusion | flops 352579584 | bytes 5328896 | tf_op jit(solution)/shard_map/dot_general | solution.py:30
  116.5 10.1 %all-to-all-done.1 = f32[16,40,128]{2,1,0:T(8,128)S(1)} async-done(((f32[16,40,128]{2,1,0:T(8,128)}), f32[16,40,128]{2,1,0:T(8,128)S(1)}, u32[]{:S(2)}, u32[]{:S(2)}) %all-to-all-start.1) | async-done | bytes 327712 | tf_op jit(solution)/shard_map/all_to_all | solution.py:264
  127.2 1.6 collective-permute-start.11
  129.3 0.8 collective-permute-done.11
  130.1 1.1 collective-permute-start.14
  131.2 1.2 collective-permute-start.13
  132.4 1.0 collective-permute-start.12
  133.5 1.4 collective-permute-done.14
  134.9 1.0 collective-permute-done.13
  136.5 0.6 fusion.26
  137.1 3.5 %all-to-all-start.2 = ((f32[16,8,128]{2,1,0:T(8,128)}), f32[16,8,128]{2,1,0:T(8,128)S(1)}, u32[]{:S(2)}, u32[]{:S(2)}) async-start(f32[16,8,128]{2,1,0:T(8,128)} %bitcast.32), calls=%async_computation.2 | async-start | bytes 131072 | tf_op jit(solution)/shard_map/all_to_all | solution.py:274
  140.7 2.9 %cholesky.17 = f32[32,32]{1,0:T(8,128)S(1)} custom-call(f32[32,32]{1,0:T(8,128)S(1)} %fusion.40), custom_call_target="Cholesky" | custom-call | tf_op jit(solution)/shard_map/jit(cholesky)/cholesky | solution.py:281
  143.7 0.6 compare_reduce_fusion
  144.3 3.5 %all-to-all-done.2 = f32[16,8,128]{2,1,0:T(8,128)S(1)} async-done(((f32[16,8,128]{2,1,0:T(8,128)}), f32[16,8,128]{2,1,0:T(8,128)S(1)}, u32[]{:S(2)}, u32[]{:S(2)}) %all-to-all-start.2) | async-done | bytes 65568 | tf_op jit(solution)/shard_map/all_to_all | solution.py:274
  147.8 0.7 broadcast_in_dim.6
  148.5 5.5 %all-to-all-start.3 = ((f32[64,8,128]{2,1,0:T(8,128)}), f32[64,8,128]{2,1,0:T(8,128)S(1)}, u32[]{:S(2)}, u32[]{:S(2)}) async-start(f32[64,8,128]{2,1,0:T(8,128)} %broadcast_in_dim.6), calls=%async_computation.3 | async-start | bytes 524288 | tf_op jit(solution)/shard_map/all_to_all | solution.py:275
  154.1 0.7 fusion.35
  154.7 2.4 %custom-call.7 = f32[1,32,32]{1,2,0:T(8,128)S(1)} custom-call(f32[1,32,32]{2,1,0:T(8,128)S(1)} %fusion.35), custom_call_target="InvertDiagBlocksLowerTriangular" | custom-call | tf_op jit(solution)/shard_map/jit(_solve_triangular)/triangular_solve | solution.py:282
  157.4 6.0 %all-to-all-done.3 = f32[64,8,128]{2,1,0:T(8,128)S(1)} async-done(((f32[64,8,128]{2,1,0:T(8,128)}), f32[64,8,128]{2,1,0:T(8,128)S(1)}, u32[]{:S(2)}, u32[]{:S(2)}) %all-to-all-start.3) | async-done | bytes 262176 | tf_op jit(solution)/shard_map/all_to_all | solution.py:275
  163.4 3.7 %collective-permute-start.15 = (f32[4,16,8,128]{3,2,1,0:T(8,128)S(1)}, f32[4,16,8,128]{3,2,1,0:T(8,128)S(1)}, u32[]{:S(2)}, u32[]{:S(2)}) collective-permute-start(f32[4,16,8,128]{3,2,1,0:T(8,128)S(1)} %bitcast.102), channel_id=1, source_target_pairs={{0,1},{1,0},{2,3},{3,2},{4,5},{5,4},{6,7},{7,6},{8,9},{9,8},{10,11... | collective-permute-start | bytes 786440 | tf_op jit(solution)/shard_map/ppermute | solution.py:40
  168.3 0.6 constant_dynamic-update-slice_fusion.2
  170.2 0.6 copy-done.1
  170.8 0.6 copy-done
  171.4 3.6 %shard_map.112 = (f32[448,1024]{1,0:T(8,128)}, f32[448,1024]{1,0:T(8,128)}, f32[448,1024]{1,0:T(8,128)}) custom-call(s32[1]{0:T(128)} %bitcast.40.p, bf16[448,192]{1,0:T(8,128)(2,1)S(1)} %bitcast.96, bf16[192,4096]{1,0:T(8,128)(2,1)S(1)} %fusion.28.basis_ref, f32[448,1024]{1,0:T(8,128)S(1)} %bitcast.93, f32[448,1024]{1,0:T(8,128)S(1)} %bitcast.94, ...), custom_call_target="tpu_custom_call" | custom-call | flops 176160768 | bytes 11010048 | tf_op jit(solution)/shard_map/pallas_call | solution.py:218
  175.0 1.9 all-gather.2.cloned.1.call-done.acts_ref
  176.9 22.5 %shard_map.111 = bf16[448,4096]{1,0:T(8,128)(2,1)} custom-call(bf16[32,448,128]{2,1,0:T(8,128)(2,1)} %all-to-all-done.g_ref.got_ref, bf16[4096,4096]{1,0:T(8,128)(2,1)} %all-gather.2.cloned.1.call-done.acts_ref, bf16[448,4096]{1,0:T(8,128)(2,1)} %bitcast.100, bf16[448,192]{1,0:T(8,128)(2,1)S(1)} %bitcast.97, bf16[192,4096]{1,0:T(8,128)(2,1)S(1)} %fusion.28.basis_ref), custom_call_target="tpu_custom_call" | custom-call | flops 15737028608 | bytes 44564480 | tf_op jit(solution)/shard_map/pallas_call | solution.py:177
  (70 shorter events, 8.2 us)
Async XLA Ops:
  7.2 1.9 copy-start.4
  7.2 169.7 %all-gather.2.cloned.1.call-start = ((), (), s32[]{:S(2)}) async-start(), calls=%async_computation.4 | async-start | bytes 34603008 | tf_op jit(solution)/shard_map/all_gather | solution.py:249
  9.6 10.7 %collective-permute-start.1 = (f32[32,128]{1,0:T(8,128)S(1)}, f32[32,128]{1,0:T(8,128)S(1)}, u32[]{:S(2)}, u32[]{:S(2)}) collective-permute-start(f32[32,128]{1,0:T(8,128)S(1)} %fusion.37), channel_id=1, source_target_pairs={{0,4},{2,6},{4,0},{6,2},{1,5},{3,7},{5,1},{7,3},{8,12},{10,14},{12... | collective-permute-start | bytes 49160 | tf_op jit(solution)/shard_map/ppermute | solution.py:40
  13.4 6.8 %collective-permute-start = (f32[32,128]{1,0:T(8,128)S(1)}, f32[32,128]{1,0:T(8,128)S(1)}, u32[]{:S(2)}, u32[]{:S(2)}) collective-permute-start(f32[32,128]{1,0:T(8,128)S(1)} %fusion.37), channel_id=1, source_target_pairs={{0,2},{2,0},{4,6},{6,4},{1,3},{3,1},{5,7},{7,5},{8,10},{10,8},{12,... | collective-permute-start | bytes 49160 | tf_op jit(solution)/shard_map/ppermute | solution.py:40
  13.8 6.4 %collective-permute-start.2 = (f32[32,128]{1,0:T(8,128)S(1)}, f32[32,128]{1,0:T(8,128)S(1)}, u32[]{:S(2)}, u32[]{:S(2)}) collective-permute-start(f32[32,128]{1,0:T(8,128)S(1)} %fusion.37), channel_id=1, source_target_pairs={{0,6},{2,4},{4,2},{6,0},{1,7},{3,5},{5,3},{7,1},{8,14},{10,12},{12... | collective-permute-start | bytes 49160 | tf_op jit(solution)/shard_map/ppermute | solution.py:40
  20.3 69.4 %all-to-all-start = ((bf16[32,448,128]{2,1,0:T(8,128)(2,1)}), bf16[32,448,128]{2,1,0:T(8,128)(2,1)}, u32[]{:S(2)}, u32[]{:S(2)}) async-start(bf16[32,448,128]{2,1,0:T(8,128)(2,1)} %bitcast.98), calls=%async_computation | async-start | bytes 7340032 | tf_op jit(solution)/shard_map/all_to_all | solution.py:253
  32.8 29.9 %collective-permute-start.5 = (f32[4,32,128]{2,1,0:T(8,128)S(1)}, f32[4,32,128]{2,1,0:T(8,128)S(1)}, u32[]{:S(2)}, u32[]{:S(2)}) collective-permute-start(f32[4,32,128]{2,1,0:T(8,128)S(1)} %bitcast.110), channel_id=1, source_target_pairs={{0,24},{8,16},{16,8},{24,0},{1,25},{9,17},{17,9},{25,1},{2,26},{10... | collective-permute-start | bytes 196616 | tf_op jit(solution)/shard_map/ppermute | solution.py:40
  35.6 47.9 %collective-permute-start.4 = (f32[4,32,128]{2,1,0:T(8,128)S(1)}, f32[4,32,128]{2,1,0:T(8,128)S(1)}, u32[]{:S(2)}, u32[]{:S(2)}) collective-permute-start(f32[4,32,128]{2,1,0:T(8,128)S(1)} %bitcast.111), channel_id=1, source_target_pairs={{0,16},{8,24},{16,0},{24,8},{1,17},{9,25},{17,1},{25,9},{2,18},{10... | collective-permute-start | bytes 196616 | tf_op jit(solution)/shard_map/ppermute | solution.py:40
  36.1 50.5 %collective-permute-start.3 = (f32[4,32,128]{2,1,0:T(8,128)S(1)}, f32[4,32,128]{2,1,0:T(8,128)S(1)}, u32[]{:S(2)}, u32[]{:S(2)}) collective-permute-start(f32[4,32,128]{2,1,0:T(8,128)S(1)} %bitcast.112), channel_id=1, source_target_pairs={{0,8},{8,0},{16,24},{24,16},{1,9},{9,1},{17,25},{25,17},{2,10},{10... | collective-permute-start | bytes 196616 | tf_op jit(solution)/shard_map/ppermute | solution.py:40
  86.9 1.7 collective-permute-start.6
  93.0 4.4 %collective-permute-start.9 = (f32[32,448]{1,0:T(8,128)S(1)}, f32[32,448]{1,0:T(8,128)S(1)}, u32[]{:S(2)}, u32[]{:S(2)}) collective-permute-start(f32[32,448]{1,0:T(8,128)S(1)} %fusion.25), channel_id=1, source_target_pairs={{0,96},{32,64},{64,32},{96,0},{1,97},{33,65},{65,33},{97,1},{2,98}... | collective-permute-start | bytes 172040 | tf_op jit(solution)/shard_map/ppermute | solution.py:40
  95.4 4.7 %collective-permute-start.8 = (f32[32,448]{1,0:T(8,128)S(1)}, f32[32,448]{1,0:T(8,128)S(1)}, u32[]{:S(2)}, u32[]{:S(2)}) collective-permute-start(f32[32,448]{1,0:T(8,128)S(1)} %fusion.25), channel_id=1, source_target_pairs={{0,64},{32,96},{64,0},{96,32},{1,65},{33,97},{65,1},{97,33},{2,66}... | collective-permute-start | bytes 172040 | tf_op jit(solution)/shard_map/ppermute | solution.py:40
  96.0 4.1 %collective-permute-start.7 = (f32[32,448]{1,0:T(8,128)S(1)}, f32[32,448]{1,0:T(8,128)S(1)}, u32[]{:S(2)}, u32[]{:S(2)}) collective-permute-start(f32[32,448]{1,0:T(8,128)S(1)} %fusion.25), channel_id=1, source_target_pairs={{0,32},{32,0},{64,96},{96,64},{1,33},{33,1},{65,97},{97,65},{2,34}... | collective-permute-start | bytes 172040 | tf_op jit(solution)/shard_map/ppermute | solution.py:40
  102.9 3.3 %collective-permute-start.10 = (f32[16,40,128]{2,1,0:T(8,128)S(1)}, f32[16,40,128]{2,1,0:T(8,128)S(1)}, u32[]{:S(2)}, u32[]{:S(2)}) collective-permute-start(f32[16,40,128]{2,1,0:T(8,128)S(1)} %get-tuple-element.21), channel_id=1, source_target_pairs={{0,1},{1,0},{2,3},{3,2},{4,5},{5,4},{6,7},{7,6},{8,9},{9,8},{10,11... | collective-permute-start | bytes 983048 | tf_op jit(solution)/shard_map/ppermute | solution.py:40
  107.0 19.6 %all-to-all-start.1 = ((f32[16,40,128]{2,1,0:T(8,128)}), f32[16,40,128]{2,1,0:T(8,128)S(1)}, u32[]{:S(2)}, u32[]{:S(2)}) async-start(f32[16,40,128]{2,1,0:T(8,128)} %add.101), calls=%async_computation.1 | async-start | bytes 655360 | tf_op jit(solution)/shard_map/all_to_all | solution.py:264
  127.2 2.8 %collective-permute-start.11 = (f32[32,2048]{1,0:T(8,128)S(1)}, f32[32,2048]{1,0:T(8,128)S(1)}, u32[]{:S(2)}, u32[]{:S(2)}) collective-permute-start(f32[32,2048]{1,0:T(8,128)S(1)} %constant_dynamic-slice_fusion), channel_id=1, source_target_pairs={{0,1},{1,0},{2,3},{3,2},{4,5},{5,4},{6,7},{7,6},{8,9},{9,8},{10,11... | collective-permute-start | bytes 786440 | tf_op jit(solution)/shard_map/ppermute | solution.py:40
  130.1 4.8 %collective-permute-start.14 = (f32[8,2048]{1,0:T(8,128)S(1)}, f32[8,2048]{1,0:T(8,128)S(1)}, u32[]{:S(2)}, u32[]{:S(2)}) collective-permute-start(f32[8,2048]{1,0:T(8,128)S(1)} %get-tuple-element.41), channel_id=1, source_target_pairs={{0,96},{32,64},{64,32},{96,0},{1,97},{33,65},{65,33},{97,1},{2,98}... | collective-permute-start | bytes 196616 | tf_op jit(solution)/shard_map/ppermute | solution.py:40
  131.2 4.7 %collective-permute-start.13 = (f32[8,2048]{1,0:T(8,128)S(1)}, f32[8,2048]{1,0:T(8,128)S(1)}, u32[]{:S(2)}, u32[]{:S(2)}) collective-permute-start(f32[8,2048]{1,0:T(8,128)S(1)} %get-tuple-element.42), channel_id=1, source_target_pairs={{0,64},{32,96},{64,0},{96,32},{1,65},{33,97},{65,1},{97,33},{2,66}... | collective-permute-start | bytes 196616 | tf_op jit(solution)/shard_map/ppermute | solution.py:40
  132.4 4.1 %collective-permute-start.12 = (f32[8,2048]{1,0:T(8,128)S(1)}, f32[8,2048]{1,0:T(8,128)S(1)}, u32[]{:S(2)}, u32[]{:S(2)}) collective-permute-start(f32[8,2048]{1,0:T(8,128)S(1)} %get-tuple-element.43), channel_id=1, source_target_pairs={{0,32},{32,0},{64,96},{96,64},{1,33},{33,1},{65,97},{97,65},{2,34}... | collective-permute-start | bytes 196616 | tf_op jit(solution)/shard_map/ppermute | solution.py:40
  137.1 10.6 %all-to-all-start.2 = ((f32[16,8,128]{2,1,0:T(8,128)}), f32[16,8,128]{2,1,0:T(8,128)S(1)}, u32[]{:S(2)}, u32[]{:S(2)}) async-start(f32[16,8,128]{2,1,0:T(8,128)} %bitcast.32), calls=%async_computation.2 | async-start | bytes 131072 | tf_op jit(solution)/shard_map/all_to_all | solution.py:274
  148.5 14.9 %all-to-all-start.3 = ((f32[64,8,128]{2,1,0:T(8,128)}), f32[64,8,128]{2,1,0:T(8,128)S(1)}, u32[]{:S(2)}, u32[]{:S(2)}) async-start(f32[64,8,128]{2,1,0:T(8,128)} %broadcast_in_dim.6), calls=%async_computation.3 | async-start | bytes 524288 | tf_op jit(solution)/shard_map/all_to_all | solution.py:275
  163.4 4.8 %collective-permute-start.15 = (f32[4,16,8,128]{3,2,1,0:T(8,128)S(1)}, f32[4,16,8,128]{3,2,1,0:T(8,128)S(1)}, u32[]{:S(2)}, u32[]{:S(2)}) collective-permute-start(f32[4,16,8,128]{3,2,1,0:T(8,128)S(1)} %bitcast.102), channel_id=1, source_target_pairs={{0,1},{1,0},{2,3},{3,2},{4,5},{5,4},{6,7},{7,6},{8,9},{9,8},{10,11... | collective-permute-start | bytes 786440 | tf_op jit(solution)/shard_map/ppermute | solution.py:40
  168.2 2.0 copy-start.2
  168.9 0.8 copy-start.3
  168.9 1.9 copy-start.1
  168.9 2.4 %copy-start = (f32[1024,448]{0,1:T(8,128)S(1)}, f32[1024,448]{0,1:T(8,128)}, u32[]{:S(2)}) copy-start(f32[1024,448]{0,1:T(8,128)} %param.11) | copy-start | bytes 5505028
Sparse Core Ops, SparseCore 0:
  10.3 166.5 all-gather.1
